TPU v7x, 32 devices: a whole 2x2x4 slice. The times are simulated.
32 devices in a mesh: img: 16 (over z, y, x), seq: 2 (over core).
Axes of the slice: x: 2, y: 2, z: 4, core: 2. Of those that a mesh axis runs over, the one named last changes fastest.
Arguments:
- pixels: bfloat16 [256, 49, 3072], P(('img', 'seq')), may hold values from -6 to 6
- keep_mask: int32 [256, 49], P(('img', 'seq')), may hold values from 0 to 1, as said below
- partner_index: int32 [256], P(('img', 'seq')), may hold values from 0 to 255, each once
- partner_emb: bfloat16 [256, 768], P(('img', 'seq')), may hold values from -0.796875 to 0.796875
- masters: float32 [512, 32, 1024], P('img', 'seq'), may hold values from -0.1875 to 0.1875
- first_moment_slots: float32 [512, 32, 1024], P('img', 'seq'), may hold values from -0.0009822747 to 0.0009822747
- second_moment_slots: float32 [512, 32, 1024], P('img', 'seq'), may hold values from 6.030397e-08 to 2.4121587e-07
- slot_unit_index: int32 [512], replicated, may hold values from 0 to 511, as said below
- small_params: float32 [66, 1024], replicated
- small_first: float32 [66, 1024], replicated, may hold values from -0.0019645493 to 0.0019645493
- small_second: float32 [66, 1024], replicated, may hold values from 6.030397e-08 to 9.648635e-07
- step_count: int32 [], replicated, may hold values from 2 to 20
Outputs:
- new_masters: float32 [512, 32, 1024], P('img', 'seq')
- new_first: float32 [512, 32, 1024], P('img', 'seq')
- new_second: float32 [512, 32, 1024], P('img', 'seq')
- new_small: float32 [66, 1024], replicated
- new_small_first: float32 [66, 1024], replicated
- new_small_second: float32 [66, 1024], replicated
- loss: float32 [], replicated
- grad_norm: float32 [], replicated
Inputs may be any that keep to these rules, and one draw needn't show every extreme that they name: `keep_mask`: each image keeps at least half of its 49 patches, rounded up; some image keeps all and some keeps exactly that least. `slot_unit_index`: a permutation of the slots; values of 504 or more mark slots that hold no unit; the slot of value u differs from u by at most 2. `partner_index`: a permutation of the images.
All inputs are finite; a program needn't handle non-finite values.
Results may differ from a plain program's by a relative error of at most 0.015.
Values may be sent and summed in bfloat16 or wider, within the bound.
No kernel may reach another device: no remote copies, remote signals or barrier semaphores. Data moves between devices by JAX's collectives and lax.ppermute only.
A program may use at most 384 MiB of HBM per device.

v0:
```python
import jax
import jax.numpy as jnp
from jax import lax
from jax.sharding import PartitionSpec as P

MODEL_WIDTH = 1024
HEADS = 16
HEAD_DIM = 64
FF = 4096
PIX = 3072
PROJ = 768
TOKS = 50
ROWS_PER_UNIT = 32
UNIT_COUNT = 504


EPS_NORM = 1e-06
SOFTMAX_SCALE = 0.07
LEARN_RATE = 0.03
BETA_ONE = 0.5
BETA_TWO = 0.5
DECAY_RATE = 0.05
ADAM_EPS = 1e-08
MASKED = -1000000000.0


def layer_norm(values, gain, shift):
    center = values - jnp.mean(values, axis=-1, keepdims=True)
    spread = jnp.mean(center * center, axis=-1, keepdims=True)
    return center * lax.rsqrt(spread + EPS_NORM) * gain + shift


def normalize(values):
    return values * lax.rsqrt(jnp.sum(values * values, axis=-1, keepdims=True) + EPS_NORM)


def exact_gelu(values):
    return jax.nn.gelu(values, approximate=False)


def cast_bfloat_narrow(values):
    return values.astype(jnp.bfloat16)


def small_parts(small):
    base = 1 + TOKS
    tail = base + 8 + FF // MODEL_WIDTH
    return (
        small[0],
        small[1:base],
        small[base],
        small[base + 1],
        small[base + 2],
        small[base + 3],
        small[base + 4],
        small[base + 5],
        small[base + 6],
        small[base + 7],
        small[base + 8 : tail].reshape(FF),
        small[tail],
        small[tail + 1],
        small[tail + 2],
    )


def table_parts(flat):
    offset = PIX
    embed_w = flat[:offset]
    qkv_w = flat[offset : offset + 3 * MODEL_WIDTH].reshape(3, MODEL_WIDTH, MODEL_WIDTH)
    offset = offset + 3 * MODEL_WIDTH
    output_w = flat[offset : offset + MODEL_WIDTH]
    offset = offset + MODEL_WIDTH
    fc_in_w = flat[offset : offset + FF]
    offset = offset + FF
    fc_out_w = flat[offset : offset + FF]
    offset = offset + FF
    proj_w = flat[offset : offset + PROJ]
    return (embed_w, qkv_w[0], qkv_w[1:], output_w, fc_in_w, fc_out_w, proj_w)


def adamw(weight, grad, first, second, step):
    first_new = BETA_ONE * first + (1.0 - BETA_ONE) * grad
    second_new = BETA_TWO * second + (1.0 - BETA_TWO) * grad * grad
    first_hat = first_new / (1.0 - jnp.power(BETA_ONE, step))
    second_hat = second_new / (1.0 - jnp.power(BETA_TWO, step))
    weight_new = weight - LEARN_RATE * (
        first_hat / (jnp.sqrt(second_hat) + ADAM_EPS) + DECAY_RATE * weight
    )
    return (weight_new, first_new, second_new)


def per_device(
    pixels,
    keep_mask,
    partner_index,
    partner_emb,
    masters,
    first_moment_slots,
    second_moment_slots,
    slot_unit_index,
    small_params,
    small_first,
    small_second,
    step_count,
):
    single_float = jnp.float32
    seq_count = lax.axis_size("seq")
    slots = masters.shape[0]
    slot_total = slot_unit_index.shape[0]
    img_dev = pixels.shape[0]
    scale = HEAD_DIM ** (-0.5)
    gathered = lax.all_gather(cast_bfloat_narrow(masters), ("img", "seq"), axis=0, tiled=True)
    unit_slot_index = (
        jnp.zeros((slot_total,), jnp.int32)
        .at[slot_unit_index]
        .set(jnp.arange(slot_total, dtype=jnp.int32))[:UNIT_COUNT]
    )
    owner = unit_slot_index // slots
    within = unit_slot_index % slots
    halves_ids = jnp.arange(seq_count, dtype=jnp.int32)[None, :]
    rows_index = ((owner[:, None] * seq_count + halves_ids) * slots + within[:, None]).reshape(-1)
    flat = jnp.take(gathered, rows_index, axis=0).reshape(UNIT_COUNT * ROWS_PER_UNIT, MODEL_WIDTH)
    embed_w, query_w, keyval_w, output_w, fc_in_w, fc_out_w, proj_w = table_parts(flat)
    (
        class_row,
        pos_rows,
        patch_bias,
        gain_one,
        shift_one,
        query_bias,
        value_bias,
        out_bias,
        gain_two,
        shift_two,
        fc_in_bias,
        fc_out_bias,
        gain_end,
        shift_end,
    ) = small_parts(small_params)
    embedded = cast_bfloat_narrow(
        jnp.einsum("itp,pd->itd", pixels, embed_w, preferred_element_type=single_float)
    )
    patch_state = embedded.astype(single_float) + patch_bias + pos_rows[1:]
    class_state = class_row + pos_rows[0]
    tokens = jnp.concatenate(
        [jnp.broadcast_to(class_state, (img_dev, 1, MODEL_WIDTH)), patch_state], axis=1
    )
    hidden_bf = cast_bfloat_narrow(layer_norm(tokens, gain_one, shift_one))
    value_add = jnp.stack([jnp.zeros_like(value_bias), value_bias])
    keyval = cast_bfloat_narrow(
        jnp.einsum("itd,cde->itce", hidden_bf, keyval_w, preferred_element_type=single_float)
        + value_add
    )
    keys = keyval[:, :, 0].reshape(img_dev, TOKS, HEADS, HEAD_DIM)
    values = keyval[:, :, 1].reshape(img_dev, TOKS, HEADS, HEAD_DIM)
    full_keep = jnp.concatenate([jnp.ones((img_dev, 1), jnp.int32), keep_mask], axis=1)
    class_bf = hidden_bf[:, 0]
    query = cast_bfloat_narrow(
        (jnp.dot(class_bf, query_w, preferred_element_type=single_float) + query_bias) * scale
    )
    query_heads = query.reshape(img_dev, HEADS, HEAD_DIM)
    scores = jnp.einsum("ihd,ithd->iht", query_heads, keys, preferred_element_type=single_float)
    scores = jnp.where(full_keep[:, None, :] > 0, scores, MASKED)
    weights = jax.nn.softmax(scores, axis=-1)
    weights_bf = cast_bfloat_narrow(weights)
    attended = cast_bfloat_narrow(
        jnp.einsum("iht,ithd->ihd", weights_bf, values, preferred_element_type=single_float)
    )
    attended_flat = attended.reshape(img_dev, MODEL_WIDTH)
    resid = (
        class_state
        + jnp.dot(attended_flat, output_w, preferred_element_type=single_float)
        + out_bias
    )
    hidden_two = cast_bfloat_narrow(layer_norm(resid, gain_two, shift_two))
    preact = (
        jnp.einsum("id,fd->if", hidden_two, fc_in_w, preferred_element_type=single_float)
        + fc_in_bias
    )
    active = cast_bfloat_narrow(exact_gelu(preact))
    state = resid + jnp.dot(active, fc_out_w, preferred_element_type=single_float) + fc_out_bias
    final = cast_bfloat_narrow(layer_norm(state, gain_end, shift_end))
    projected = jnp.einsum("id,pd->ip", final, proj_w, preferred_element_type=single_float)
    unit_half_weights = cast_bfloat_narrow(normalize(projected))
    gathered_partners = lax.all_gather(partner_emb, ("img", "seq"), axis=0, tiled=True)
    image_total = gathered_partners.shape[0]
    cosine_score_matrix = (
        jnp.einsum(
            "cl,kl->ck", unit_half_weights, gathered_partners, preferred_element_type=single_float
        )
        / SOFTMAX_SCALE
    )
    total = jax.nn.logsumexp(cosine_score_matrix, axis=-1)
    target = jnp.take_along_axis(cosine_score_matrix, partner_index[:, None], axis=1)[:, 0]
    loss_part = jnp.sum(total - target) / image_total
    onehot = (jnp.arange(image_total, dtype=jnp.int32)[None, :] == partner_index[:, None]).astype(
        single_float
    )
    score_matrix_derivative = (jax.nn.softmax(cosine_score_matrix, axis=-1) - onehot) / image_total
    matmul_derivative = cast_bfloat_narrow(score_matrix_derivative / SOFTMAX_SCALE)
    grad_unit = jnp.dot(matmul_derivative, gathered_partners, preferred_element_type=single_float)
    grad_projected = cast_bfloat_narrow(jax.vjp(normalize, projected)[1](grad_unit)[0])
    grad_proj_w = jnp.einsum(
        "ip,id->pd", grad_projected, final, preferred_element_type=single_float
    )
    grad_final = jnp.dot(grad_projected, proj_w, preferred_element_type=single_float)
    grad_state, grad_gain_end, grad_shift_end = jax.vjp(layer_norm, state, gain_end, shift_end)[1](
        grad_final
    )
    grad_fc_out_bias = jnp.sum(grad_state, axis=0)
    grad_state_bf = cast_bfloat_narrow(grad_state)
    grad_fc_out_w = jnp.einsum(
        "if,id->fd", active, grad_state_bf, preferred_element_type=single_float
    )
    grad_active = jnp.einsum(
        "id,fd->if", grad_state_bf, fc_out_w, preferred_element_type=single_float
    )
    grad_preact = cast_bfloat_narrow(jax.vjp(exact_gelu, preact)[1](grad_active)[0])
    grad_fc_in_bias = jnp.sum(grad_preact.astype(single_float), axis=0)
    grad_fc_in_w = jnp.einsum(
        "if,id->fd", grad_preact, hidden_two, preferred_element_type=single_float
    )
    grad_hidden_two = jnp.dot(grad_preact, fc_in_w, preferred_element_type=single_float)
    grad_resid_norm, grad_gain_two, grad_shift_two = jax.vjp(
        layer_norm, resid, gain_two, shift_two
    )[1](grad_hidden_two)
    grad_resid = grad_state + grad_resid_norm
    grad_out_bias = jnp.sum(grad_resid, axis=0)
    grad_resid_bf = cast_bfloat_narrow(grad_resid)
    grad_output_w = jnp.einsum(
        "ie,id->ed", attended_flat, grad_resid_bf, preferred_element_type=single_float
    )
    grad_attended = cast_bfloat_narrow(
        jnp.einsum("id,ed->ie", grad_resid_bf, output_w, preferred_element_type=single_float)
    )
    grad_attended = grad_attended.reshape(img_dev, HEADS, HEAD_DIM)
    grad_weights = jnp.einsum(
        "ihd,ithd->iht", grad_attended, values, preferred_element_type=single_float
    )
    grad_values = jnp.einsum(
        "iht,ihd->ithd", weights_bf, grad_attended, preferred_element_type=single_float
    )
    grad_scores = weights * (grad_weights - jnp.sum(weights * grad_weights, axis=-1, keepdims=True))
    grad_scores_bf = cast_bfloat_narrow(grad_scores)
    grad_query = cast_bfloat_narrow(
        jnp.einsum("iht,ithd->ihd", grad_scores_bf, keys, preferred_element_type=single_float)
    )
    grad_keys = jnp.einsum(
        "iht,ihd->ithd", grad_scores_bf, query_heads, preferred_element_type=single_float
    )
    grad_keyval_bf = cast_bfloat_narrow(
        jnp.stack(
            [
                grad_keys.reshape(img_dev, TOKS, MODEL_WIDTH),
                grad_values.reshape(img_dev, TOKS, MODEL_WIDTH),
            ],
            axis=2,
        )
    )
    grad_query_scaled = grad_query.reshape(img_dev, MODEL_WIDTH).astype(single_float) * scale
    grad_query_bias = jnp.sum(grad_query_scaled, axis=0)
    grad_query_scaled_bf = cast_bfloat_narrow(grad_query_scaled)
    grad_query_w = jnp.einsum(
        "id,ie->de", class_bf, grad_query_scaled_bf, preferred_element_type=single_float
    )
    grad_class_hidden = jnp.einsum(
        "ie,de->id", grad_query_scaled_bf, query_w, preferred_element_type=single_float
    )
    grad_value_bias = jnp.sum(grad_keyval_bf[:, :, 1].astype(single_float), axis=(0, 1))
    grad_keyval_w = jnp.einsum(
        "itd,itce->cde", hidden_bf, grad_keyval_bf, preferred_element_type=single_float
    )
    grad_hidden = jnp.einsum(
        "itce,cde->itd", grad_keyval_bf, keyval_w, preferred_element_type=single_float
    )
    grad_hidden = grad_hidden.at[:, 0].add(grad_class_hidden)
    grad_tokens, grad_gain_tok, grad_shift_tok = jax.vjp(layer_norm, tokens, gain_one, shift_one)[
        1
    ](grad_hidden)
    grad_class = jnp.sum(grad_tokens[:, 0], axis=0) + jnp.sum(grad_resid, axis=0)
    grad_patch = grad_tokens[:, 1:]
    grad_pos = jnp.concatenate([grad_class[None], jnp.sum(grad_patch, axis=0)], axis=0)
    grad_patch_bias = jnp.sum(grad_patch, axis=(0, 1))
    grad_embed_w = jnp.einsum(
        "itp,itd->pd", pixels, cast_bfloat_narrow(grad_patch), preferred_element_type=single_float
    )
    small_grad = jnp.concatenate(
        [
            grad_class[None],
            grad_pos,
            grad_patch_bias[None],
            grad_gain_tok[None],
            grad_shift_tok[None],
            grad_query_bias[None],
            grad_value_bias[None],
            grad_out_bias[None],
            grad_gain_two[None],
            grad_shift_two[None],
            grad_fc_in_bias.reshape(FF // MODEL_WIDTH, MODEL_WIDTH),
            grad_fc_out_bias[None],
            grad_gain_end[None],
            grad_shift_end[None],
        ],
        axis=0,
    )
    grad_table = jnp.concatenate(
        [
            grad_embed_w,
            grad_query_w,
            grad_keyval_w.reshape(2 * MODEL_WIDTH, MODEL_WIDTH),
            grad_output_w,
            grad_fc_in_w,
            grad_fc_out_w,
            grad_proj_w,
        ],
        axis=0,
    ).reshape(UNIT_COUNT, ROWS_PER_UNIT, MODEL_WIDTH)
    small_total, loss = lax.psum((small_grad, loss_part), ("img", "seq"))
    slot_grads = jnp.take(grad_table, slot_unit_index, axis=0, mode="fill", fill_value=0.0)
    core_half = lax.psum_scatter(
        slot_grads.astype(jnp.bfloat16), "seq", scatter_dimension=1, tiled=True
    ).astype(jnp.float32)
    owned = lax.psum_scatter(core_half, "img", scatter_dimension=0, tiled=True)
    owner_squares = jnp.sum(owned * owned)
    owner_total = lax.psum(owner_squares, ("img", "seq"))
    grad_norm = jnp.sqrt(owner_total + jnp.sum(small_total * small_total))
    factor = 1.0 / jnp.maximum(grad_norm, 1.0)
    step_value = step_count.astype(single_float)
    new_masters, new_first, new_second = adamw(
        masters, owned * factor, first_moment_slots, second_moment_slots, step_value
    )
    new_small, new_small_first, new_small_second = adamw(
        small_params, small_total * factor, small_first, small_second, step_value
    )
    return (
        new_masters,
        new_first,
        new_second,
        new_small,
        new_small_first,
        new_small_second,
        loss,
        grad_norm,
    )


def solution(mesh):
    return jax.shard_map(
        per_device,
        mesh=mesh,
        in_specs=(
            P(("img", "seq"), None, None),
            P(("img", "seq"), None),
            P(("img", "seq")),
            P(("img", "seq"), None),
            P("img", "seq", None),
            P("img", "seq", None),
            P("img", "seq", None),
            P(),
            P(),
            P(),
            P(),
            P(),
        ),
        out_specs=(
            P("img", "seq", None),
            P("img", "seq", None),
            P("img", "seq", None),
            P(),
            P(),
            P(),
            P(),
            P(),
        ),
        check_vma=False,
    )
```

profile of v0, /device:TPU:0, one launch (start us, length us, event | category | flops | bytes accessed | tf_op | source)
XLA Modules:
  0.0 1421.1 jit_solution(7540486390523453937)
XLA Ops:
  7.3 2.9 convert_element_type.98
  14.3 48.5 %all_gather.7 = bf16[256,768]{1,0:T(8,128)(2,1)} all-gather(bf16[8,768]{1,0:T(8,128)(2,1)S(1)} %copy-done.52), channel_id=1, replica_groups=mesh['img'=16,'seq'=2] {'img','seq'}, dimensions={0}, use_global_device_ids=true | all-gather | bytes 405504 | tf_op jit(solution)/shard_map/all_gather | solution.py:185
  63.2 147.1 %all-gather.2.cloned.1.call-done = bf16[1024,16,1024]{2,1,0:T(8,128)(2,1)} async-done(((bf16[32,16,1024]{2,1,0:T(8,128)(2,1)}), bf16[1024,16,1024]{2,1,0:T(8,128)(2,1)}) %all-gather.2.cloned.1.call-update) | async-done | bytes 33554448 | tf_op jit(solution)/shard_map/all_gather | solution.py:112
  210.3 35.4 %gather_fusion = bf16[1008,16,1024]{2,1,0:T(8,128)(2,1)} fusion(bf16[1024,16,1024]{2,1,0:T(8,128)(2,1)} %all-gather.2.cloned.1.call-done, s32[1024]{0:T(1024)S(1)} %pad_clamp_fusion.1), kind=kCustom, calls=%fused_computation | custom fusion | bytes 66064320 | tf_op jit(solution)/shard_map/jit(_take)/gather | solution.py:122
  245.7 22.6 %broadcast_select_fusion = bf16[1008,16,1024]{2,1,0:T(8,128)(2,1)} fusion(bf16[1008,16,1024]{2,1,0:T(8,128)(2,1)} %gather_fusion, pred[1008]{0:T(1024)(128)(4,1)S(1)} %compare_and_fusion), kind=kLoop, calls=%fused_computation.5 | loop fusion | flops 16515072 | bytes 66061296 | tf_op jit(solution)/shard_map/jit(_take)/select_n | solution.py:122
  271.2 5.0 slice.177
  276.1 4.2 fusion.81
  280.3 13.4 fusion.80
  293.7 3.3 bitcast_add_fusion
  300.2 4.3 add_convert_fusion
  305.5 3.1 reshape.383
  318.8 5.9 multiply_convert_fusion.2
  324.7 4.8 fusion.85
  333.2 2.9 convert_reduce_fusion.1
  346.5 2.9 stack_reshape.8
  357.8 6.2 convolution_bitcast_fusion.1
  364.0 4.4 fusion.25
  379.8 3.4 fusion.71
  386.2 6.9 convolution_bitcast_fusion
  393.1 8.7 copy.48
  401.8 6.1 constant_dynamic-update-slice_fusion.1
  415.3 5.6 convolution_dynamic-update-slice_fusion.1
  420.9 5.7 convolution_dynamic-update-slice_fusion
  428.5 22.9 %gather_fusion.1 = bf16[512,32,1024]{2,1,0:T(8,128)(2,1)} fusion(bf16[504,32,1024]{2,1,0:T(8,128)(2,1)} %bitcast.167, s32[1024]{0:T(1024)S(1)} %copy-done.53), kind=kCustom, calls=%fused_computation.1 | custom fusion | bytes 67110912 | tf_op jit(solution)/shard_map/jit(_take)/gather | solution.py:319
  451.4 23.0 %select_convert_fusion = bf16[512,32,1024]{2,1,0:T(8,128)(2,1)} fusion(bf16[512,32,1024]{2,1,0:T(8,128)(2,1)} %gather_fusion.1, pred[512]{0:T(512)(128)(4,1)S(1)} %copy-done.64), kind=kLoop, calls=%fused_computation.4 | loop fusion | flops 16777216 | bytes 67109376 | tf_op jit(solution)/shard_map/convert_element_type | solution.py:321
  474.4 43.5 %reduce-scatter.3.cloned.1.call-done = bf16[512,16,1024]{2,1,0:T(8,128)(2,1)} async-done(((bf16[512,32,1024]{2,1,0:T(8,128)(2,1)}), bf16[512,16,1024]{2,1,0:T(8,128)(2,1)}) %reduce-scatter.3.cloned.1.call-update) | async-done | bytes 16777232 | tf_op jit(solution)/shard_map/reduce_scatter | solution.py:320
  517.9 18.9 %convert_element_type.124 = f32[512,16,1024]{2,1,0:T(8,128)} convert(bf16[512,16,1024]{2,1,0:T(8,128)(2,1)} %reduce-scatter.3.cloned.1.call-done) | non-fusion elementwise | flops 8388608 | bytes 50331648 | tf_op jit(solution)/shard_map/convert_element_type | solution.py:322
  540.5 4.8 concatenate.17
  545.4 676.3 %reduce-scatter.5.cloned.1.call-done = f32[32,16,1024]{2,1,0:T(8,128)} async-done(((f32[512,16,1024]{2,1,0:T(8,128)}), f32[32,16,1024]{2,1,0:T(8,128)}) %reduce-scatter.5.cloned.1.call-update) | async-done | bytes 2097168 | tf_op jit(solution)/shard_map/reduce_scatter | solution.py:323
  1224.4 134.4 %all-reduce.5.cloned.1.call-done = f32[66,1024]{1,0:T(8,128)} async-done(((f32[66,1024]{1,0:T(8,128)}), f32[66,1024]{1,0:T(8,128)}) %all-reduce.5.cloned.1.call-update) | async-done | bytes 270352 | tf_op jit(solution)/shard_map/psum | solution.py:318
  1360.4 41.4 %all-reduce.2 = (f32[]{:T(128)}, f32[]{:T(128)}) all-reduce(f32[]{:T(128)} %multiply_reduce_fusion, f32[]{:T(128)S(6)} %div.166), channel_id=1, replica_groups=mesh['img'=16,'seq'=2] {'img','seq'}, use_global_device_ids=true, to_apply=%region_23.24 | all-reduce | flops 2 | bytes 16 | tf_op jit(solution)/shard_map/psum | solution.py:325
  1405.2 7.7 multiply_subtract_fusion
  (266 shorter events, 76.1 us)
Async XLA Ops:
  7.2 286.5 %copy-start = (bf16[8,49,3072]{2,0,1:T(8,128)(2,1)S(1)}, bf16[8,49,3072]{2,0,1:T(8,128)(2,1)}, u32[]{:S(2)}) copy-start(bf16[8,49,3072]{2,0,1:T(8,128)(2,1)} %param.14) | copy-start | bytes 7225348
  7.2 6.1 copy-start.63
  7.2 6.3 copy-start.12
  7.2 7.0 copy-start.52
  7.2 203.1 %all-gather.2.cloned.1.call-start = ((), (), s32[]{:S(2)}) async-start(), calls=%async_computation.2 | async-start | bytes 34603008 | tf_op jit(solution)/shard_map/all_gather | solution.py:112
  10.2 507.7 %reduce-scatter.3.cloned.1.call-start = ((), (), s32[]{:S(2)}) async-start(), calls=%async_computation.3 | async-start | bytes 50331648 | tf_op jit(solution)/shard_map/reduce_scatter | solution.py:320
  13.6 284.2 %copy-start.26 = (f32[1,1024]{1,0:T(1,128)}, f32[1,1024]{1,0:T(1,128)S(1)}, u32[]{:S(2)}) copy-start(f32[1,1024]{1,0:T(1,128)S(1)} %get-tuple-element.68) | copy-start | bytes 12292
  13.6 305.1 %copy-start.36 = (f32[1,1024]{1,0:T(1,128)}, f32[1,1024]{1,0:T(1,128)S(1)}, u32[]{:S(2)}) copy-start(f32[1,1024]{1,0:T(1,128)S(1)} %get-tuple-element.62) | copy-start | bytes 12292
  13.6 316.1 %copy-start.34 = (f32[1,1024]{1,0:T(1,128)}, f32[1,1024]{1,0:T(1,128)S(1)}, u32[]{:S(2)}) copy-start(f32[1,1024]{1,0:T(1,128)S(1)} %get-tuple-element.71) | copy-start | bytes 12292
  13.6 319.3 %copy-start.28 = (f32[1,1024]{1,0:T(1,128)}, f32[1,1024]{1,0:T(1,128)S(1)}, u32[]{:S(2)}) copy-start(f32[1,1024]{1,0:T(1,128)S(1)} %get-tuple-element.60) | copy-start | bytes 12292
  280.3 18.0 %copy-start.4 = (bf16[64,16,1024]{2,1,0:T(8,128)(2,1)}, bf16[64,16,1024]{2,1,0:T(8,128)(2,1)S(1)}, u32[]{:S(2)}) copy-start(bf16[64,16,1024]{2,1,0:T(8,128)(2,1)S(1)} %get-tuple-element.56) | copy-start | bytes 6291460
  280.3 13.4 slice-start
  298.3 6.1 copy-start.21
  318.5 19.4 %copy-start.50 = (f32[8]{0:T(128)}, f32[8]{0:T(128)S(1)}, u32[]{:S(2)}) copy-start(f32[8]{0:T(128)S(1)} %broadcast_multiply_fusion.2) | copy-start | bytes 100
  318.7 19.2 %copy-start.57 = (f32[8]{0:T(128)}, f32[8]{0:T(128)S(1)}, u32[]{:S(2)}) copy-start(f32[8]{0:T(128)S(1)} %fusion.65) | copy-start | bytes 100
  318.7 11.0 copy-start.7
  318.7 14.4 %slice-start.3 = ((s8[8388608]{0:T(1024)(128)(4,1)}), s8[4194304]{0:T(1024)(128)(4,1)S(1)}, s32[]{:S(2)}) async-start(s8[8388608]{0:T(1024)(128)(4,1)} %bitcast.164), calls=%async_computation.9 | async-start | bytes 8388608
  324.7 8.5 slice-start.4
  324.7 11.4 slice-start.1
  357.8 6.2 copy-start.15
  357.8 6.2 copy-start.16
  370.0 9.8 copy-start.27
  376.4 6.8 copy-start.40
  376.4 6.8 copy-start.31
  401.8 6.1 copy-start.22
  428.5 22.9 %copy-start.64 = (pred[512]{0:T(512)(128)(4,1)S(1)}, pred[512]{0:T(512)(128)(4,1)}, u32[]{:S(2)}) copy-start(pred[512]{0:T(512)(128)(4,1)} %compare_and_fusion.1) | copy-start | bytes 1540
  474.4 747.3 %reduce-scatter.5.cloned.1.call-start = ((), (), s32[]{:S(2)}) async-start(), calls=%async_computation.4 | async-start | bytes 35651584 | tf_op jit(solution)/shard_map/reduce_scatter | solution.py:323
  537.0 821.8 %all-reduce.5.cloned.1.call-start = ((), (), s32[]{:S(2)}) async-start(), calls=%async_computation.5 | async-start | bytes 589824 | tf_op jit(solution)/shard_map/psum | solution.py:318
  540.4 862.8 %copy-start.13 = (f32[66,1024]{1,0:T(8,128)S(1)}, f32[66,1024]{1,0:T(8,128)}, u32[]{:S(2)}) copy-start(f32[66,1024]{1,0:T(8,128)} %param.22) | copy-start | bytes 811012
  540.4 862.8 %copy-start.17 = (f32[66,1024]{1,0:T(8,128)S(1)}, f32[66,1024]{1,0:T(8,128)}, u32[]{:S(2)}) copy-start(f32[66,1024]{1,0:T(8,128)} %param.24) | copy-start | bytes 811012
  540.4 862.8 %copy-start.18 = (f32[66,1024]{1,0:T(8,128)S(1)}, f32[66,1024]{1,0:T(8,128)}, u32[]{:S(2)}) copy-start(f32[66,1024]{1,0:T(8,128)} %param.23) | copy-start | bytes 811012
  1405.2 7.7 copy-start.1
  (45 other events, 144.0 us)
Sparse Core Ops, SparseCore 0:
  11.5 198.7 all-gather.1
  474.5 43.3 reduce-scatter.2
  537.0 684.6 reduce-scatter.4
  1227.4 131.2 all-reduce.4
where the time goes:
time: 1430 us; the launch traced here: 1420 us
  waiting for transfers between devices  1000 us (70%)
  local copies, waits for them, and re-layouts  133 us (9%)
  other arithmetic  103 us (7%)
  blocking collectives  89.8 us (6%)
  matrix products  74.3 us (5%)
  between operations  19.2 us (1%)
    reduce_scatter x1, waiting for transfers between devices, per_device(): owned = lax.psum_scatter(core_half, 'img', scatter_dimension=0, tiled=True)  676 us
    all_gather x1, waiting for transfers between devices, per_device(): lax.all_gather(cast_bfloat_narrow(masters), ('img', 'seq'), axis=0, tiled...  147 us
    psum x1, waiting for transfers between devices, per_device(): small_total, loss = lax.psum((small_grad, loss_part), ('img', 'seq'))  134 us
    all_gather x1, blocking collectives, per_device(): lax.all_gather(partner_emb, ('img', 'seq'), axis=0, tiled=True)  48.5 us
    reduce_scatter x1, waiting for transfers between devices, per_device(): lax.psum_scatter(slot_grads.astype(jnp.bfloat16), 'seq', scatter_dimensio...  43.5 us
    psum x1, blocking collectives, per_device(): owner_total = lax.psum(owner_squares, ('img', 'seq'))  41.4 us
    gather x1, local copies, waits for them, and re-layouts, per_device(): jnp.take(gathered, rows_index, axis=0)  35.4 us
  transfers between devices with their start and end apart: 4, of which 4 were waited for; matrix products, arithmetic and copies ran while one was open for 1% of the time, Pallas kernels for 0%

commit v1 on v0

v1 whole, which is shorter than its diff:
```python
import functools

import jax
import jax.numpy as jnp
from jax import lax
from jax.experimental import pallas as pl
from jax.experimental.pallas import tpu as pltpu
from jax.sharding import PartitionSpec as P

WIDTH = 1024
HEADS = 16
HEAD_DIM = 64
FF = 4096
PIX = 3072
PROJ = 768
TOKS = 50
PATCHES = TOKS - 1
ROWS_PER_UNIT = 32
UNIT_COUNT = 504
JITTER = 2

EPS_NORM = 1e-06
SOFTMAX_SCALE = 0.07
LEARN_RATE = 0.03
BETA_ONE = 0.5
BETA_TWO = 0.5
DECAY_RATE = 0.05
ADAM_EPS = 1e-08
MASKED = -1000000000.0
SCALE = HEAD_DIM ** (-0.5)

F32 = jnp.float32
BF = jnp.bfloat16
ROW_BASE = 1 + TOKS
ROW_TAIL = ROW_BASE + 8 + FF // WIDTH
SLOT = 64


def low(values):
    return values.astype(BF)


def dot(a, b, dims=((1,), (0,)), precision=None):
    return lax.dot_general(a, b, (dims, ((), ())), precision=precision, preferred_element_type=F32)


NN = ((1,), (0,))
NT = ((1,), (1,))
TN = ((0,), (0,))


def layer_norm(values, gain, shift):
    center = values - jnp.mean(values, axis=-1, keepdims=True)
    spread = jnp.mean(center * center, axis=-1, keepdims=True)
    return center * lax.rsqrt(spread + EPS_NORM) * gain + shift


def normalize(values):
    return values * lax.rsqrt(jnp.sum(values * values, axis=-1, keepdims=True) + EPS_NORM)


def exact_gelu(values):
    return jax.nn.gelu(values, approximate=False)


def small_parts(small):
    base, tail = ROW_BASE, ROW_TAIL
    return (
        small[0],
        small[1:base],
        small[base],
        small[base + 1],
        small[base + 2],
        small[base + 3],
        small[base + 4],
        small[base + 5],
        small[base + 6],
        small[base + 7],
        small[base + 8 : tail].reshape(FF),
        small[tail],
        small[tail + 1],
        small[tail + 2],
    )


def adamw(weight, grad, first, second, step):
    first_new = BETA_ONE * first + (1.0 - BETA_ONE) * grad
    second_new = BETA_TWO * second + (1.0 - BETA_TWO) * grad * grad
    first_hat = first_new / (1.0 - jnp.power(BETA_ONE, step))
    second_hat = second_new / (1.0 - jnp.power(BETA_TWO, step))
    weight_new = weight - LEARN_RATE * (
        first_hat / (jnp.sqrt(second_hat) + ADAM_EPS) + DECAY_RATE * weight
    )
    return (weight_new, first_new, second_new)


def with_halo(values, chips):
    before = lax.ppermute(values[-JITTER:], "img", [(i, i + 1) for i in range(chips - 1)])
    after = lax.ppermute(values[:JITTER], "img", [(i + 1, i) for i in range(chips - 1)])
    return jnp.concatenate([before, values, after], axis=0)


def slots_near(slot_unit_index, img, slots):
    padded = jnp.pad(slot_unit_index, (JITTER, JITTER), constant_values=-1)
    return lax.dynamic_slice(padded, (img * slots,), (slots + 2 * JITTER,))


def pick(ext, matches, slots):
    out = jnp.zeros((slots,) + ext.shape[1:], ext.dtype)
    for shift in range(2 * JITTER + 1):
        out = jnp.where(matches[shift][:, None, None], ext[shift : shift + slots], out)
    return out


def to_units(values, near, img, chips):
    slots = values.shape[0]
    ids = img * slots + jnp.arange(slots, dtype=jnp.int32)
    matches = [near[s : s + slots] == ids for s in range(2 * JITTER + 1)]
    return pick(with_halo(values, chips), matches, slots)


def to_slots(values, near, img, chips):
    slots = values.shape[0]
    here = near[JITTER : JITTER + slots]
    ids = img * slots + jnp.arange(slots, dtype=jnp.int32)
    matches = [
        (here == ids + (s - JITTER)) & (here < UNIT_COUNT) for s in range(2 * JITTER + 1)
    ]
    return pick(with_halo(values, chips), matches, slots)


def shuffle_matrix():
    source = lax.broadcasted_iota(jnp.int32, (256, 256), 0)
    target = lax.broadcasted_iota(jnp.int32, (256, 256), 1)
    moved = ((source // 16) % 2) * 128 + (source // 32) * 16 + source % 16
    return (moved == target).astype(F32).astype(BF)


def full_spec():
    return pl.BlockSpec(memory_space=pltpu.VMEM)


def smem_spec():
    return pl.BlockSpec(memory_space=pltpu.SMEM)


def prep_kernel(pix_ref, shuffle_ref, out_ref):
    shuffle = shuffle_ref[...]
    for block in range(PIX // 256):
        moved = dot(pix_ref[0, :, 256 * block : 256 * block + 256], shuffle).astype(BF)
        out_ref[0, 0, :, 128 * block : 128 * block + 128] = moved[:, :128]
        out_ref[1, 0, :, 128 * block : 128 * block + 128] = moved[:, 128:]


def prep(padded, shuffle):
    images = padded.shape[0]
    return pl.pallas_call(
        prep_kernel,
        grid=(images,),
        in_specs=[
            pl.BlockSpec((1, SLOT, PIX), lambda i: (i, 0, 0)),
            pl.BlockSpec((256, 256), lambda i: (0, 0)),
        ],
        out_specs=pl.BlockSpec((2, 1, SLOT, PIX // 2), lambda i: (0, i, 0, 0)),
        out_shape=jax.ShapeDtypeStruct((2, images, SLOT, PIX // 2), BF),
        compiler_params=pltpu.CompilerParams(vmem_limit_bytes=24 * 2**20),
        cost_estimate=pl.CostEstimate(flops=8 * 10**8, bytes_accessed=6 * 2**20, transcendentals=0),
        name="prep",
    )(padded, shuffle)


def head_mask(rows):
    lane = lax.broadcasted_iota(jnp.int32, (rows, WIDTH), 1) // HEAD_DIM
    row = lax.broadcasted_iota(jnp.int32, (rows, WIDTH), 0) % HEADS
    return lane == row


def forward_kernel(pieces, images, where_ref, pix_ref, *refs):
    count = len(pieces)
    own, peer = refs[:count], refs[count : 2 * count]
    add_ref, rows_ref, qk_ref, valid_ref, shuffle_ref = refs[2 * count : 2 * count + 5]
    hid_ref, xhat_ref, rstd_ref, p_ref, pooled_ref, mass_ref, wv_ref, o_ref = refs[
        2 * count + 5 : 2 * count + 13
    ]
    acc_ref, pool_ref = refs[2 * count + 13 :]
    col, core = where_ref[0], where_ref[1]
    acc_ref[...] = add_ref[...]
    for flip, group in ((0, own), (1, peer)):
        half = core ^ flip
        for (source, first, rows), ref in zip(pieces, group):
            block = col ^ source

            @pl.when(block < 3)
            def _():
                lanes = pl.ds(pl.multiple_of(block * 512 + first, 128), rows)
                acc_ref[...] += dot(pix_ref[half, :, lanes], ref[...])

            @pl.when(block == 3)
            def _():
                wv_ref[half, first : first + rows] = ref[...]

    gain, shift, value_bias = rows_ref[0:1], rows_ref[1:2], rows_ref[2:3]
    valid = valid_ref[...] > 0
    qk = qk_ref[...]
    for i in range(images):
        part = slice(SLOT * i, SLOT * (i + 1))
        x = acc_ref[part]
        center = x - jnp.mean(x, axis=-1, keepdims=True)
        rstd = lax.rsqrt(jnp.mean(center * center, axis=-1, keepdims=True) + EPS_NORM)
        xhat = center * rstd
        hid = low(xhat * gain + shift)
        xhat_ref[part] = xhat
        rstd_ref[part] = jnp.broadcast_to(rstd, (SLOT, 128))
        hid_ref[part] = hid
        scores = jnp.where(valid[part], dot(hid, qk, NT), MASKED)
        e = jnp.exp(scores - jnp.max(scores, axis=0, keepdims=True))
        p = e / jnp.sum(e, axis=0, keepdims=True)
        p_ref[part] = p
        pb = low(p)
        pool_ref[HEADS * i : HEADS * (i + 1)] = low(dot(pb, hid, TN))
        mass_ref[HEADS * i : HEADS * (i + 1)] = dot(pb, jnp.ones((SLOT, 128), BF), TN)
    shuffle = shuffle_ref[...]
    for block in range(WIDTH // 256):
        moved = low(dot(pool_ref[:, 256 * block : 256 * block + 256], shuffle))
        pooled_ref[0, :, 128 * block : 128 * block + 128] = moved[:, :128]
        pooled_ref[1, :, 128 * block : 128 * block + 128] = moved[:, 128:]
    rows = images * HEADS
    mixed = dot(pooled_ref[0], wv_ref[0]) + dot(pooled_ref[1], wv_ref[1])
    mixed = mixed + mass_ref[:, 0:1] * value_bias
    mixed = jnp.where(head_mask(rows), mixed, 0.0)
    joined = low(jnp.sum(mixed.reshape(images, HEADS, WIDTH), axis=1))
    for block in range(WIDTH // 256):
        moved = low(dot(joined[:, 256 * block : 256 * block + 256], shuffle))
        o_ref[0, :, 128 * block : 128 * block + 128] = moved[:, :128]
        o_ref[1, :, 128 * block : 128 * block + 128] = moved[:, 128:]


def forward_call(pieces, images, where, pix, own, peer, add, rows, qk, valid, shuffle):
    tokens = images * SLOT
    n_in = 1 + 2 * len(pieces) + 5
    return pl.pallas_call(
        functools.partial(forward_kernel, pieces, images),
        in_specs=[smem_spec()] + [full_spec()] * n_in,
        out_specs=[full_spec()] * 8,
        out_shape=[
            jax.ShapeDtypeStruct((tokens, WIDTH), BF),
            jax.ShapeDtypeStruct((tokens, WIDTH), F32),
            jax.ShapeDtypeStruct((tokens, 128), F32),
            jax.ShapeDtypeStruct((tokens, HEADS), F32),
            jax.ShapeDtypeStruct((2, images * HEADS, WIDTH // 2), BF),
            jax.ShapeDtypeStruct((images * HEADS, 128), F32),
            jax.ShapeDtypeStruct((2, WIDTH // 2, WIDTH), BF),
            jax.ShapeDtypeStruct((2, images, WIDTH // 2), BF),
        ],
        scratch_shapes=[
            pltpu.VMEM((tokens, WIDTH), F32),
            pltpu.VMEM((images * HEADS, WIDTH), BF),
        ],
        compiler_params=pltpu.CompilerParams(vmem_limit_bytes=48 * 2**20),
        cost_estimate=pl.CostEstimate(flops=4 * 10**9, bytes_accessed=18 * 2**20, transcendentals=0),
        name="forward",
    )(where, pix, *own, *peer, add, rows, qk, valid, shuffle)


def backward_kernel(
    images, do_ref, wv_ref, hid_ref, xhat_ref, rstd_ref, p_ref, mass_ref, qk_ref, rows_ref,
    shuffle_ref, de_ref, pos_ref, vec_ref, pull_ref, dom_ref, da_ref,
):
    rows = images * HEADS
    gain, value_bias = rows_ref[0:1], rows_ref[2:3]
    spread = jnp.broadcast_to(do_ref[...].reshape(images, 1, WIDTH).astype(F32), (images, HEADS, WIDTH))
    wide = jnp.where(head_mask(rows), spread.reshape(rows, WIDTH), 0.0)
    dom_ref[...] = low(wide)
    vec_ref[...] = jnp.zeros_like(vec_ref)
    vec_ref[2:3] = jnp.sum(wide * mass_ref[:, 0:1], axis=0, keepdims=True)
    first = low(dot(dom_ref[...], wv_ref[0], NT))
    second = low(dot(dom_ref[...], wv_ref[1], NT))
    shuffle = shuffle_ref[...]
    for block in range(WIDTH // 256):
        both = jnp.concatenate(
            [first[:, 128 * block : 128 * block + 128], second[:, 128 * block : 128 * block + 128]],
            axis=1,
        )
        da_ref[:, 256 * block : 256 * block + 256] = low(dot(both, shuffle, NT))
    qk = qk_ref[...]
    bias_rows = low(jnp.broadcast_to(value_bias, (8, WIDTH)))
    real = lax.broadcasted_iota(jnp.int32, (SLOT, WIDTH), 0) < PATCHES
    for i in range(images):
        part = slice(SLOT * i, SLOT * (i + 1))
        mine = slice(HEADS * i, HEADS * (i + 1))
        hid, p, da = hid_ref[part], p_ref[part], da_ref[mine]
        dp = dot(hid, da, NT) + dot(bias_rows, dom_ref[mine], NT)[0:1]
        ds = low(p * (dp - jnp.sum(p * dp, axis=0, keepdims=True)))
        dh = dot(low(p), da) + dot(ds, qk)
        pull = dot(ds, hid, TN)
        xhat, rstd = xhat_ref[part], rstd_ref[part, 0:1]
        gy = dh * gain
        dx = rstd * (
            gy
            - jnp.mean(gy, axis=-1, keepdims=True)
            - xhat * jnp.mean(gy * xhat, axis=-1, keepdims=True)
        )
        de_ref[part] = low(jnp.where(real, dx, 0.0))
        vec_ref[0:1] += jnp.sum(dh * xhat, axis=0, keepdims=True)
        vec_ref[1:2] += jnp.sum(dh, axis=0, keepdims=True)
        if i == 0:
            pos_ref[...] = dx
            pull_ref[...] = pull
        else:
            pos_ref[...] += dx
            pull_ref[...] += pull


def backward_call(images, do, wv, hid, xhat, rstd, p, mass, qk, rows, shuffle):
    tokens = images * SLOT
    return pl.pallas_call(
        functools.partial(backward_kernel, images),
        in_specs=[full_spec()] * 10,
        out_specs=[full_spec()] * 4,
        out_shape=[
            jax.ShapeDtypeStruct((tokens, WIDTH), BF),
            jax.ShapeDtypeStruct((SLOT, WIDTH), F32),
            jax.ShapeDtypeStruct((8, WIDTH), F32),
            jax.ShapeDtypeStruct((HEADS, WIDTH), F32),
        ],
        scratch_shapes=[
            pltpu.VMEM((images * HEADS, WIDTH), BF),
            pltpu.VMEM((images * HEADS, WIDTH), BF),
        ],
        compiler_params=pltpu.CompilerParams(vmem_limit_bytes=40 * 2**20),
        cost_estimate=pl.CostEstimate(flops=10**9, bytes_accessed=8 * 2**20, transcendentals=0),
        name="backward",
    )(do, wv, hid, xhat, rstd, p, mass, qk, rows, shuffle)


def embed_grad_kernel(
    images, where_ref, pix_ref, pixp_ref, de_ref, dep_ref, pooled_ref, pooledp_ref, do_ref,
    dop_ref, own_ref, x_ref, y_ref, d_ref,
):
    col = where_ref[0]
    rows = images * HEADS
    for source, out_ref in ((3, d_ref), (1, x_ref), (2, y_ref), (0, own_ref)):
        block = col ^ source

        @pl.when(block < 3)
        def _():
            lanes = pl.ds(pl.multiple_of(block * 512, 128), 512)
            total = dot(pix_ref[:, lanes], de_ref[...], TN) + dot(pixp_ref[:, lanes], dep_ref[...], TN)
            out_ref[...] = total.astype(out_ref.dtype)

        @pl.when(block == 3)
        def _():
            total = None
            for pooled, do in ((pooled_ref, do_ref), (pooledp_ref, dop_ref)):
                spread = jnp.broadcast_to(
                    do[...].reshape(images, 1, WIDTH).astype(F32), (images, HEADS, WIDTH)
                )
                wide = low(jnp.where(head_mask(rows), spread.reshape(rows, WIDTH), 0.0))
                term = dot(pooled[...], wide, TN)
                total = term if total is None else total + term
            out_ref[...] = total.astype(out_ref.dtype)


def embed_grad_call(images, where, pix, pixp, de, dep, pooled, pooledp, do, dop):
    return pl.pallas_call(
        functools.partial(embed_grad_kernel, images),
        in_specs=[smem_spec()] + [full_spec()] * 8,
        out_specs=[full_spec()] * 4,
        out_shape=[
            jax.ShapeDtypeStruct((512, WIDTH), F32),
            jax.ShapeDtypeStruct((512, WIDTH), BF),
            jax.ShapeDtypeStruct((512, WIDTH), BF),
            jax.ShapeDtypeStruct((512, WIDTH), BF),
        ],
        compiler_params=pltpu.CompilerParams(vmem_limit_bytes=40 * 2**20),
        cost_estimate=pl.CostEstimate(flops=4 * 10**9, bytes_accessed=12 * 2**20, transcendentals=0),
        name="embed_grad",
    )(where, pix, pixp, de, dep, pooled, pooledp, do, dop)


CHIPS = 16
FLIP_X = [(i, i ^ 1) for i in range(CHIPS)]
FLIP_Y = [(i, i ^ 2) for i in range(CHIPS)]
FLIP_CORE = [(0, 1), (1, 0)]
CHUNKS = 2


def hop(values, pairs):
    return lax.ppermute(values, "img", pairs)


def swap(values):
    return lax.ppermute(values, "seq", FLIP_CORE)


def among(img, chips):
    hit = img == chips[0]
    for chip in chips[1:]:
        hit = hit | (img == chip)
    return hit


def spread_blocks(base, img, sources, rounds):
    got = []
    for pairs, sent in rounds:
        got.append(hop(base if sent < 0 else got[sent], pairs))
    total = jnp.where(among(img, sources), base, jnp.zeros_like(base))
    for part in got:
        total = total + part
    return total


def plane_gather(block):
    half = block.shape[0] // 2
    by_x, by_y = hop(block, FLIP_X), hop(block, FLIP_Y)
    first, second = hop(by_y[:half], FLIP_X), hop(by_x[half:], FLIP_Y)
    return [block, by_x, by_y, first, second]


def everywhere(values):
    sent = jnp.broadcast_to(values[None], (CHIPS,) + values.shape)
    got = lax.all_to_all(sent, "img", 0, 0, tiled=True)
    got = got.reshape((CHIPS * values.shape[0],) + values.shape[1:])
    return jnp.concatenate([got, swap(got)], axis=0)


def back_home(partial, images, sources):
    half = partial.shape[0] // 2
    mine = partial[:half] + swap(partial[half:])
    sent = low(mine).reshape(CHIPS, images, partial.shape[-1])
    got = lax.all_to_all(sent, "img", 0, 0, tiled=True)
    return jnp.sum(got[sources[0] : sources[-1] + 1].astype(F32), axis=0)


def from_all(values):
    sent = jnp.broadcast_to(values[None], (2 * CHIPS,) + values.shape)
    return lax.all_to_all(sent, ("img", "seq"), 0, 0, tiled=True)


def natural(values):
    lead = values.shape[:-2]
    units = values.shape[-1] // 16
    split = values.reshape(lead + (2, units, 16))
    return jnp.swapaxes(split, -3, -2).reshape(lead + (units * 32,))


def halves(values):
    lead = values.shape[:-1]
    units = values.shape[-1] // 32
    return jnp.swapaxes(values.reshape(lead + (units, 2, 16)), -3, -2).reshape(
        lead + (2, units * 16)
    )


FF_CHIPS = (7, 8, 9, 10)
T1_SOURCES = (0, 1, 2, 7)
T1_ROUNDS = [
    ([(0, 4), (1, 5), (2, 6), (7, 11)], -1),
    ([(4, 8), (5, 9), (6, 10), (11, 15)], 0),
    ([(8, 12), (9, 13), (10, 14)], 1),
    ([(7, 3)], -1),
]
T2_SOURCES = (4, 1, 6, 15)
T2_ROUNDS = [
    ([(4, 8), (1, 5), (6, 10), (15, 11)], -1),
    ([(8, 12), (5, 9), (10, 14), (11, 7)], 0),
    ([(9, 13), (7, 3)], 1),
    ([(4, 0), (6, 2)], -1),
]


def per_device_16(
    pixels, keep_mask, partner_index, partner_emb, masters, first_moment_slots,
    second_moment_slots, slot_unit_index, small_params, small_first, small_second, step_count,
):
    img, core = lax.axis_index("img"), lax.axis_index("seq")
    col = img % 4
    images = pixels.shape[0]
    total_images = images * 2 * CHIPS
    slots = masters.shape[0]
    where = jnp.stack([col, core]).astype(jnp.int32)
    shuffle = shuffle_matrix()
    (
        class_row, pos_rows, patch_bias, gain_one, shift_one, query_bias, value_bias, out_bias,
        gain_two, shift_two, fc_in_bias, fc_out_bias, gain_end, shift_end,
    ) = small_parts(small_params)
    class_state = class_row + pos_rows[0]

    near = slots_near(slot_unit_index, img, slots)
    own_w = to_units(low(masters), near, img, CHIPS).reshape(512, WIDTH)

    step = 512 // CHUNKS
    pieces, own_pieces = [], []
    for chunk in range(CHUNKS):
        part = own_w[step * chunk : step * (chunk + 1)]
        base = jnp.where(img == 7, hop(part, [(5, 7)]), part)
        block = spread_blocks(base, img, T1_SOURCES, T1_ROUNDS)
        got = plane_gather(block)
        first = step * chunk
        pieces += [
            (0, first, step), (1, first, step), (2, first, step),
            (3, first, step // 2), (3, first + step // 2, step // 2),
        ]
        own_pieces += got
    peer_pieces = [swap(piece) for piece in own_pieces]

    base = jnp.where(img == 1, hop(own_w, [(3, 1)]), own_w)
    got = plane_gather(spread_blocks(base, img, T2_SOURCES, T2_ROUNDS))
    table = jnp.zeros((4, 512, WIDTH), BF)
    table = lax.dynamic_update_slice(table, got[0][None], (col, 0, 0))
    table = lax.dynamic_update_slice(table, got[1][None], (col ^ 1, 0, 0))
    table = lax.dynamic_update_slice(table, got[2][None], (col ^ 2, 0, 0))
    table = lax.dynamic_update_slice(table, got[3][None], (col ^ 3, 0, 0))
    table = lax.dynamic_update_slice(table, got[4][None], (col ^ 3, 256, 0))
    table_peer = swap(table)

    def both(block, rows=512):
        mine, theirs = table[block, :rows], table_peer[block, :rows]
        return jnp.where(core == 0, mine, theirs), jnp.where(core == 0, theirs, mine)

    w_two = hop(own_w, [(11, 7), (12, 8), (13, 9), (14, 10)])

    class_hidden = low(layer_norm(class_state, gain_one, shift_one))
    class_halves = halves(class_hidden)
    class_half = jnp.where(core == 0, class_halves[0], class_halves[1])
    query_parts = from_all(dot(class_half[None], own_w))
    query = low((query_parts[6, 0] + query_parts[7, 0] + query_bias) * SCALE)
    mask16 = head_mask(HEADS)
    query_heads = jnp.where(mask16, query[None], jnp.zeros((), BF))
    pulled = from_all(low(dot(query_heads, own_w, NT)))
    qk = natural(jnp.stack([pulled[8], pulled[9]], axis=1))

    padded = jnp.pad(pixels, ((0, 0), (0, SLOT - PATCHES), (0, 0)))
    pix = prep(padded, shuffle).reshape(2, images * SLOT, PIX // 2)
    pix_own = jnp.where(core == 0, pix[0], pix[1])
    pix_peer = swap(jnp.where(core == 0, pix[1], pix[0]))

    add_image = jnp.concatenate(
        [
            pos_rows[1:] + patch_bias,
            class_state[None],
            jnp.zeros((SLOT - TOKS, WIDTH), F32),
        ],
        axis=0,
    )
    add = jnp.tile(add_image, (images, 1))
    valid = jnp.concatenate(
        [
            keep_mask,
            jnp.ones((images, 1), jnp.int32),
            jnp.zeros((images, SLOT - TOKS), jnp.int32),
        ],
        axis=1,
    ).reshape(images * SLOT, 1)
    rows = jnp.stack([gain_one, shift_one, value_bias] + [jnp.zeros_like(gain_one)] * 5)
    hid, xhat, rstd, p, pooled, mass, wv, attended = forward_call(
        pieces, images, where, pix, own_pieces, peer_pieces, add, rows, qk, valid, shuffle
    )

    wo = both(2)
    resid = class_state + dot(attended[0], wo[0]) + dot(attended[1], wo[1]) + out_bias
    hidden_two = low(layer_norm(resid, gain_two, shift_two))
    hidden_all = everywhere(hidden_two)
    ff_block = jnp.clip(img - FF_CHIPS[0], 0, 3)
    is_ff = among(img, FF_CHIPS)
    bias_part = lax.dynamic_slice(
        fc_in_bias.reshape(4, 32, 2, 16), (ff_block, 0, core, 0), (1, 32, 1, 16)
    ).reshape(512)
    preact = dot(hidden_all, own_w, NT) + bias_part
    active = low(exact_gelu(preact))
    state = resid + back_home(dot(active, w_two), images, FF_CHIPS) + fc_out_bias
    final = low(layer_norm(state, gain_end, shift_end))
    proj = both(3, PROJ // 2)
    projected = jnp.concatenate([dot(final, proj[0], NT), dot(final, proj[1], NT)], axis=1)

    partners = everywhere(halves(partner_emb).reshape(images, PROJ))
    unit = low(normalize(projected))
    logits = dot(unit, partners, NT) / SOFTMAX_SCALE
    ids = jnp.arange(CHIPS, dtype=jnp.int32)[None, :, None] * (2 * images)
    ids = ids + (core ^ jnp.arange(2, dtype=jnp.int32))[:, None, None] * images
    ids = (ids + jnp.arange(images, dtype=jnp.int32)[None, None, :]).reshape(1, total_images)
    onehot = (ids == partner_index[:, None]).astype(F32)
    total = jax.nn.logsumexp(logits, axis=-1)
    target = jnp.sum(logits * onehot, axis=-1)
    loss_part = jnp.sum(total - target) / total_images
    d_logits = (jax.nn.softmax(logits, axis=-1) - onehot) / total_images
    d_unit = dot(low(d_logits / SOFTMAX_SCALE), partners)
    d_projected = low(jax.vjp(normalize, projected)[1](d_unit)[0])
    d_final = dot(d_projected[:, : PROJ // 2], proj[0]) + dot(d_projected[:, PROJ // 2 :], proj[1])
    d_state, d_gain_end, d_shift_end = jax.vjp(layer_norm, state, gain_end, shift_end)[1](d_final)
    d_state_low = low(d_state)
    d_state_all = everywhere(d_state_low)
    d_active = dot(d_state_all, w_two, NT)
    d_preact = low(jax.vjp(exact_gelu, preact)[1](d_active)[0])
    d_preact = jnp.where(is_ff, d_preact, jnp.zeros((), BF))
    d_hidden_two = back_home(dot(d_preact, own_w), images, FF_CHIPS)
    d_norm, d_gain_two, d_shift_two = jax.vjp(layer_norm, resid, gain_two, shift_two)[1](
        d_hidden_two
    )
    d_resid = d_state + d_norm
    d_resid_low = low(d_resid)
    d_attended = low(
        natural(jnp.stack([dot(d_resid_low, wo[0], NT), dot(d_resid_low, wo[1], NT)], axis=1))
    )

    d_embed, d_pos, d_vec, pull = backward_call(
        images, d_attended, wv, hid, xhat, rstd, p, mass, qk, rows, shuffle
    )
    pooled_own = jnp.where(core == 0, pooled[0], pooled[1])
    pooled_peer = swap(jnp.where(core == 0, pooled[1], pooled[0]))
    grad_own, grad_x, grad_y, grad_d = embed_grad_call(
        images, where, pix_own, pix_peer, d_embed, swap(d_embed), pooled_own, pooled_peer,
        d_attended, swap(d_attended),
    )
    reduced = []
    for chunk in range(CHUNKS):
        first, middle, last = step * chunk, step * chunk + step // 2, step * (chunk + 1)
        to_y = hop(grad_d[first:middle], FLIP_X)
        to_x = hop(grad_d[middle:last], FLIP_Y)
        send_y = jnp.concatenate(
            [low(grad_y[first:middle].astype(F32) + to_y.astype(F32)), grad_y[middle:last]], axis=0
        )
        send_x = jnp.concatenate(
            [grad_x[first:middle], low(grad_x[middle:last].astype(F32) + to_x.astype(F32))], axis=0
        )
        got_x, got_y = hop(send_x, FLIP_X), hop(send_y, FLIP_Y)
        acc = grad_own[first:last] + got_x.astype(F32) + got_y.astype(F32)
        got = hop(low(acc), [(12, 8), (13, 9), (14, 10), (15, 11), (3, 7)])
        acc = acc + got.astype(F32)
        got = hop(low(acc), [(8, 4), (9, 5), (10, 6), (11, 7)])
        acc = acc + got.astype(F32)
        got = hop(low(acc), [(4, 0), (5, 1), (6, 2), (7, 5)]).astype(F32)
        reduced.append(jnp.where(img == 5, got, acc + got))
    reduced = jnp.concatenate(reduced, axis=0)

    wk, wq = both(0), both(1)
    pull_halves = low(halves(pull))
    d_query = jnp.where(mask16, dot(pull_halves[:, 0], wk[0]) + dot(pull_halves[:, 1], wk[1]), 0.0)
    d_query = jnp.sum(d_query, axis=0, keepdims=True) * SCALE
    d_query_low = low(d_query)
    d_class_hidden = natural(
        jnp.stack([dot(d_query_low, wq[0], NT), dot(d_query_low, wq[1], NT)], axis=1)
    )
    d_class, d_gain_cls, d_shift_cls = jax.vjp(layer_norm, class_state[None], gain_one, shift_one)[
        1
    ](d_class_hidden)
    d_resid_sum = jnp.sum(d_resid, axis=0)
    d_class = d_class[0] + d_pos[PATCHES] + d_resid_sum
    bias_sum = jnp.sum(d_preact.astype(F32), axis=0).reshape(1, 32, 1, 16)
    d_fc_in_bias = lax.dynamic_update_slice(
        jnp.zeros((4, 32, 2, 16), F32), bias_sum, (ff_block, 0, core, 0)
    ).reshape(FF // WIDTH, WIDTH)
    small_local = jnp.concatenate(
        [
            d_class[None],
            d_class[None],
            d_pos[:PATCHES],
            jnp.sum(d_pos[:PATCHES], axis=0, keepdims=True),
            (d_vec[0] + d_gain_cls)[None],
            (d_vec[1] + d_shift_cls)[None],
            d_query,
            d_vec[2:3],
            d_resid_sum[None],
            d_gain_two[None],
            d_shift_two[None],
            d_fc_in_bias,
            jnp.sum(d_state, axis=0, keepdims=True),
            d_gain_end[None],
            d_shift_end[None],
            pull,
            jnp.broadcast_to(loss_part, (1, WIDTH)),
            jnp.zeros((13, WIDTH), F32),
        ],
        axis=0,
    )
    shares = lax.all_to_all(small_local.reshape(32, 3, WIDTH), ("img", "seq"), 0, 0, tiled=True)
    small_total = from_all(jnp.sum(shares, axis=0)).reshape(96, WIDTH)
    small_grad, pull_total, loss = small_total[:66], small_total[66:82], small_total[82, 0]

    extra = jnp.concatenate(
        [attended[0], attended[1], d_resid_low, d_projected, final], axis=1
    )
    extra, d_embed = lax.optimization_barrier((extra, d_embed))
    extra = everywhere(extra)
    att_half = jnp.where(core == 0, extra[:, :512], extra[:, 512:1024])
    proj_half = jnp.where(core == 0, extra[:, 2048 : 2048 + 384], extra[:, 2048 + 384 : 2816])
    proj_half = jnp.pad(proj_half, ((0, 0), (0, 128)))
    left = jnp.where(img == 6, att_half, jnp.where(img == 15, proj_half, d_preact))
    right = jnp.where(
        img == 6, extra[:, 1024:2048], jnp.where(img == 15, extra[:, 2816:], hidden_all)
    )
    formed = dot(left, right, TN)
    from_ff = hop(
        low(dot(active, d_state_all, TN)), [(7, 11), (8, 12), (9, 13), (10, 14)]
    ).astype(F32)
    pull_half = halves(pull_total)
    pull_half = jnp.where(core == 0, pull_half[:, 0], pull_half[:, 1])
    key_grad = dot(pull_half, query_heads.astype(F32), TN, precision=lax.Precision.HIGHEST)
    query_grad = class_half.astype(F32)[:, None] * small_total[54][None, :]
    own_grad = jnp.where(among(img, (0, 1, 2, 5)), reduced, formed)
    own_grad = jnp.where(among(img, (11, 12, 13, 14)), from_ff, own_grad)
    own_grad = jnp.where(img == 3, query_grad, jnp.where(img == 4, key_grad, own_grad))

    squares = jnp.broadcast_to(jnp.sum(own_grad * own_grad), (1, 128))
    owner_total = jnp.sum(from_all(squares)[:, 0, 0])
    grad_norm = jnp.sqrt(owner_total + jnp.sum(small_grad * small_grad))
    factor = 1.0 / jnp.maximum(grad_norm, 1.0)
    slot_grad = to_slots(own_grad.reshape(slots, 16, WIDTH), near, img, CHIPS)
    step_value = step_count.astype(F32)
    new_masters, new_first, new_second = adamw(
        masters, slot_grad * factor, first_moment_slots, second_moment_slots, step_value
    )
    new_small, new_small_first, new_small_second = adamw(
        small_params, small_grad * factor, small_first, small_second, step_value
    )
    return (
        new_masters, new_first, new_second, new_small, new_small_first, new_small_second,
        loss, grad_norm,
    )


def per_device_any(
    pixels, keep_mask, partner_index, partner_emb, masters, first_moment_slots,
    second_moment_slots, slot_unit_index, small_params, small_first, small_second, step_count,
):
    chips, seq = lax.axis_size("img"), lax.axis_size("seq")
    img = lax.axis_index("img")
    images = pixels.shape[0]
    slots, part = masters.shape[0], masters.shape[1]
    near = slots_near(slot_unit_index, img, slots)
    own_w = to_units(low(masters), near, img, chips)
    gathered = lax.all_gather(own_w, ("img", "seq"), axis=0, tiled=False)
    flat = gathered.reshape(chips, seq, slots, part, WIDTH).transpose(0, 2, 1, 3, 4)
    flat = flat.reshape(chips * slots * ROWS_PER_UNIT, WIDTH)
    bounds = [0, PIX, WIDTH, WIDTH, WIDTH, WIDTH, FF, FF, PROJ]
    parts, offset = [], 0
    for size in bounds[1:]:
        parts.append(flat[offset : offset + size])
        offset += size
    embed_w, query_w, key_w, value_w, output_w, fc_in_w, fc_out_w, proj_w = parts
    (
        class_row, pos_rows, patch_bias, gain_one, shift_one, query_bias, value_bias, out_bias,
        gain_two, shift_two, fc_in_bias, fc_out_bias, gain_end, shift_end,
    ) = small_parts(small_params)
    class_state = class_row + pos_rows[0]
    embedded = jnp.einsum("itp,pd->itd", pixels, embed_w, preferred_element_type=F32)
    tokens = jnp.concatenate(
        [
            jnp.broadcast_to(class_state, (images, 1, WIDTH)),
            embedded + patch_bias + pos_rows[1:],
        ],
        axis=1,
    )
    hidden = low(layer_norm(tokens, gain_one, shift_one))
    class_hidden = hidden[0, 0]
    mask16 = head_mask(HEADS)
    query = low((dot(class_hidden[None], query_w)[0] + query_bias) * SCALE)
    query_heads = jnp.where(mask16, query[None], jnp.zeros((), BF))
    qk = low(dot(query_heads, key_w, NT))
    scores = jnp.einsum("hd,itd->iht", qk, hidden, preferred_element_type=F32)
    keep = jnp.concatenate([jnp.ones((images, 1), jnp.int32), keep_mask], axis=1)
    scores = jnp.where(keep[:, None, :] > 0, scores, MASKED)
    weights = jax.nn.softmax(scores, axis=-1)
    weights_low = low(weights)
    pooled = low(jnp.einsum("iht,itd->ihd", weights_low, hidden, preferred_element_type=F32))
    mass = jnp.sum(weights_low.astype(F32), axis=-1)
    mixed = dot(pooled.reshape(-1, WIDTH), value_w).reshape(images, HEADS, WIDTH)
    mixed = mixed + mass[:, :, None] * value_bias
    attended = low(jnp.sum(jnp.where(mask16, mixed, 0.0), axis=1))
    resid = class_state + dot(attended, output_w) + out_bias
    hidden_two = low(layer_norm(resid, gain_two, shift_two))
    preact = dot(hidden_two, fc_in_w, NT) + fc_in_bias
    active = low(exact_gelu(preact))
    state = resid + dot(active, fc_out_w) + fc_out_bias
    final = low(layer_norm(state, gain_end, shift_end))
    projected = dot(final, proj_w, NT)
    unit = low(normalize(projected))
    partners = lax.all_gather(partner_emb, ("img", "seq"), axis=0, tiled=True)
    count = partners.shape[0]
    logits = dot(unit, partners, NT) / SOFTMAX_SCALE
    onehot = (jnp.arange(count, dtype=jnp.int32)[None] == partner_index[:, None]).astype(F32)
    total = jax.nn.logsumexp(logits, axis=-1)
    loss_part = jnp.sum(total - jnp.sum(logits * onehot, axis=-1)) / count
    d_logits = (jax.nn.softmax(logits, axis=-1) - onehot) / count
    d_unit = dot(low(d_logits / SOFTMAX_SCALE), partners)
    d_projected = low(jax.vjp(normalize, projected)[1](d_unit)[0])
    d_final = dot(d_projected, proj_w)
    d_state, d_gain_end, d_shift_end = jax.vjp(layer_norm, state, gain_end, shift_end)[1](d_final)
    d_state_low = low(d_state)
    d_active = dot(d_state_low, fc_out_w, NT)
    d_preact = low(jax.vjp(exact_gelu, preact)[1](d_active)[0])
    d_hidden_two = dot(d_preact, fc_in_w)
    d_norm, d_gain_two, d_shift_two = jax.vjp(layer_norm, resid, gain_two, shift_two)[1](
        d_hidden_two
    )
    d_resid = d_state + d_norm
    d_resid_low = low(d_resid)
    d_attended = low(dot(d_resid_low, output_w, NT))
    wide = jnp.where(mask16, d_attended[:, None, :], jnp.zeros((), BF))
    d_pooled = low(dot(wide.reshape(-1, WIDTH), value_w, NT)).reshape(images, HEADS, WIDTH)
    d_weights = jnp.einsum("ihd,itd->iht", d_pooled, hidden, preferred_element_type=F32)
    d_weights = d_weights + jnp.sum(wide.astype(F32) * value_bias, axis=-1)[:, :, None]
    d_scores = low(weights * (d_weights - jnp.sum(weights * d_weights, axis=-1, keepdims=True)))
    d_hidden = jnp.einsum("iht,ihd->itd", weights_low, d_pooled, preferred_element_type=F32)
    d_hidden = d_hidden + jnp.einsum("iht,hd->itd", d_scores, qk, preferred_element_type=F32)
    pull = jnp.einsum("iht,itd->hd", d_scores, hidden, preferred_element_type=F32)
    d_query = jnp.sum(jnp.where(mask16, dot(low(pull), key_w), 0.0), axis=0) * SCALE
    d_class_hidden = dot(low(d_query)[None], query_w, NT)
    d_tokens, d_gain_one, d_shift_one = jax.vjp(layer_norm, tokens, gain_one, shift_one)[1](
        d_hidden
    )
    d_class, d_gain_cls, d_shift_cls = jax.vjp(layer_norm, class_state[None], gain_one, shift_one)[
        1
    ](d_class_hidden)
    d_class = d_class[0] + jnp.sum(d_tokens[:, 0], axis=0) + jnp.sum(d_resid, axis=0)
    d_patch = d_tokens[:, 1:]
    d_embed_w = jnp.einsum("itp,itd->pd", pixels, low(d_patch), preferred_element_type=F32)
    d_value_w = dot(pooled.reshape(-1, WIDTH), wide.reshape(-1, WIDTH), TN)
    d_key_w = dot(pull, query_heads.astype(F32), TN, precision=lax.Precision.HIGHEST)
    small_local = jnp.concatenate(
        [
            d_class[None],
            d_class[None],
            jnp.sum(d_patch, axis=0),
            jnp.sum(d_patch, axis=(0, 1))[None],
            (d_gain_one + d_gain_cls)[None],
            (d_shift_one + d_shift_cls)[None],
            d_query[None],
            jnp.sum(wide.astype(F32) * mass[:, :, None], axis=(0, 1))[None],
            jnp.sum(d_resid, axis=0)[None],
            d_gain_two[None],
            d_shift_two[None],
            jnp.sum(d_preact.astype(F32), axis=0).reshape(FF // WIDTH, WIDTH),
            jnp.sum(d_state, axis=0)[None],
            d_gain_end[None],
            d_shift_end[None],
        ],
        axis=0,
    )
    grad_table = jnp.concatenate(
        [
            d_embed_w,
            class_hidden.astype(F32)[:, None] * d_query[None, :],
            d_key_w,
            d_value_w,
            dot(attended, d_resid_low, TN),
            dot(d_preact, hidden_two, TN),
            dot(active, d_state_low, TN),
            dot(d_projected, final, TN),
            jnp.zeros(((chips * slots - UNIT_COUNT) * ROWS_PER_UNIT, WIDTH), F32),
        ],
        axis=0,
    ).reshape(chips * slots, ROWS_PER_UNIT, WIDTH)
    small_grad, loss = lax.psum((small_local, loss_part), ("img", "seq"))
    core_half = lax.psum_scatter(low(grad_table), "seq", scatter_dimension=1, tiled=True)
    own_grad = lax.psum_scatter(core_half.astype(F32), "img", scatter_dimension=0, tiled=True)
    owner_total = lax.psum(jnp.sum(own_grad * own_grad), ("img", "seq"))
    grad_norm = jnp.sqrt(owner_total + jnp.sum(small_grad * small_grad))
    factor = 1.0 / jnp.maximum(grad_norm, 1.0)
    slot_grad = to_slots(own_grad, near, img, chips)
    step_value = step_count.astype(F32)
    new_masters, new_first, new_second = adamw(
        masters, slot_grad * factor, first_moment_slots, second_moment_slots, step_value
    )
    new_small, new_small_first, new_small_second = adamw(
        small_params, small_grad * factor, small_first, small_second, step_value
    )
    return (
        new_masters, new_first, new_second, new_small, new_small_first, new_small_second,
        loss, grad_norm,
    )


def solution(mesh):
    sixteen = mesh.shape["img"] == CHIPS and mesh.shape["seq"] == 2
    return jax.shard_map(
        per_device_16 if sixteen else per_device_any,
        mesh=mesh,
        in_specs=(
            P(("img", "seq"), None, None),
            P(("img", "seq"), None),
            P(("img", "seq")),
            P(("img", "seq"), None),
            P("img", "seq", None),
            P("img", "seq", None),
            P("img", "seq", None),
            P(),
            P(),
            P(),
            P(),
            P(),
        ),
        out_specs=(
            P("img", "seq", None),
            P("img", "seq", None),
            P("img", "seq", None),
            P(),
            P(),
            P(),
            P(),
            P(),
        ),
        check_vma=False,
    )
```

time: 1430 us -> 627 us (0.44)
  waiting for transfers between devices: 1000 us -> 212 us
  starting transfers between devices: 0.16 us -> 180 us
  blocking collectives: 89.8 us -> 12.5 us
  local copies, waits for them, and re-layouts: 133 us -> 67.9 us
  matrix products: 74.3 us -> 36.4 us
  other arithmetic: 103 us -> 69.9 us
  Pallas kernels: 0 us -> 28.7 us
    reduce_scatter x2 -> x0, waiting for transfers between devices: 720 us -> none  [the longest x1 676 us: per_device(): owned = lax.psum_scatter(core_half, 'img', scatter_dimension=0, tiled=True)]
    ppermute x0 -> x68, waiting for transfers between devices: none -> 165 us  [the longest x43 157 us: hop(): return lax.ppermute(values, 'img', pairs)]
    all_gather x1 -> x0, waiting for transfers between devices: 147 us -> none  [per_device(): lax.all_gather(cast_bfloat_narrow(masters), ('img', 'seq'), axis=0, tiled...]
    psum x1 -> x0, waiting for transfers between devices: 134 us -> none  [per_device(): small_total, loss = lax.psum((small_grad, loss_part), ('img', 'seq'))]
    ppermute x0 -> x68, starting transfers between devices: none -> 107 us  [the longest x43 93 us: hop(): return lax.ppermute(values, 'img', pairs)]
    all_to_all x0 -> x10, starting transfers between devices: none -> 72.7 us  [the longest x3 32.7 us: everywhere(): got = lax.all_to_all(sent, 'img', 0, 0, tiled=True)]
    gather x3 -> x0, local copies, waits for them, and re-layouts: 58.9 us -> none  [the longest x1 35.4 us: per_device(): jnp.take(gathered, rows_index, axis=0)]
    all_gather x1 -> x0, blocking collectives: 48.5 us -> none  [per_device(): lax.all_gather(partner_emb, ('img', 'seq'), axis=0, tiled=True)]
  transfers between devices with their start and end apart: 4 -> 78, of which waited for: 4 -> 31; matrix products, arithmetic and copies ran while one was open for 1% -> 18% of each run, Pallas kernels for 0% -> 5%
where the time goes in v1:
time: 627 us; the launch traced here: 617 us
  waiting for transfers between devices  212 us (34%)
  starting transfers between devices  180 us (29%)
  other arithmetic  69.9 us (11%)
  local copies, waits for them, and re-layouts  67.9 us (11%)
  matrix products  36.4 us (6%)
  Pallas kernels  28.7 us (5%)
  blocking collectives  12.5 us (2%)
  between operations  9.69 us (2%)
    ppermute x43, waiting for transfers between devices, hop(): return lax.ppermute(values, 'img', pairs)  157 us
    ppermute x43, starting transfers between devices, hop(): return lax.ppermute(values, 'img', pairs)  93 us
    dot_general x23, matrix products, dot(): lax.dot_general(a, b, (dims, ((), ())), precision=precision, preferred_el...  36.4 us
    all_to_all x3, starting transfers between devices, everywhere(): got = lax.all_to_all(sent, 'img', 0, 0, tiled=True)  32.7 us
    all_to_all x4, starting transfers between devices, from_all(): return lax.all_to_all(sent, ('img', 'seq'), 0, 0, tiled=True)  28.3 us
    unnamed x238, local copies, waits for them, and re-layouts  24.1 us
    all_to_all x3, waiting for transfers between devices, everywhere(): got = lax.all_to_all(sent, 'img', 0, 0, tiled=True)  18.7 us
    pallas_call x1, Pallas kernels, forward_call(): pl.pallas_call(functools.partial(forward_kernel, pieces, images), in_spec...  15.3 us
  transfers between devices with their start and end apart: 78, of which 31 were waited for; matrix products, arithmetic and copies ran while one was open for 18% of the time, Pallas kernels for 5%

profile of v1, /device:TPU:0, one launch (start us, length us, event | category | flops | bytes accessed | tf_op | source)
XLA Modules:
  0.0 617.2 jit_solution(3589904098685983818)
XLA Ops:
  2.4 4.8 collective-permute-start.1
  21.2 45.0 %collective-permute-done.34 = bf16[512,1024]{1,0:T(8,128)(2,1)} collective-permute-done((bf16[512,1024]{1,0:T(8,128)(2,1)S(1)}, bf16[512,1024]{1,0:T(8,128)(2,1)}, u32[]{:S(2)}, u32[]{:S(2)}) %collective-permute-start.34) | collective-permute-done | bytes 1048608 | tf_op jit(solution)/shard_map/ppermute | solution.py:389
  68.7 4.4 bitcast_dynamic-update-slice_fusion.2
  76.4 23.4 %collective-permute-start.36 = (bf16[512,1024]{1,0:T(8,128)(2,1)}, bf16[512,1024]{1,0:T(8,128)(2,1)S(1)}, u32[]{:S(2)}, u32[]{:S(2)}) collective-permute-start(bf16[512,1024]{1,0:T(8,128)(2,1)} %get-tuple-element.79), channel_id=1, source_target_pairs={{0,4},{2,6},{4,0},{6,2},{8,12},{10,14},{12,8},{14,10},{16,20},{18,... | collective-permute-start | bytes 3145736 | tf_op jit(solution)/shard_map/ppermute | solution.py:389
  110.4 9.0 %collective-permute-done.36 = bf16[512,1024]{1,0:T(8,128)(2,1)S(1)} collective-permute-done((bf16[512,1024]{1,0:T(8,128)(2,1)}, bf16[512,1024]{1,0:T(8,128)(2,1)S(1)}, u32[]{:S(2)}, u32[]{:S(2)}) %collective-permute-start.36) | collective-permute-done | bytes 1048608 | tf_op jit(solution)/shard_map/ppermute | solution.py:389
  119.4 18.4 %collective-permute-start.37 = (bf16[256,1024]{1,0:T(8,128)(2,1)S(1)}, bf16[256,1024]{1,0:T(8,128)(2,1)S(1)}, u32[]{:S(2)}, u32[]{:S(2)}) collective-permute-start(bf16[256,1024]{1,0:T(8,128)(2,1)S(1)} %slice.470), channel_id=1, source_target_pairs={{0,2},{2,0},{4,6},{6,4},{8,10},{10,8},{12,14},{14,12},{16,18},{18,... | collective-permute-start | bytes 1572872 | tf_op jit(solution)/shard_map/ppermute | solution.py:389
  140.1 4.8 collective-permute-done.37
  151.3 10.1 %collective-permute-done.12 = bf16[256,1024]{1,0:T(8,128)(2,1)S(1)} collective-permute-done((bf16[256,1024]{1,0:T(8,128)(2,1)S(1)}, bf16[256,1024]{1,0:T(8,128)(2,1)S(1)}, u32[]{:S(2)}, u32[]{:S(2)}) %collective-permute-start.12) | collective-permute-done | bytes 524320 | tf_op jit(solution)/shard_map/ppermute | solution.py:389
  167.3 5.4 collective-permute-start.7
  173.8 15.1 %all-to-all-start = ((f32[32,1,1024]{2,1,0:T(1,128)}), f32[32,1,1024]{2,1,0:T(1,128)S(1)}, u32[]{:S(2)}, u32[]{:S(2)}) async-start(f32[32,1,1024]{2,1,0:T(1,128)} %broadcast_in_dim.249), calls=%async_computation | async-start | bytes 262144 | tf_op jit(solution)/shard_map/all_to_all | solution.py:437
  199.8 7.1 %all-to-all-start.1 = ((bf16[32,16,512]{2,1,0:T(8,128)(2,1)}), bf16[32,16,512]{2,1,0:T(8,128)(2,1)}, u32[]{:S(2)}, u32[]{:S(2)}) async-start(bf16[32,16,512]{2,1,0:T(8,128)(2,1)} %broadcast_in_dim.253), calls=%async_computation.1 | async-start | bytes 1048576 | tf_op jit(solution)/shard_map/all_to_all | solution.py:437
  216.6 4.8 collective-permute-done.9.refs_3_
  222.4 4.2 collective-permute-done.18.refs_8_
  242.8 15.3 %forward.1 = (bf16[512,1024]{1,0:T(8,128)(2,1)}, f32[512,1024]{1,0:T(8,128)}, f32[512,128]{1,0:T(8,128)S(1)}, f32[512,16]{1,0:T(8,128)S(1)}, bf16[2,128,512]{2,1...) custom-call(s32[2]{0:T(128)S(1)} %pad_add_fusion.where_ref, ...), custom_call_target="tpu_custom_call" | custom-call | flops 4000000000 | bytes 18874368 | tf_op jit(solution)/shard_map/forward/pallas_call | solution.py:241
  265.0 6.7 %all-to-all-start.2 = ((bf16[16,8,1024]{2,1,0:T(8,128)(2,1)}), bf16[16,8,1024]{2,1,0:T(8,128)(2,1)S(1)}, u32[]{:S(2)}, u32[]{:S(2)}) async-start(bf16[16,8,1024]{2,1,0:T(8,128)(2,1)} %broadcast_in_dim.262), calls=%async_computation.2 | async-start | bytes 524288 | tf_op jit(solution)/shard_map/all_to_all | solution.py:422
  272.5 10.1 %all-to-all-done.2 = bf16[16,8,1024]{2,1,0:T(8,128)(2,1)S(1)} async-done(((bf16[16,8,1024]{2,1,0:T(8,128)(2,1)}), bf16[16,8,1024]{2,1,0:T(8,128)(2,1)S(1)}, u32[]{:S(2)}, u32[]{:S(2)}) %all-to-all-start.2) | async-done | bytes 262176 | tf_op jit(solution)/shard_map/all_to_all | solution.py:422
  291.3 20.2 %all-to-all-start.4 = ((bf16[16,8,768]{2,1,0:T(8,128)(2,1)}), bf16[16,8,768]{2,1,0:T(8,128)(2,1)S(1)}, u32[]{:S(2)}, u32[]{:S(2)}) async-start(bf16[16,8,768]{2,1,0:T(8,128)(2,1)} %broadcast_in_dim.264), calls=%async_computation.4 | async-start | bytes 393216 | tf_op jit(solution)/shard_map/all_to_all | solution.py:422
  312.4 8.5 %all-to-all-done.4 = bf16[16,8,768]{2,1,0:T(8,128)(2,1)S(1)} async-done(((bf16[16,8,768]{2,1,0:T(8,128)(2,1)}), bf16[16,8,768]{2,1,0:T(8,128)(2,1)S(1)}, u32[]{:S(2)}, u32[]{:S(2)}) %all-to-all-start.4) | async-done | bytes 196640 | tf_op jit(solution)/shard_map/all_to_all | solution.py:422
  324.8 9.1 %all-to-all-done.3 = bf16[16,8,1024]{2,1,0:T(8,128)(2,1)S(1)} async-done(((bf16[16,8,1024]{2,1,0:T(8,128)(2,1)}), bf16[16,8,1024]{2,1,0:T(8,128)(2,1)S(1)}, u32[]{:S(2)}, u32[]{:S(2)}) %all-to-all-start.3) | async-done | bytes 262176 | tf_op jit(solution)/shard_map/all_to_all | solution.py:431
  344.9 12.5 %all_to_all.55 = bf16[16,8,1024]{2,1,0:T(8,128)(2,1)S(1)} all-to-all(bf16[16,8,1024]{2,1,0:T(8,128)(2,1)S(1)} %broadcast_in_dim.268), channel_id=1, replica_groups=mesh['img'=16,'seq'=2] {'img'}, dimensions={0} | all-to-all | bytes 524288 | tf_op jit(solution)/shard_map/all_to_all | solution.py:422
  366.4 4.7 all-to-all-start.6
  427.6 12.9 %all-to-all-done.7 = f32[32,3,1024]{2,1,0:T(4,128)} async-done(((f32[32,3,1024]{2,1,0:T(4,128)}), f32[32,3,1024]{2,1,0:T(4,128)}, u32[]{:S(2)}, u32[]{:S(2)}) %all-to-all-start.7) | async-done | bytes 393248 | tf_op jit(solution)/shard_map/all_to_all | solution.py:676
  450.9 6.5 %embed_grad.1 = (f32[512,1024]{1,0:T(8,128)S(1)}, bf16[512,1024]{1,0:T(8,128)(2,1)S(1)}, bf16[512,1024]{1,0:T(8,128)(2,1)S(1)}, bf16[512,1024]{1,0:T(8,128)(2,1)S(1)}) custom-call(s32[2]{0:T(128)S(1)} %copy-done.29, bf16[512,1536]{1,0:T(8,128)(2,1)S(1)} %bitcast.174, bf16[512,1536]{1,0:T(8,128)(2,1)} %collective-permute-done.47.pixp_ref, ...), custom_call_target="tpu_custom_call" | custom-call | flops 4000000000 | bytes 12582912 | tf_op jit(solution)/shard_map/embed_grad/pallas_call | solution.py:365
  467.4 4.9 collective-permute-done.60
  476.5 5.8 all-to-all-start.9
  488.8 5.9 collective-permute-done.54
  494.7 12.7 %collective-permute-done.52 = bf16[256,1024]{1,0:T(8,128)(2,1)S(1)} collective-permute-done((bf16[256,1024]{1,0:T(8,128)(2,1)S(1)}, bf16[256,1024]{1,0:T(8,128)(2,1)S(1)}, u32[]{:S(2)}, u32[]{:S(2)}) %collective-permute-start.52) | collective-permute-done | bytes 524320 | tf_op jit(solution)/shard_map/ppermute | solution.py:389
  509.2 8.4 %collective-permute-done.59 = bf16[256,1024]{1,0:T(8,128)(2,1)S(1)} collective-permute-done((bf16[256,1024]{1,0:T(8,128)(2,1)S(1)}, bf16[256,1024]{1,0:T(8,128)(2,1)S(1)}, u32[]{:S(2)}, u32[]{:S(2)}) %collective-permute-start.59) | collective-permute-done | bytes 524320 | tf_op jit(solution)/shard_map/ppermute | solution.py:389
  543.6 26.8 %collective-permute-done.64 = bf16[256,1024]{1,0:T(8,128)(2,1)S(1)} collective-permute-done((bf16[256,1024]{1,0:T(8,128)(2,1)S(1)}, bf16[256,1024]{1,0:T(8,128)(2,1)S(1)}, u32[]{:S(2)}, u32[]{:S(2)}) %collective-permute-start.64) | collective-permute-done | bytes 524320 | tf_op jit(solution)/shard_map/ppermute | solution.py:389
  570.8 10.9 %collective-permute-done.57 = bf16[256,1024]{1,0:T(8,128)(2,1)S(1)} collective-permute-done((bf16[256,1024]{1,0:T(8,128)(2,1)S(1)}, bf16[256,1024]{1,0:T(8,128)(2,1)S(1)}, u32[]{:S(2)}, u32[]{:S(2)}) %collective-permute-start.57) | collective-permute-done | bytes 524320 | tf_op jit(solution)/shard_map/ppermute | solution.py:389
  582.0 4.6 multiply_reduce_fusion
  604.3 11.6 %multiply_subtract_fusion = (f32[32,16,1024]{2,1,0:T(8,128)}, f32[32,16,1024]{2,1,0:T(8,128)}, f32[32,16,1024]{2,1,0:T(8,128)}) fusion(f32[32,16,1024]{2,1,0:T(8,128)S(1)} %copy-done.36, f32[]{:T(128)S(6)} %sub.126, f32[32,16,1024]{2,1,0:T(8,128)} %param.18, f32[32,16,1024]{2,1,0:T(8,128)} %param.17, f32[]{:T(128)S(6)} %div.172, ...), kind=kLoop, calls=%fused_computation.21 | loop fusion | flops 12582912 | bytes 14942376 | tf_op jit(solution)/shard_map/sub | solution.py:91
  (565 shorter events, 252.6 us)
Async XLA Ops:
  18.1 48.0 %collective-permute-start.34 = (bf16[512,1024]{1,0:T(8,128)(2,1)S(1)}, bf16[512,1024]{1,0:T(8,128)(2,1)}, u32[]{:S(2)}, u32[]{:S(2)}) collective-permute-start(bf16[512,1024]{1,0:T(8,128)(2,1)S(1)} %broadcast_select_fusion.2), channel_id=1, source_target_pairs={{8,0},{12,4},{9,1},{13,5}} | collective-permute-start | bytes 3145736 | tf_op jit(solution)/shard_map/ppermute | solution.py:389
  19.4 46.7 %collective-permute-start.33 = (bf16[512,1024]{1,0:T(8,128)(2,1)}, bf16[512,1024]{1,0:T(8,128)(2,1)}, u32[]{:S(2)}, u32[]{:S(2)}) collective-permute-start(bf16[512,1024]{1,0:T(8,128)(2,1)} %collective-permute-done.32), channel_id=1, source_target_pairs={{18,26},{14,6},{19,27},{15,7}} | collective-permute-start | bytes 3145736 | tf_op jit(solution)/shard_map/ppermute | solution.py:389
  73.1 64.7 %collective-permute-start.35 = (bf16[512,1024]{1,0:T(8,128)(2,1)}, bf16[512,1024]{1,0:T(8,128)(2,1)S(1)}, u32[]{:S(2)}, u32[]{:S(2)}) collective-permute-start(bf16[512,1024]{1,0:T(8,128)(2,1)} %get-tuple-element.79), channel_id=1, source_target_pairs={{0,2},{2,0},{4,6},{6,4},{8,10},{10,8},{12,14},{14,12},{16,18},{18,... | collective-permute-start | bytes 3145736 | tf_op jit(solution)/shard_map/ppermute | solution.py:389
  76.4 42.9 %collective-permute-start.36 = (bf16[512,1024]{1,0:T(8,128)(2,1)}, bf16[512,1024]{1,0:T(8,128)(2,1)S(1)}, u32[]{:S(2)}, u32[]{:S(2)}) collective-permute-start(bf16[512,1024]{1,0:T(8,128)(2,1)} %get-tuple-element.79), channel_id=1, source_target_pairs={{0,4},{2,6},{4,0},{6,2},{8,12},{10,14},{12,8},{14,10},{16,20},{18,... | collective-permute-start | bytes 3145736 | tf_op jit(solution)/shard_map/ppermute | solution.py:389
  107.1 40.8 %collective-permute-start.11 = (bf16[256,1024]{1,0:T(8,128)(2,1)}, bf16[256,1024]{1,0:T(8,128)(2,1)S(1)}, u32[]{:S(2)}, u32[]{:S(2)}) collective-permute-start(bf16[256,1024]{1,0:T(8,128)(2,1)} %bitcast.188), channel_id=1, source_target_pairs={{10,14},{11,15}} | collective-permute-start | bytes 1572872 | tf_op jit(solution)/shard_map/ppermute | solution.py:389
  108.9 41.0 %collective-permute-start.3 = (bf16[256,1024]{1,0:T(8,128)(2,1)S(1)}, bf16[256,1024]{1,0:T(8,128)(2,1)S(1)}, u32[]{:S(2)}, u32[]{:S(2)}) collective-permute-start(bf16[256,1024]{1,0:T(8,128)(2,1)S(1)} %broadcast_select_fusion.10), channel_id=1, source_target_pairs={{0,8},{2,10},{4,12},{14,22},{1,9},{3,11},{5,13},{15,23}} | collective-permute-start | bytes 1572872 | tf_op jit(solution)/shard_map/ppermute | solution.py:389
  119.4 25.5 %collective-permute-start.37 = (bf16[256,1024]{1,0:T(8,128)(2,1)S(1)}, bf16[256,1024]{1,0:T(8,128)(2,1)S(1)}, u32[]{:S(2)}, u32[]{:S(2)}) collective-permute-start(bf16[256,1024]{1,0:T(8,128)(2,1)S(1)} %slice.470), channel_id=1, source_target_pairs={{0,2},{2,0},{4,6},{6,4},{8,10},{10,8},{12,14},{14,12},{16,18},{18,... | collective-permute-start | bytes 1572872 | tf_op jit(solution)/shard_map/ppermute | solution.py:389
  147.9 110.3 %collective-permute-start.39 = (bf16[4,512,1024]{2,1,0:T(8,128)(2,1)}, bf16[4,512,1024]{2,1,0:T(8,128)(2,1)}, u32[]{:S(2)}, u32[]{:S(2)}) collective-permute-start(bf16[4,512,1024]{2,1,0:T(8,128)(2,1)} %bitcast_dynamic-update-slice_fusion.3), channel_id=1, source_target_pairs={{0,1},{1,0},{2,3},{3,2},{4,5},{5,4},{6,7},{7,6},{8,9},{9,8},{10,11... | collective-permute-start | bytes 12582920 | tf_op jit(solution)/shard_map/ppermute | solution.py:393
  164.3 24.6 %collective-permute-start.15 = (bf16[256,1024]{1,0:T(8,128)(2,1)S(1)}, bf16[256,1024]{1,0:T(8,128)(2,1)}, u32[]{:S(2)}, u32[]{:S(2)}) collective-permute-start(bf16[256,1024]{1,0:T(8,128)(2,1)S(1)} %broadcast_select_fusion.9), channel_id=1, source_target_pairs={{14,6},{15,7}} | collective-permute-start | bytes 1572872 | tf_op jit(solution)/shard_map/ppermute | solution.py:389
  165.7 23.2 %collective-permute-start.14 = (bf16[256,1024]{1,0:T(8,128)(2,1)}, bf16[256,1024]{1,0:T(8,128)(2,1)}, u32[]{:S(2)}, u32[]{:S(2)}) collective-permute-start(bf16[256,1024]{1,0:T(8,128)(2,1)} %collective-permute-done.13), channel_id=1, source_target_pairs={{16,24},{18,26},{20,28},{17,25},{19,27},{21,29}} | collective-permute-start | bytes 1572872 | tf_op jit(solution)/shard_map/ppermute | solution.py:389
  167.3 26.6 %collective-permute-start.7 = (bf16[256,1024]{1,0:T(8,128)(2,1)S(1)}, bf16[256,1024]{1,0:T(8,128)(2,1)S(1)}, u32[]{:S(2)}, u32[]{:S(2)}) collective-permute-start(bf16[256,1024]{1,0:T(8,128)(2,1)S(1)} %add_add_fusion.2.refs_0_), channel_id=1, source_target_pairs={{0,2},{2,0},{4,6},{6,4},{8,10},{10,8},{12,14},{14,12},{16,18},{18,... | collective-permute-start | bytes 1572872 | tf_op jit(solution)/shard_map/ppermute | solution.py:389
  172.8 21.1 %collective-permute-start.8 = (bf16[256,1024]{1,0:T(8,128)(2,1)S(1)}, bf16[256,1024]{1,0:T(8,128)(2,1)S(1)}, u32[]{:S(2)}, u32[]{:S(2)}) collective-permute-start(bf16[256,1024]{1,0:T(8,128)(2,1)S(1)} %add_add_fusion.2.refs_0_), channel_id=1, source_target_pairs={{0,4},{2,6},{4,0},{6,2},{8,12},{10,14},{12,8},{14,10},{16,20},{18,... | collective-permute-start | bytes 1572872 | tf_op jit(solution)/shard_map/ppermute | solution.py:389
  173.8 23.5 %all-to-all-start = ((f32[32,1,1024]{2,1,0:T(1,128)}), f32[32,1,1024]{2,1,0:T(1,128)S(1)}, u32[]{:S(2)}, u32[]{:S(2)}) async-start(f32[32,1,1024]{2,1,0:T(1,128)} %broadcast_in_dim.249), calls=%async_computation | async-start | bytes 262144 | tf_op jit(solution)/shard_map/all_to_all | solution.py:437
  190.6 19.4 %collective-permute-start.16 = (bf16[256,1024]{1,0:T(8,128)(2,1)S(1)}, bf16[256,1024]{1,0:T(8,128)(2,1)S(1)}, u32[]{:S(2)}, u32[]{:S(2)}) collective-permute-start(bf16[256,1024]{1,0:T(8,128)(2,1)S(1)} %add_add_fusion.1.refs_5_), channel_id=1, source_target_pairs={{0,2},{2,0},{4,6},{6,4},{8,10},{10,8},{12,14},{14,12},{16,18},{18,... | collective-permute-start | bytes 1572872 | tf_op jit(solution)/shard_map/ppermute | solution.py:389
  199.8 36.1 %all-to-all-start.1 = ((bf16[32,16,512]{2,1,0:T(8,128)(2,1)}), bf16[32,16,512]{2,1,0:T(8,128)(2,1)}, u32[]{:S(2)}, u32[]{:S(2)}) async-start(bf16[32,16,512]{2,1,0:T(8,128)(2,1)} %broadcast_in_dim.253), calls=%async_computation.1 | async-start | bytes 1048576 | tf_op jit(solution)/shard_map/all_to_all | solution.py:437
  290.2 21.4 %collective-permute-start.42 = (f32[128,1024]{1,0:T(8,128)}, f32[128,1024]{1,0:T(8,128)S(1)}, u32[]{:S(2)}, u32[]{:S(2)}) collective-permute-start(f32[128,1024]{1,0:T(8,128)} %slice.475), channel_id=1, source_target_pairs={{0,1},{1,0},{2,3},{3,2},{4,5},{5,4},{6,7},{7,6},{8,9},{9,8},{10,11... | collective-permute-start | bytes 1572872 | tf_op jit(solution)/shard_map/ppermute | solution.py:393
  291.3 29.5 %all-to-all-start.4 = ((bf16[16,8,768]{2,1,0:T(8,128)(2,1)}), bf16[16,8,768]{2,1,0:T(8,128)(2,1)S(1)}, u32[]{:S(2)}, u32[]{:S(2)}) async-start(bf16[16,8,768]{2,1,0:T(8,128)(2,1)} %broadcast_in_dim.264), calls=%async_computation.4 | async-start | bytes 393216 | tf_op jit(solution)/shard_map/all_to_all | solution.py:422
  365.3 80.6 %collective-permute-start.47 = (bf16[512,1536]{1,0:T(8,128)(2,1)}, bf16[512,1536]{1,0:T(8,128)(2,1)}, u32[]{:S(2)}, u32[]{:S(2)}) collective-permute-start(bf16[512,1536]{1,0:T(8,128)(2,1)} %bitcast.73), channel_id=1, source_target_pairs={{0,1},{1,0},{2,3},{3,2},{4,5},{5,4},{6,7},{7,6},{8,9},{9,8},{10,11... | collective-permute-start | bytes 4718600 | tf_op jit(solution)/shard_map/ppermute | solution.py:393
  419.8 26.3 %collective-permute-start.48 = (bf16[512,1024]{1,0:T(8,128)(2,1)S(1)}, bf16[512,1024]{1,0:T(8,128)(2,1)S(1)}, u32[]{:S(2)}, u32[]{:S(2)}) collective-permute-start(bf16[512,1024]{1,0:T(8,128)(2,1)S(1)} %copy-done.22), channel_id=1, source_target_pairs={{0,1},{1,0},{2,3},{3,2},{4,5},{5,4},{6,7},{7,6},{8,9},{9,8},{10,11... | collective-permute-start | bytes 3145736 | tf_op jit(solution)/shard_map/ppermute | solution.py:393
  425.1 20.9 %collective-permute-start.49 = (bf16[128,512]{1,0:T(8,128)(2,1)S(1)}, bf16[128,512]{1,0:T(8,128)(2,1)S(1)}, u32[]{:S(2)}, u32[]{:S(2)}) collective-permute-start(bf16[128,512]{1,0:T(8,128)(2,1)S(1)} %get-tuple-element.118), channel_id=1, source_target_pairs={{0,1},{1,0},{2,3},{3,2},{4,5},{5,4},{6,7},{7,6},{8,9},{9,8},{10,11... | collective-permute-start | bytes 393224 | tf_op jit(solution)/shard_map/ppermute | solution.py:393
  425.4 20.6 %collective-permute-start.50 = (bf16[8,1024]{1,0:T(8,128)(2,1)S(1)}, bf16[8,1024]{1,0:T(8,128)(2,1)S(1)}, u32[]{:S(2)}, u32[]{:S(2)}) collective-permute-start(bf16[8,1024]{1,0:T(8,128)(2,1)S(1)} %convert_element_type.228.do_ref), channel_id=1, source_target_pairs={{0,1},{1,0},{2,3},{3,2},{4,5},{5,4},{6,7},{7,6},{8,9},{9,8},{10,11... | collective-permute-start | bytes 49160 | tf_op jit(solution)/shard_map/ppermute | solution.py:393
  442.6 32.8 %all-to-all-start.8 = ((f32[32,3,1024]{2,1,0:T(4,128)}), f32[32,3,1024]{2,1,0:T(4,128)}, u32[]{:S(2)}, u32[]{:S(2)}) async-start(f32[32,3,1024]{2,1,0:T(4,128)} %broadcast_in_dim.281), calls=%async_computation.8 | async-start | bytes 1048576 | tf_op jit(solution)/shard_map/all_to_all | solution.py:437
  460.3 22.0 %collective-permute-start.51 = (bf16[128,1024]{1,0:T(8,128)(2,1)}, bf16[128,1024]{1,0:T(8,128)(2,1)}, u32[]{:S(2)}, u32[]{:S(2)}) collective-permute-start(bf16[128,1024]{1,0:T(8,128)(2,1)} %get-tuple-element.94), channel_id=1, source_target_pairs={{0,4},{2,6},{4,0},{6,2},{8,12},{10,14},{12,8},{14,10},{16,20},{18,... | collective-permute-start | bytes 786440 | tf_op jit(solution)/shard_map/ppermute | solution.py:389
  461.9 20.4 %collective-permute-start.58 = (bf16[128,1024]{1,0:T(8,128)(2,1)}, bf16[128,1024]{1,0:T(8,128)(2,1)}, u32[]{:S(2)}, u32[]{:S(2)}) collective-permute-start(bf16[128,1024]{1,0:T(8,128)(2,1)} %get-tuple-element.96), channel_id=1, source_target_pairs={{0,4},{2,6},{4,0},{6,2},{8,12},{10,14},{12,8},{14,10},{16,20},{18,... | collective-permute-start | bytes 786440 | tf_op jit(solution)/shard_map/ppermute | solution.py:389
  473.9 20.8 %collective-permute-start.54 = (bf16[256,1024]{1,0:T(8,128)(2,1)}, bf16[256,1024]{1,0:T(8,128)(2,1)}, u32[]{:S(2)}, u32[]{:S(2)}) collective-permute-start(bf16[256,1024]{1,0:T(8,128)(2,1)} %pad_maximum_fusion.8), channel_id=1, source_target_pairs={{0,4},{2,6},{4,0},{6,2},{8,12},{10,14},{12,8},{14,10},{16,20},{18,... | collective-permute-start | bytes 1572872 | tf_op jit(solution)/shard_map/ppermute | solution.py:389
  476.5 58.2 %all-to-all-start.9 = ((bf16[16,8,3840]{2,1,0:T(8,128)(2,1)}), bf16[16,8,3840]{2,1,0:T(8,128)(2,1)}, u32[]{:S(2)}, u32[]{:S(2)}) async-start(bf16[16,8,3840]{2,1,0:T(8,128)(2,1)} %broadcast_in_dim.282), calls=%async_computation.9 | async-start | bytes 1966080 | tf_op jit(solution)/shard_map/all_to_all | solution.py:422
  484.6 22.9 %collective-permute-start.52 = (bf16[256,1024]{1,0:T(8,128)(2,1)S(1)}, bf16[256,1024]{1,0:T(8,128)(2,1)S(1)}, u32[]{:S(2)}, u32[]{:S(2)}) collective-permute-start(bf16[256,1024]{1,0:T(8,128)(2,1)S(1)} %pad_maximum_fusion.7), channel_id=1, source_target_pairs={{0,2},{2,0},{4,6},{6,4},{8,10},{10,8},{12,14},{14,12},{16,18},{18,... | collective-permute-start | bytes 1572872 | tf_op jit(solution)/shard_map/ppermute | solution.py:389
  486.6 22.6 %collective-permute-start.61 = (bf16[256,1024]{1,0:T(8,128)(2,1)S(1)}, bf16[256,1024]{1,0:T(8,128)(2,1)S(1)}, u32[]{:S(2)}, u32[]{:S(2)}) collective-permute-start(bf16[256,1024]{1,0:T(8,128)(2,1)S(1)} %pad_maximum_fusion.10), channel_id=1, source_target_pairs={{0,4},{2,6},{4,0},{6,2},{8,12},{10,14},{12,8},{14,10},{16,20},{18,... | collective-permute-start | bytes 1572872 | tf_op jit(solution)/shard_map/ppermute | solution.py:389
  488.2 29.4 %collective-permute-start.59 = (bf16[256,1024]{1,0:T(8,128)(2,1)S(1)}, bf16[256,1024]{1,0:T(8,128)(2,1)S(1)}, u32[]{:S(2)}, u32[]{:S(2)}) collective-permute-start(bf16[256,1024]{1,0:T(8,128)(2,1)S(1)} %pad_maximum_fusion.9), channel_id=1, source_target_pairs={{0,2},{2,0},{4,6},{6,4},{8,10},{10,8},{12,14},{14,12},{16,18},{18,... | collective-permute-start | bytes 1572872 | tf_op jit(solution)/shard_map/ppermute | solution.py:389
  525.0 57.0 %collective-permute-start.46 = (bf16[512,1024]{1,0:T(8,128)(2,1)}, bf16[512,1024]{1,0:T(8,128)(2,1)}, u32[]{:S(2)}, u32[]{:S(2)}) collective-permute-start(bf16[512,1024]{1,0:T(8,128)(2,1)} %convolution_convert_fusion), channel_id=1, source_target_pairs={{14,22},{16,24},{18,26},{20,28},{15,23},{17,25},{19,27},{21,29}} | collective-permute-start | bytes 3145736 | tf_op jit(solution)/shard_map/ppermute | solution.py:389
  538.0 32.4 %collective-permute-start.64 = (bf16[256,1024]{1,0:T(8,128)(2,1)S(1)}, bf16[256,1024]{1,0:T(8,128)(2,1)S(1)}, u32[]{:S(2)}, u32[]{:S(2)}) collective-permute-start(bf16[256,1024]{1,0:T(8,128)(2,1)S(1)} %fusion.71), channel_id=1, source_target_pairs={{8,0},{10,2},{12,4},{14,10},{9,1},{11,3},{13,5},{15,11}} | collective-permute-start | bytes 1572872 | tf_op jit(solution)/shard_map/ppermute | solution.py:389
  539.6 42.1 %collective-permute-start.57 = (bf16[256,1024]{1,0:T(8,128)(2,1)S(1)}, bf16[256,1024]{1,0:T(8,128)(2,1)S(1)}, u32[]{:S(2)}, u32[]{:S(2)}) collective-permute-start(bf16[256,1024]{1,0:T(8,128)(2,1)S(1)} %fusion.70), channel_id=1, source_target_pairs={{8,0},{10,2},{12,4},{14,10},{9,1},{11,3},{13,5},{15,11}} | collective-permute-start | bytes 1572872 | tf_op jit(solution)/shard_map/ppermute | solution.py:389
  (163 other events, 1808.2 us)

commit v2 on v1

v2 whole, which is shorter than its diff:
```python
import functools
import math

import jax
import jax.numpy as jnp
from jax import lax
from jax.experimental import pallas as pl
from jax.experimental.pallas import tpu as pltpu
from jax.sharding import PartitionSpec as P

WIDTH = 1024
HEADS = 16
HEAD_DIM = 64
FF = 4096
PIX = 3072
PROJ = 768
TOKS = 50
PATCHES = TOKS - 1
ROWS_PER_UNIT = 32
UNIT_COUNT = 504
JITTER = 2

EPS_NORM = 1e-06
SOFTMAX_SCALE = 0.07
LEARN_RATE = 0.03
BETA_ONE = 0.5
BETA_TWO = 0.5
DECAY_RATE = 0.05
ADAM_EPS = 1e-08
MASKED = -1000000000.0
SCALE = HEAD_DIM ** (-0.5)

F32 = jnp.float32
BF = jnp.bfloat16
ROW_BASE = 1 + TOKS
ROW_TAIL = ROW_BASE + 8 + FF // WIDTH
SLOT = 64


def low(values):
    return values.astype(BF)


def dot(a, b, dims=((1,), (0,)), precision=None):
    return lax.dot_general(a, b, (dims, ((), ())), precision=precision, preferred_element_type=F32)


NN = ((1,), (0,))
NT = ((1,), (1,))
TN = ((0,), (0,))


def layer_norm(values, gain, shift):
    center = values - jnp.mean(values, axis=-1, keepdims=True)
    spread = jnp.mean(center * center, axis=-1, keepdims=True)
    return center * lax.rsqrt(spread + EPS_NORM) * gain + shift


def normalize(values):
    return values * lax.rsqrt(jnp.sum(values * values, axis=-1, keepdims=True) + EPS_NORM)


def exact_gelu(values):
    return jax.nn.gelu(values, approximate=False)


def small_parts(small):
    base, tail = ROW_BASE, ROW_TAIL
    return (
        small[0],
        small[1:base],
        small[base],
        small[base + 1],
        small[base + 2],
        small[base + 3],
        small[base + 4],
        small[base + 5],
        small[base + 6],
        small[base + 7],
        small[base + 8 : tail].reshape(FF),
        small[tail],
        small[tail + 1],
        small[tail + 2],
    )


def adamw(weight, grad, first, second, step):
    first_new = BETA_ONE * first + (1.0 - BETA_ONE) * grad
    second_new = BETA_TWO * second + (1.0 - BETA_TWO) * grad * grad
    first_hat = first_new / (1.0 - jnp.power(BETA_ONE, step))
    second_hat = second_new / (1.0 - jnp.power(BETA_TWO, step))
    weight_new = weight - LEARN_RATE * (
        first_hat / (jnp.sqrt(second_hat) + ADAM_EPS) + DECAY_RATE * weight
    )
    return (weight_new, first_new, second_new)


def halo(values, chips, axes):
    before = lax.ppermute(values[-JITTER:], axes, [(i, i + 1) for i in range(chips - 1)])
    behind = lax.ppermute(values[:JITTER], axes, [(i + 1, i) for i in range(chips - 1)])
    return before, behind


def with_halo(values, chips, axes):
    before, behind = halo(values, chips, axes)
    return jnp.concatenate([before, values, behind], axis=0)


def slots_near(slot_unit_index, img, slots):
    padded = jnp.pad(slot_unit_index, (JITTER, JITTER), constant_values=-1)
    return lax.dynamic_slice(padded, (img * slots,), (slots + 2 * JITTER,))


def pick(ext, matches, slots):
    out = jnp.zeros((slots,) + ext.shape[1:], ext.dtype)
    for shift in range(2 * JITTER + 1):
        out = jnp.where(matches[shift][:, None, None], ext[shift : shift + slots], out)
    return out


def to_units(values, near, img, chips, axes="img"):
    slots = values.shape[0]
    ids = img * slots + jnp.arange(slots, dtype=jnp.int32)
    matches = [near[s : s + slots] == ids for s in range(2 * JITTER + 1)]
    return pick(with_halo(values, chips, axes), matches, slots)


def to_slots(values, near, img, chips, axes="img"):
    slots = values.shape[0]
    here = near[JITTER : JITTER + slots]
    ids = img * slots + jnp.arange(slots, dtype=jnp.int32)
    matches = [
        (here == ids + (s - JITTER)) & (here < UNIT_COUNT) for s in range(2 * JITTER + 1)
    ]
    return pick(with_halo(values, chips, axes), matches, slots)


def shuffle_matrix():
    source = lax.broadcasted_iota(jnp.int32, (256, 256), 0)
    target = lax.broadcasted_iota(jnp.int32, (256, 256), 1)
    moved = ((source // 16) % 2) * 128 + (source // 32) * 16 + source % 16
    return (moved == target).astype(F32).astype(BF)


def vmem():
    return pl.BlockSpec(memory_space=pltpu.VMEM)


def smem():
    return pl.BlockSpec(memory_space=pltpu.SMEM)


def shape(dims, dtype):
    return jax.ShapeDtypeStruct(dims, dtype)


def call(kernel, name, scalars, arrays, outs, scratch=(), mib=40, flops=10**9):
    moved = sum(a.size * a.dtype.itemsize for a in list(arrays) + list(outs))
    return pl.pallas_call(
        kernel,
        in_specs=[smem()] * len(scalars) + [vmem()] * len(arrays),
        out_specs=[vmem()] * len(outs),
        out_shape=list(outs),
        scratch_shapes=list(scratch),
        compiler_params=pltpu.CompilerParams(vmem_limit_bytes=mib * 2**20),
        cost_estimate=pl.CostEstimate(flops=flops, bytes_accessed=moved, transcendentals=0),
        name=name,
    )(*scalars, *arrays)


def prep_kernel(pix_ref, shuffle_ref, out_ref):
    shuffle = shuffle_ref[...]
    for block in range(PIX // 256):
        moved = dot(pix_ref[0, :, 256 * block : 256 * block + 256], shuffle).astype(BF)
        out_ref[0, 0, :, 128 * block : 128 * block + 128] = moved[:, :128]
        out_ref[1, 0, :, 128 * block : 128 * block + 128] = moved[:, 128:]


def prep(padded, shuffle):
    images = padded.shape[0]
    return pl.pallas_call(
        prep_kernel,
        grid=(images,),
        in_specs=[
            pl.BlockSpec((1, SLOT, PIX), lambda i: (i, 0, 0)),
            pl.BlockSpec((256, 256), lambda i: (0, 0)),
        ],
        out_specs=pl.BlockSpec((2, 1, SLOT, PIX // 2), lambda i: (0, i, 0, 0)),
        out_shape=jax.ShapeDtypeStruct((2, images, SLOT, PIX // 2), BF),
        compiler_params=pltpu.CompilerParams(vmem_limit_bytes=24 * 2**20),
        cost_estimate=pl.CostEstimate(flops=8 * 10**8, bytes_accessed=6 * 2**20, transcendentals=0),
        name="prep",
    )(padded, shuffle)


def head_mask(rows):
    lane = lax.broadcasted_iota(jnp.int32, (rows, WIDTH), 1) // HEAD_DIM
    row = lax.broadcasted_iota(jnp.int32, (rows, WIDTH), 0) % HEADS
    return lane == row


def norm_parts(values):
    center = values - jnp.mean(values, axis=-1, keepdims=True)
    rstd = lax.rsqrt(jnp.mean(center * center, axis=-1, keepdims=True) + EPS_NORM)
    return center * rstd, rstd


def norm_back(grad, gain, xhat, rstd):
    gy = grad * gain
    return rstd * (
        gy - jnp.mean(gy, axis=-1, keepdims=True) - xhat * jnp.mean(gy * xhat, axis=-1, keepdims=True)
    )


def rowsum(values):
    return jnp.sum(values, axis=0, keepdims=True)


def to_halves(values, shuffle):
    first, second = [], []
    for block in range(values.shape[1] // 256):
        moved = low(dot(values[:, 256 * block : 256 * block + 256], shuffle))
        first.append(moved[:, :128])
        second.append(moved[:, 128:])
    return jnp.concatenate(first, axis=1), jnp.concatenate(second, axis=1)


def to_natural(first, second, shuffle):
    out = []
    for block in range(first.shape[1] // 128):
        lanes = slice(128 * block, 128 * block + 128)
        both = jnp.concatenate([first[:, lanes], second[:, lanes]], axis=1)
        out.append(low(dot(both, shuffle, NT)))
    return jnp.concatenate(out, axis=1)


R_PATCH, R_GAIN1, R_SHIFT1, R_VB, R_OB, R_GAIN2, R_SHIFT2 = 51, 52, 53, 55, 56, 57, 58
R_C2, R_GAINF, R_SHIFTF, R_SMALL = 63, 64, 65, 66
LATE = 128


def forward_kernel(segments, images, where_ref, pix_ref, *refs):
    count = len(segments)
    own, peer = refs[:count], refs[count : 2 * count]
    rows_ref, qk_ref, valid_ref, shuffle_ref = refs[2 * count : 2 * count + 4]
    hid_ref, xhat_ref, rstd_ref, p_ref, pooled_ref, mass_ref, wv_ref, o_ref = refs[
        2 * count + 4 : 2 * count + 12
    ]
    acc_ref, pool_ref = refs[2 * count + 12 :]
    col, core = where_ref[0], where_ref[1]
    patch = rows_ref[2 : 1 + TOKS] + rows_ref[R_PATCH : R_PATCH + 1]
    class_state = rows_ref[0:1] + rows_ref[1:2]
    for i in range(images):
        acc_ref[SLOT * i : SLOT * i + PATCHES] = patch
        acc_ref[SLOT * i + PATCHES : SLOT * i + TOKS] = class_state
        acc_ref[SLOT * i + TOKS : SLOT * (i + 1)] = jnp.zeros((SLOT - TOKS, WIDTH), F32)
    for flip, group in ((0, own), (1, peer)):
        half = core ^ flip
        for (source, parts), ref in zip(segments, group):
            block = col ^ source

            @pl.when(block < 3)
            def _():
                for row, lane, rows in parts:
                    lanes = pl.ds(pl.multiple_of(block * 512 + lane, 128), rows)
                    acc_ref[...] += dot(pix_ref[half, :, lanes], ref[row : row + rows])

            @pl.when(block == 3)
            def _():
                for row, lane, rows in parts:
                    wv_ref[half, lane : lane + rows] = ref[row : row + rows]

    gain, shift, value_bias = (rows_ref[r : r + 1] for r in (R_GAIN1, R_SHIFT1, R_VB))
    valid = valid_ref[...] > 0
    qk = qk_ref[...]
    for i in range(images):
        part = slice(SLOT * i, SLOT * (i + 1))
        xhat, rstd = norm_parts(acc_ref[part])
        hid = low(xhat * gain + shift)
        xhat_ref[part] = xhat
        rstd_ref[part] = jnp.broadcast_to(rstd, (SLOT, 128))
        hid_ref[part] = hid
        scores = jnp.where(valid[part], dot(hid, qk, NT), MASKED)
        e = jnp.exp(scores - jnp.max(scores, axis=0, keepdims=True))
        p = e / jnp.sum(e, axis=0, keepdims=True)
        p_ref[part] = p
        pb = low(p)
        pool_ref[HEADS * i : HEADS * (i + 1)] = low(dot(pb, hid, TN))
        mass_ref[HEADS * i : HEADS * (i + 1)] = dot(pb, jnp.ones((SLOT, 128), BF), TN)
    shuffle = shuffle_ref[...]
    pooled_ref[0], pooled_ref[1] = to_halves(pool_ref[...], shuffle)
    rows = images * HEADS
    mixed = dot(pooled_ref[0], wv_ref[0]) + dot(pooled_ref[1], wv_ref[1])
    mixed = mixed + mass_ref[:, 0:1] * value_bias
    mixed = jnp.where(head_mask(rows), mixed, 0.0)
    joined = low(jnp.sum(mixed.reshape(images, HEADS, WIDTH), axis=1))
    first, second = to_halves(joined, shuffle)
    o_ref[:, : WIDTH // 2] = first
    o_ref[:, WIDTH // 2 :] = second


def forward_call(segments, images, where, pix, own, peer, rows, qk, valid, shuffle):
    tokens = images * SLOT
    outs = [
        shape((tokens, WIDTH), BF),
        shape((tokens, WIDTH), F32),
        shape((tokens, 128), F32),
        shape((tokens, HEADS), F32),
        shape((2, images * HEADS, WIDTH // 2), BF),
        shape((images * HEADS, 128), F32),
        shape((2, WIDTH // 2, WIDTH), BF),
        shape((images, WIDTH), BF),
    ]
    return call(
        functools.partial(forward_kernel, segments, images), "forward", [where],
        [pix, *own, *peer, rows, qk, valid, shuffle], outs,
        [pltpu.VMEM((tokens, WIDTH), F32), pltpu.VMEM((images * HEADS, WIDTH), BF)], mib=50,
    )


def late_lanes(where_ref, flip, source, rows=LATE):
    at = ((where_ref[1] ^ flip) * 4 + (where_ref[0] ^ source)) * rows
    return pl.ds(pl.multiple_of(at, 128), rows)


def resid_kernel(where_ref, att_ref, rows_ref, *refs):
    late, (resid_ref, low_ref) = refs[:8], refs[8:]
    resid = rows_ref[0:1] + rows_ref[1:2] + rows_ref[R_OB : R_OB + 1]
    for number, piece in enumerate(late):
        lanes = late_lanes(where_ref, number // 4, number % 4)
        resid = resid + dot(att_ref[:, lanes], piece[:LATE])
    resid_ref[...] = resid
    xhat, _ = norm_parts(resid)
    hidden = low(xhat * rows_ref[R_GAIN2 : R_GAIN2 + 1] + rows_ref[R_SHIFT2 : R_SHIFT2 + 1])
    low_ref[...] = jnp.broadcast_to(hidden[None], low_ref.shape)


def fetch(pick_ref, slot, candidates, out_ref, sem):
    for number, candidate in enumerate(candidates):

        @pl.when(pick_ref[slot] == number)
        def _():
            pltpu.make_async_copy(candidate, out_ref, sem).start()


def arrived(candidate, out_ref, sem):
    pltpu.make_async_copy(candidate, out_ref, sem).wait()


def ff_kernel(pick_ref, hid_ref, bias_ref, *refs):
    candidates, (pre_ref, act_ref, part_ref, w1_ref, w2_ref, sems) = refs[:6], refs[6:]
    fetch(pick_ref, 0, candidates, w1_ref, sems.at[0])
    fetch(pick_ref, 1, candidates, w2_ref, sems.at[1])
    hidden = hid_ref[...].reshape(-1, WIDTH)
    arrived(candidates[0], w1_ref, sems.at[0])
    pre = dot(hidden, w1_ref[...], NT) + bias_ref[...]
    pre_ref[...] = pre
    active = low(0.5 * pre * (1.0 + lax.erf(pre * (0.5**0.5))))
    act_ref[...] = active
    arrived(candidates[0], w2_ref, sems.at[1])
    part_ref[...] = low(dot(active, w2_ref[...])).reshape(part_ref.shape)


def ff_back_kernel(pick_ref, dst_ref, pre_ref, *refs):
    candidates, (dpre_ref, sum_ref, part_ref, w1_ref, w2_ref, sems) = refs[:6], refs[6:]
    fetch(pick_ref, 1, candidates, w2_ref, sems.at[1])
    fetch(pick_ref, 0, candidates, w1_ref, sems.at[0])
    d_state = dst_ref[...].reshape(-1, WIDTH)
    pre = pre_ref[...]
    slope = 0.5 * (1.0 + lax.erf(pre * (0.5**0.5))) + pre * jnp.exp(-0.5 * pre * pre) * (
        1.0 / (2.0 * math.pi) ** 0.5
    )
    arrived(candidates[0], w2_ref, sems.at[1])
    d_pre = low(dot(d_state, w2_ref[...], NT) * slope)
    dpre_ref[...] = d_pre
    sum_ref[...] = rowsum(d_pre.astype(F32))
    arrived(candidates[0], w1_ref, sems.at[0])
    part_ref[...] = low(dot(d_pre, w1_ref[...])).reshape(part_ref.shape)


def ff_call(kernel, name, pick, arrays, candidates, outs):
    moved = sum(a.size * a.dtype.itemsize for a in list(arrays) + list(outs))
    return pl.pallas_call(
        kernel,
        in_specs=[smem()]
        + [vmem()] * len(arrays)
        + [pl.BlockSpec(memory_space=pl.ANY)] * len(candidates),
        out_specs=[vmem()] * len(outs),
        out_shape=list(outs),
        scratch_shapes=[
            pltpu.VMEM((512, WIDTH), BF),
            pltpu.VMEM((512, WIDTH), BF),
            pltpu.SemaphoreType.DMA((2,)),
        ],
        compiler_params=pltpu.CompilerParams(vmem_limit_bytes=24 * 2**20),
        cost_estimate=pl.CostEstimate(
            flops=2 * 10**8, bytes_accessed=moved + 2 * 2**20, transcendentals=0
        ),
        name=name,
    )(pick, *arrays, *candidates)


def head_kernel(
    where_ref, part_ref, resid_ref, partners_ref, target_ref, rows_ref, *refs
):
    late, (state_ref, low_ref, final_ref, dz_ref, vec_ref, z_ref) = refs[:8], refs[8:]
    images = resid_ref.shape[0]
    state = resid_ref[...] + jnp.sum(part_ref[...].astype(F32), axis=0) + rows_ref[R_C2 : R_C2 + 1]
    gain = rows_ref[R_GAINF : R_GAINF + 1]
    xhat, rstd = norm_parts(state)
    final = low(xhat * gain + rows_ref[R_SHIFTF : R_SHIFTF + 1])
    final_ref[...] = final
    for number, piece in enumerate(late):
        z_ref[:, late_lanes(where_ref, number // 4, number % 4)] = dot(final, piece[LATE:], NT)
    z = z_ref[...]
    inv = lax.rsqrt(jnp.sum(z * z, axis=-1, keepdims=True) + EPS_NORM)
    partners = partners_ref[...]
    logits = dot(low(z * inv), partners, NT) / SOFTMAX_SCALE
    total = logits.shape[1]
    hit = lax.broadcasted_iota(jnp.int32, (images, total), 1) == target_ref[...]
    top = jnp.max(logits, axis=-1, keepdims=True)
    e = jnp.exp(logits - top)
    mass = jnp.sum(e, axis=-1, keepdims=True)
    aim = jnp.sum(jnp.where(hit, logits, 0.0), axis=-1, keepdims=True)
    losses = jnp.log(mass) + top - aim
    d_logits = (e / mass - jnp.where(hit, 1.0, 0.0)) / total
    d_unit = dot(low(d_logits / SOFTMAX_SCALE), partners)
    along = jnp.sum(d_unit * z, axis=-1, keepdims=True)
    dz_ref[...] = low(d_unit * inv - z * (along * inv * inv * inv))
    d_final = jnp.zeros((images, WIDTH), F32)
    for number, piece in enumerate(late):
        lanes = late_lanes(where_ref, number // 4, number % 4)
        d_final = d_final + dot(dz_ref[:, lanes], piece[LATE:])
    d_state = norm_back(d_final, gain, xhat, rstd)
    state_ref[...] = d_state
    low_ref[...] = jnp.broadcast_to(low(d_state)[None], low_ref.shape)
    vec_ref[...] = jnp.zeros_like(vec_ref)
    vec_ref[0:1] = rowsum(d_state)
    vec_ref[1:2] = rowsum(d_final * xhat)
    vec_ref[2:3] = rowsum(d_final)
    vec_ref[3:4] = jnp.broadcast_to(rowsum(losses) / total, (1, WIDTH))


def backward_kernel(
    images, where_ref, part_ref, dstate_ref, resid_ref, wv_ref, hid_ref, xhat_ref,
    rstd_ref, p_ref, mass_ref, qk_ref, rows_ref, shuffle_ref, *refs,
):
    late = refs[:8]
    de_ref, do_ref, dres_ref, pos_ref, vec_ref, pull_ref, dom_ref, da_ref, att_ref = refs[8:]
    rows = images * HEADS
    gain, value_bias = rows_ref[R_GAIN1 : R_GAIN1 + 1], rows_ref[R_VB : R_VB + 1]
    shuffle = shuffle_ref[...]
    vec_ref[...] = jnp.zeros_like(vec_ref)
    d_two = jnp.sum(part_ref[...].astype(F32), axis=0)
    xhat2, rstd2 = norm_parts(resid_ref[...])
    d_resid = dstate_ref[...] + norm_back(d_two, rows_ref[R_GAIN2 : R_GAIN2 + 1], xhat2, rstd2)
    vec_ref[3:4] = rowsum(d_resid)
    vec_ref[4:5] = rowsum(d_two * xhat2)
    vec_ref[5:6] = rowsum(d_two)
    d_low = low(d_resid)
    dres_ref[...] = d_low
    for number, piece in enumerate(late):
        att_ref[:, late_lanes(where_ref, number // 4, number % 4)] = dot(d_low, piece[:LATE], NT)
    half = WIDTH // 2
    d_att = to_natural(low(att_ref[:, :half]), low(att_ref[:, half:]), shuffle)
    do_ref[...] = d_att
    spread = jnp.broadcast_to(d_att.reshape(images, 1, WIDTH).astype(F32), (images, HEADS, WIDTH))
    wide = jnp.where(head_mask(rows), spread.reshape(rows, WIDTH), 0.0)
    dom_ref[...] = low(wide)
    vec_ref[2:3] = rowsum(wide * mass_ref[:, 0:1])
    da_ref[...] = to_natural(
        low(dot(dom_ref[...], wv_ref[0], NT)), low(dot(dom_ref[...], wv_ref[1], NT)), shuffle
    )
    qk = qk_ref[...]
    bias_rows = low(jnp.broadcast_to(value_bias, (8, WIDTH)))
    real = lax.broadcasted_iota(jnp.int32, (SLOT, WIDTH), 0) < PATCHES
    for i in range(images):
        part = slice(SLOT * i, SLOT * (i + 1))
        mine = slice(HEADS * i, HEADS * (i + 1))
        hid, p, da = hid_ref[part], p_ref[part], da_ref[mine]
        dp = dot(hid, da, NT) + dot(bias_rows, dom_ref[mine], NT)[0:1]
        ds = low(p * (dp - rowsum(p * dp)))
        dh = dot(low(p), da) + dot(ds, qk)
        pull = dot(ds, hid, TN)
        xhat, rstd = xhat_ref[part], rstd_ref[part, 0:1]
        dx = norm_back(dh, gain, xhat, rstd)
        de_ref[part] = low(jnp.where(real, dx, 0.0))
        vec_ref[0:1] += rowsum(dh * xhat)
        vec_ref[1:2] += rowsum(dh)
        if i == 0:
            pos_ref[...] = dx
            pull_ref[...] = pull
        else:
            pos_ref[...] += dx
            pull_ref[...] += pull


def backward_call(images, where, arrays):
    tokens = images * SLOT
    outs = [
        shape((tokens, WIDTH), BF),
        shape((images, WIDTH), BF),
        shape((images, WIDTH), BF),
        shape((SLOT, WIDTH), F32),
        shape((8, WIDTH), F32),
        shape((HEADS, WIDTH), F32),
    ]
    scratch = [pltpu.VMEM((images * HEADS, WIDTH), BF)] * 2 + [pltpu.VMEM((images, WIDTH), F32)]
    return call(
        functools.partial(backward_kernel, images), "backward", [where], arrays, outs, scratch
    )


def embed_grad_kernel(
    images, plan, where_ref, pix_ref, pixp_ref, de_ref, dep_ref, pooled_ref, pooledp_ref,
    do_ref, dop_ref, *out_refs,
):
    col = where_ref[0]
    heads = images * HEADS
    for (source, first, rows), out_ref in zip(plan, out_refs):
        block = col ^ source

        @pl.when(block < 3)
        def _():
            lanes = pl.ds(pl.multiple_of(block * 512 + first, 128), rows)
            total = dot(pix_ref[:, lanes], de_ref[...], TN) + dot(pixp_ref[:, lanes], dep_ref[...], TN)
            out_ref[...] = total.astype(out_ref.dtype)

        @pl.when(block == 3)
        def _():
            total = None
            for pooled, do in ((pooled_ref, do_ref), (pooledp_ref, dop_ref)):
                spread = jnp.broadcast_to(
                    do[...].reshape(images, 1, WIDTH).astype(F32), (images, HEADS, WIDTH)
                )
                wide = low(jnp.where(head_mask(heads), spread.reshape(heads, WIDTH), 0.0))
                term = dot(pooled[:, first : first + rows], wide, TN)
                total = term if total is None else total + term
            out_ref[...] = total.astype(out_ref.dtype)


def embed_grad_call(images, name, plan, where, arrays):
    outs = [shape((rows, WIDTH), F32 if source == 0 else BF) for source, _, rows in plan]
    return call(
        functools.partial(embed_grad_kernel, images, plan), name, [where], arrays, outs
    )


def to_natural_exact(first, second, shuffle):
    wide = shuffle.astype(F32)
    out = []
    for block in range(first.shape[1] // 128):
        lanes = slice(128 * block, 128 * block + 128)
        both = jnp.concatenate([first[:, lanes], second[:, lanes]], axis=1)
        out.append(dot(both, wide, NT, precision=lax.Precision.HIGHEST))
    return jnp.concatenate(out, axis=1)


def collect_kernel(where_ref, pos_ref, vec_ref, head_ref, sum_ref, pull_ref, shuffle_ref, out_ref):
    col, core = where_ref[0], where_ref[1]
    out_ref[...] = jnp.zeros_like(out_ref)
    top = pos_ref[PATCHES:TOKS] + vec_ref[3:4]
    out_ref[0:1] = top
    out_ref[1:2] = top
    patches = pos_ref[0:PATCHES]
    out_ref[2 : 1 + TOKS] = patches
    out_ref[R_PATCH : R_PATCH + 1] = rowsum(patches)
    out_ref[R_GAIN1 : R_SHIFT1 + 1] = vec_ref[0:2]
    out_ref[R_VB : R_VB + 1] = vec_ref[2:3]
    out_ref[R_OB : R_SHIFT2 + 1] = vec_ref[3:6]
    sums = jnp.broadcast_to(sum_ref[...], (8, WIDTH // 2))
    nothing = jnp.zeros_like(sums)
    row = to_natural_exact(
        jnp.where(core == 0, sums, nothing), jnp.where(core == 0, nothing, sums), shuffle_ref[...]
    )
    for block in range(4):
        mine = (col + 1) % 4 == block
        out_ref[R_SHIFT2 + 1 + block : R_SHIFT2 + 2 + block] = jnp.where(mine, row[0:1], 0.0)
    out_ref[R_C2 : R_SHIFTF + 1] = head_ref[0:3]
    out_ref[R_SMALL : R_SMALL + HEADS] = pull_ref[...]
    out_ref[R_SMALL + HEADS : R_SMALL + HEADS + 1] = head_ref[3:4]


def complete_kernel(total_ref, path_ref, rows_ref, shuffle_ref, out_ref, square_ref):
    out_ref[...] = total_ref[0:R_SMALL]
    half = WIDTH // 2
    first = jnp.broadcast_to(path_ref[1:2, :half], (8, half))
    second = jnp.broadcast_to(path_ref[3:4, :half], (8, half))
    d_hidden = to_natural_exact(first, second, shuffle_ref[...])[0:1]
    xhat, rstd = norm_parts(rows_ref[0:1] + rows_ref[1:2])
    d_class = norm_back(d_hidden, rows_ref[R_GAIN1 : R_GAIN1 + 1], xhat, rstd)
    out_ref[0:1] += d_class
    out_ref[1:2] += d_class
    out_ref[R_GAIN1 : R_GAIN1 + 1] += d_hidden * xhat
    out_ref[R_SHIFT1 : R_SHIFT1 + 1] += d_hidden
    out_ref[R_SHIFT1 + 1 : R_SHIFT1 + 2] = path_ref[0:1]
    grads = out_ref[...]
    square_ref[...] = jnp.broadcast_to(
        jnp.sum(jnp.sum(grads * grads, axis=0, keepdims=True), axis=1, keepdims=True), (8, 128)
    )


def owner_kernel(role_ref, extra_ref, pull_ref, heads_ref, class_ref, dq_ref, *refs):
    ff, out_ref = refs[:6], refs[6]
    chip, core = role_ref[0], role_ref[1]
    half = WIDTH // 2

    @pl.when((chip >= 7) & (chip <= 14))
    def _():
        is_two = chip >= 11
        total = None
        for piece in ff:
            left = jnp.where(is_two, piece[:, :half], piece[:, half:WIDTH])
            right = jnp.where(is_two, piece[:, 2 * WIDTH :], piece[:, WIDTH : 2 * WIDTH])
            term = dot(left, right, TN)
            total = term if total is None else total + term
        out_ref[...] = total

    @pl.when(chip == 6)
    def _():
        lanes = pl.ds(pl.multiple_of(core * half, 128), half)
        out_ref[...] = dot(extra_ref[:, lanes], extra_ref[:, WIDTH : 2 * WIDTH], TN)

    @pl.when(chip == 15)
    def _():
        lanes = pl.ds(pl.multiple_of(2 * WIDTH + core * half, 128), half)
        wide = dot(extra_ref[:, lanes], extra_ref[:, 3 * WIDTH :], TN)
        for quarter in range(4):
            out_ref[96 * quarter : 96 * quarter + 96] = wide[128 * quarter : 128 * quarter + 96]
        out_ref[384:] = jnp.zeros((128, WIDTH), F32)

    @pl.when(chip == 4)
    def _():
        out_ref[...] = dot(
            pull_ref[...], heads_ref[...].astype(F32), TN, precision=lax.Precision.HIGHEST
        )

    @pl.when(chip == 3)
    def _():
        outer = dot(
            class_ref[...].astype(F32), jnp.concatenate([dq_ref[0:1], jnp.zeros((7, WIDTH), F32)]),
            TN, precision=lax.Precision.HIGHEST,
        )
        out_ref[...] = outer


def finish_kernel(role_ref, formed_ref, *refs):
    parts, (out_ref, square_ref) = refs[:-2], refs[-2:]
    chip = role_ref[0]
    rows = parts[0].shape[0]

    @pl.when(chip < 3)
    def _():
        for number in range(len(parts) // 2):
            out_ref[rows * number : rows * (number + 1)] = (
                parts[2 * number][...] + parts[2 * number + 1][...].astype(F32)
            )

    @pl.when(chip == 5)
    def _():
        for number in range(len(parts) // 2):
            out_ref[rows * number : rows * (number + 1)] = parts[2 * number + 1][...].astype(F32)

    @pl.when((chip >= 3) & (chip != 5))
    def _():
        out_ref[...] = formed_ref[...]

    grads = out_ref[...]
    square_ref[...] = jnp.broadcast_to(
        jnp.sum(jnp.sum(grads * grads, axis=0, keepdims=True), axis=1, keepdims=True), (8, 128)
    )


def update_kernel(
    source_ref, scalar_ref, before_ref, grad_ref, behind_ref, w_ref, m_ref, v_ref,
    nw_ref, nm_ref, nv_ref,
):
    step = pl.program_id(0)
    slots = grad_ref.shape[0]
    factor, fix_one, fix_two = scalar_ref[0], scalar_ref[1], scalar_ref[2]
    for k in range(w_ref.shape[0]):
        at = source_ref[step * w_ref.shape[0] + k]
        inside = (at >= 0) & (at < slots)
        grad = jnp.where(
            inside,
            grad_ref[jnp.clip(at, 0, slots - 1)],
            jnp.where(
                at < 0,
                before_ref[jnp.clip(at + JITTER, 0, JITTER - 1)],
                behind_ref[jnp.clip(at - slots, 0, JITTER - 1)],
            ),
        )
        grad = grad * jnp.where(at >= -JITTER, factor, 0.0)
        weight = w_ref[k]
        first = BETA_ONE * m_ref[k] + (1.0 - BETA_ONE) * grad
        second = BETA_TWO * v_ref[k] + (1.0 - BETA_TWO) * grad * grad
        nm_ref[k] = first
        nv_ref[k] = second
        nw_ref[k] = weight - LEARN_RATE * (
            (first * fix_one) / (jnp.sqrt(second * fix_two) + ADAM_EPS) + DECAY_RATE * weight
        )


def update_call(source, scalars, before, grads, behind, masters, first, second):
    slots, part, width = masters.shape
    block = 4
    spec = pl.BlockSpec((block, part, width), lambda i: (i, 0, 0))
    return pl.pallas_call(
        update_kernel,
        grid=(slots // block,),
        in_specs=[smem(), smem(), vmem(), vmem(), vmem(), spec, spec, spec],
        out_specs=[spec] * 3,
        out_shape=[shape(masters.shape, F32)] * 3,
        compiler_params=pltpu.CompilerParams(vmem_limit_bytes=24 * 2**20),
        cost_estimate=pl.CostEstimate(
            flops=2 * 10**7, bytes_accessed=7 * masters.size * 4, transcendentals=0
        ),
        name="update",
    )(source, scalars, before, grads, behind, masters, first, second)


CHIPS = 16
CHIP = ("z", "y", "x")
ALL = ("z", "y", "x", "c")
PLANE = ("y", "x", "c")
FLIP_X = [(i, i ^ 1) for i in range(CHIPS)]
FLIP_Y = [(i, i ^ 2) for i in range(CHIPS)]
FLIP_CORE = [(0, 1), (1, 0)]


def hop(values, pairs):
    return lax.ppermute(values, CHIP, pairs)


def swap(values):
    return lax.ppermute(values, "c", FLIP_CORE)


def after(values, *others):
    return lax.optimization_barrier((values,) + others)[0]


def among(img, chips):
    hit = img == chips[0]
    for chip in chips[1:]:
        hit = hit | (img == chip)
    return hit


def choose(img, cases, otherwise):
    out = otherwise
    for chips, values in cases:
        out = jnp.where(among(img, chips), values, out)
    return out


def together(*values):
    return lax.optimization_barrier(values)


def plane_gather(block, diagonal_by_x):
    by_x, by_y = hop(block, FLIP_X), hop(block, FLIP_Y)
    diagonal = hop(by_y, FLIP_X) if diagonal_by_x else hop(by_x, FLIP_Y)
    return [block, by_x, by_y, diagonal]


def in_plane(values):
    return lax.all_to_all(values, PLANE, 0, 0, tiled=True)


def from_all(values):
    sent = jnp.broadcast_to(values[None], (2 * CHIPS,) + values.shape)
    return lax.all_to_all(sent, ALL, 0, 0, tiled=True)


def natural(values):
    lead = values.shape[:-2]
    units = values.shape[-1] // 16
    split = values.reshape(lead + (2, units, 16))
    return jnp.swapaxes(split, -3, -2).reshape(lead + (units * 32,))


def halves(values):
    lead = values.shape[:-1]
    units = values.shape[-1] // 32
    return jnp.swapaxes(values.reshape(lead + (units, 2, 16)), -3, -2).reshape(
        lead + (2, units * 16)
    )


def per_device_16(
    pixels, keep_mask, partner_index, partner_emb, masters, first_moment_slots,
    second_moment_slots, slot_unit_index, small_params, small_first, small_second, step_count,
):
    img, core = lax.axis_index(CHIP), lax.axis_index("c")
    col, plane = img % 4, img // 4
    images = pixels.shape[0]
    slots = masters.shape[0]
    is_one = core == 1
    where = jnp.stack([col, core]).astype(jnp.int32)
    shuffle = shuffle_matrix()
    rows = small_params
    class_state = small_params[0] + small_params[1]

    def mine_of(pair):
        return jnp.where(is_one, pair[1], pair[0])

    def theirs_of(pair):
        return jnp.where(is_one, pair[0], pair[1])

    near = slots_near(slot_unit_index, img, slots)
    held = low(masters)
    ids = img * slots + jnp.arange(slots, dtype=jnp.int32)
    matches = [near[s : s + slots] == ids for s in range(2 * JITTER + 1)]
    middle = pick(held[6:26], [m[8:24] for m in matches], 16)
    before, behind = halo(after(held, middle), CHIPS, CHIP)
    lower = pick(jnp.concatenate([before, held[:10]]), [m[:8] for m in matches], 8)
    upper = pick(jnp.concatenate([held[22:], behind]), [m[24:] for m in matches], 8)
    outer = jnp.concatenate([lower, upper]).reshape(256, WIDTH)
    middle = middle.reshape(256, WIDTH)
    own_w = jnp.concatenate([outer[:128], middle, outer[128:]])

    class_hidden = low(layer_norm(class_state, small_params[R_GAIN1], small_params[R_SHIFT1]))
    class_half = mine_of(halves(class_hidden))
    by_quarter = halves(partner_emb).reshape(images, 2, 4, PROJ // 8)
    by_quarter = jnp.pad(by_quarter, ((0, 0), (0, 0), (0, 0), (0, LATE - PROJ // 8)))
    partners = from_all(by_quarter.reshape(images, WIDTH)).reshape(-1, WIDTH)

    one_a = hop(middle, [(0, 4), (1, 5), (2, 6), (5, 7)])
    query_parts = from_all(dot(class_half[None], own_w))
    filler = jnp.zeros((LATE - PROJ // 8, WIDTH), BF)

    def late_quarter(number):
        proj = jnp.concatenate([own_w[96 * number : 96 * number + 96], filler])
        return jnp.where(img == 15, proj, own_w[LATE * number : LATE * (number + 1)])

    quarters = [late_quarter(number) for number in range(4)]
    late = jnp.where(img == 6, quarters[2], quarters[3])
    for flip in (1, 2, 3):
        mine = jnp.where(img == 6, quarters[2 ^ flip], quarters[3 ^ flip])
        got = hop(mine, [(6, 6 ^ flip), (15, 15 ^ flip)])
        late = jnp.where(among(img, (6 ^ flip, 15 ^ flip)), got, late)
    down_one = hop(
        own_w, [(12, 8), (13, 9), (14, 10), (11, 7), (8, 4), (9, 5), (10, 6), (7, 3)]
    )
    one_a, outer, query_parts, late, partners = together(
        one_a, outer, query_parts, late, partners
    )
    one_b = hop(outer, [(0, 4), (1, 5), (2, 6), (5, 7)])
    two_a = hop(one_a, [(4, 8), (5, 9), (6, 10), (7, 11)])
    query = low((query_parts[6, 0] + query_parts[7, 0] + small_params[R_SHIFT1 + 1]) * SCALE)
    query_heads = jnp.where(head_mask(HEADS), query[None], jnp.zeros((), BF))
    pulled = from_all(low(dot(query_heads, own_w, NT)))
    late_one = hop(late, [(4, 0), (5, 1), (6, 2), (7, 3), (12, 8), (13, 9), (14, 10), (15, 11)])
    one_b, two_a, pulled, late_one, down_one = together(one_b, two_a, pulled, late_one, down_one)
    two_b = hop(one_b, [(4, 8), (5, 9), (6, 10), (7, 11)])
    three_a = hop(
        jnp.where(img == 7, one_a, two_a), [(8, 12), (9, 13), (10, 14), (11, 15), (7, 3)]
    )
    late_two = hop(
        jnp.where(plane == 1, late, late_one),
        [(4, 8), (5, 9), (6, 10), (7, 11), (8, 4), (9, 5), (10, 6), (11, 7)],
    )
    down_two = hop(down_one, [(8, 4), (9, 5), (10, 6), (7, 3), (4, 0), (5, 1), (6, 2)])
    two_b, three_a, late_two = together(two_b, three_a, late_two)
    block_a = jnp.where(img < 3, middle, one_a + two_a + three_a)
    x_a, y_a = hop(block_a, FLIP_X), hop(block_a, FLIP_Y)
    three_b = hop(
        jnp.where(img == 7, one_b, two_b), [(8, 12), (9, 13), (10, 14), (11, 15), (7, 3)]
    )
    late_three = hop(
        late_two, [(8, 12), (9, 13), (10, 14), (11, 15), (4, 0), (5, 1), (6, 2), (7, 3)]
    )
    x_a, y_a, three_b, late_three, down_two = together(x_a, y_a, three_b, late_three, down_two)
    block_b = jnp.where(img < 3, outer, one_b + two_b + three_b)
    x_b, y_b = hop(block_b, FLIP_X), hop(block_b, FLIP_Y)
    d_a = hop(y_a, FLIP_X)
    down_three = hop(down_two, [(4, 0), (5, 1), (6, 2)])
    up_one = hop(own_w, [(8, 12), (9, 13), (10, 14), (7, 11), (11, 15)])
    x_b, y_b, d_a, late_three = together(x_b, y_b, d_a, late_three)
    d_b = hop(x_b, FLIP_Y)
    wo_part = choose(plane, [((0,), late_one), ((1,), late), ((2,), late_two)], late_three)
    proj_part = choose(plane, [((3,), late), ((2,), late_one), ((1,), late_two)], late_three)
    late_own = jnp.concatenate([wo_part, proj_part])
    late_x, late_y = hop(late_own, FLIP_X), hop(late_own, FLIP_Y)
    up_two = hop(up_one, [(11, 15)])

    segments, own_pieces, peer_pieces = [], [], []
    for pieces, spans in (
        ((block_a, x_a, y_a, d_a), ((0, 128, 256),)),
        ((block_b, x_b, y_b, d_b), ((0, 0, 128), (128, 384, 128))),
    ):
        segments += [(source, spans) for source in range(4)]
        own_pieces += pieces
        peer_pieces += [swap(piece) for piece in pieces]
    late_d = jnp.concatenate([hop(late_y[:LATE], FLIP_X), hop(late_x[LATE:], FLIP_Y)])
    late_pieces = [late_own, late_x, late_y, late_d]
    late_pieces += [swap(piece) for piece in late_pieces]
    qk = natural(jnp.stack([pulled[8], pulled[9]], axis=1))

    padded = jnp.pad(pixels, ((0, 0), (0, SLOT - PATCHES), (0, 0)))
    pix = prep(padded, shuffle).reshape(2, images * SLOT, PIX // 2)
    pix_own = mine_of(pix)
    pix_peer = swap(theirs_of(pix))
    valid = jnp.concatenate(
        [
            keep_mask,
            jnp.ones((images, 1), jnp.int32),
            jnp.zeros((images, SLOT - TOKS), jnp.int32),
        ],
        axis=1,
    ).reshape(images * SLOT, 1)
    hid, xhat, rstd, p, pooled, mass, wv, attended = forward_call(
        segments, images, where, pix, own_pieces, peer_pieces, rows, qk, valid, shuffle
    )

    pooled_own = mine_of(pooled)
    pooled_peer = swap(theirs_of(pooled))

    resid, hidden_sent = call(
        resid_kernel, "resid", [where], [attended, rows, *late_pieces],
        [shape((images, WIDTH), F32), shape((8, images, WIDTH), BF)],
    )
    hidden_all = in_plane(hidden_sent)
    ff_block = (col + 1) % 4
    bias_part = lax.dynamic_slice(
        small_params[R_SHIFT2 + 1 : R_C2].reshape(4, 32, 2, 16),
        (ff_block, 0, core, 0),
        (1, 32, 1, 16),
    ).reshape(1, 512)
    candidates = [own_w, up_one, up_two, down_one, down_two, down_three]
    pick_one = choose(
        img, [((15,), 2), ((12, 13, 14, 11), 1), ((4, 5, 6, 3), 3), ((0, 1, 2), 4)], 0
    )
    pick_two = choose(
        img, [((15,), 1), ((8, 9, 10, 7), 3), ((4, 5, 6, 3), 4), ((0, 1, 2), 5)], 0
    )
    picks = jnp.stack([pick_one, pick_two]).astype(jnp.int32)
    preact, active, part = ff_call(
        ff_kernel, "ff", picks, [hidden_all, bias_part], candidates,
        [shape((8 * images, 512), F32), shape((8 * images, 512), BF), shape((8, images, WIDTH), BF)],
    )
    part = in_plane(part)
    d_state, d_state_sent, final, d_projected, head_vec = call(
        head_kernel, "head", [where],
        [part, resid, partners, partner_index[:, None], rows, *late_pieces],
        [
            shape((images, WIDTH), F32), shape((8, images, WIDTH), BF), shape((images, WIDTH), BF),
            shape((images, WIDTH), BF), shape((8, WIDTH), F32),
        ],
        [pltpu.VMEM((images, WIDTH), F32)],
    )
    d_state_all = in_plane(d_state_sent)
    d_preact, d_preact_sum, part = ff_call(
        ff_back_kernel, "ff_back", picks, [d_state_all, preact], candidates,
        [shape((8 * images, 512), BF), shape((1, 512), F32), shape((8, images, WIDTH), BF)],
    )
    part = in_plane(part)

    d_embed, d_attended, d_resid, d_pos, d_vec, pull = backward_call(
        images, where,
        [part, d_state, resid, wv, hid, xhat, rstd, p, mass, qk, rows, shuffle, *late_pieces],
    )
    arrays = [
        pix_own, pix_peer, d_embed, swap(d_embed), pooled_own, pooled_peer, d_attended,
        swap(d_attended),
    ]
    quads = [(3, 128 * number, 128) for number in range(4)]
    grad_d = embed_grad_call(images, "embed_grad_far", quads, where, arrays)
    pairs = [(source, first, 256) for source in (1, 2, 0) for first in (0, 256)]
    grads = embed_grad_call(images, "embed_grad_near", pairs, after(where, grad_d[0]), arrays)
    grad_x, grad_y, grad_own = grads[0:2], grads[2:4], grads[4:6]
    sums = []
    gate = None
    for number in range(2):
        for_y, for_x = grad_d[2 * number], grad_d[2 * number + 1]
        if number:
            for_y, for_x = after(for_y, gate), after(for_x, gate)
        got_y, got_x = hop(for_y, FLIP_X), hop(for_x, FLIP_Y)
        part_x, part_y = grad_x[number], grad_y[number]
        part_y = jnp.concatenate([low(part_y[:128].astype(F32) + got_y.astype(F32)), part_y[128:]])
        part_x = jnp.concatenate([part_x[:128], low(part_x[128:].astype(F32) + got_x.astype(F32))])
        gate = got_x
        got_x, got_y = hop(part_x, FLIP_X), hop(part_y, FLIP_Y)
        sums.append(grad_own[number] + got_x.astype(F32) + got_y.astype(F32))
    reduced = []
    for acc in sums:
        got = hop(low(acc), [(12, 8), (13, 9), (14, 10), (15, 11), (3, 7)])
        acc = acc + got.astype(F32)
        got = hop(low(acc), [(8, 4), (9, 5), (10, 6), (11, 7)])
        acc = acc + got.astype(F32)
        reduced += [acc, hop(low(acc), [(4, 0), (5, 1), (6, 2), (7, 5)])]

    d_pos, d_vec, head_vec, d_preact_sum, pull, active, attended, _ = together(
        d_pos, d_vec, head_vec, d_preact_sum, pull, active, attended, grad_own[0]
    )
    (small_local,) = call(
        collect_kernel, "collect", [where], [d_pos, d_vec, head_vec, d_preact_sum, pull, shuffle],
        [shape((96, WIDTH), F32)],
    )
    shares = lax.all_to_all(small_local.reshape(32, 3, WIDTH), ALL, 0, 0, tiled=True)
    small_total = from_all(jnp.sum(shares, axis=0)).reshape(96, WIDTH)
    pull_total, loss = small_total[R_SMALL : R_SMALL + HEADS], small_total[R_SMALL + HEADS, 0]
    pull_half = halves(pull_total)
    pull_half = mine_of((pull_half[:, 0], pull_half[:, 1]))
    d_query = jnp.where(head_mask(HEADS), dot(low(pull_half), own_w), 0.0)
    d_query = jnp.sum(d_query, axis=0, keepdims=True) * SCALE
    d_query = hop(d_query + swap(d_query), [(4, 3)])
    toward = dot(low(d_query), own_w, NT)
    path = jnp.concatenate([d_query, jnp.pad(toward, ((0, 0), (0, WIDTH // 2)))])
    path = from_all(path)
    small_grad, small_square = call(
        complete_kernel, "complete", [], [small_total, path[6:8].reshape(4, WIDTH), rows, shuffle],
        [shape((R_SMALL, WIDTH), F32), shape((8, 128), F32)],
    )

    ff_rows = jnp.concatenate(
        [
            active,
            d_preact,
            hidden_all.reshape(-1, WIDTH),
            d_state_all.reshape(-1, WIDTH),
        ],
        axis=1,
    )
    rise = [(i, i + 4) for i in range(12)]
    up_one = hop(ff_rows, rise)
    up_two = hop(up_one, rise[4:])
    up_three = hop(up_two, rise[8:])
    down_one = hop(ff_rows, [(12, 8), (13, 9), (14, 10), (15, 11), (11, 7)])
    down_two = hop(down_one, [(11, 7)])
    every = [ff_rows, up_one, up_two, up_three, down_one, down_two]
    extra = jnp.concatenate([attended, d_resid, d_projected, final], axis=1)
    extra = after(extra, small_total)
    sent = jnp.broadcast_to(extra[None], (CHIPS,) + extra.shape)
    extra = lax.all_to_all(sent, CHIP, 0, 0, tiled=True).reshape(CHIPS * images, -1)
    extra = jnp.concatenate([extra, swap(extra)], axis=0)
    class_rows = jnp.concatenate([class_half[None], jnp.zeros((7, WIDTH // 2), BF)])
    role = jnp.stack([img, core]).astype(jnp.int32)
    (formed,) = call(
        owner_kernel, "owner", [role],
        [extra, pull_half, query_heads, class_rows, d_query, *every],
        [shape((512, WIDTH), F32)],
    )
    own_grad, square = call(
        finish_kernel, "finish", [role], [formed, *reduced],
        [shape((512, WIDTH), F32), shape((8, 128), F32)],
    )
    owner_total = jnp.sum(from_all(square[0:1])[:, 0, 0])
    grad_norm = jnp.sqrt(owner_total + small_square[0, 0])
    factor = 1.0 / jnp.maximum(grad_norm, 1.0)
    own_grad = own_grad.reshape(slots, 16, WIDTH)
    before, behind = halo(own_grad, CHIPS, CHIP)
    here = near[JITTER : JITTER + slots]
    source = jnp.where(here < UNIT_COUNT, here - img * slots, -100)
    step_value = step_count.astype(F32)
    scalars = jnp.stack(
        [
            factor,
            1.0 / (1.0 - jnp.power(BETA_ONE, step_value)),
            1.0 / (1.0 - jnp.power(BETA_TWO, step_value)),
        ]
    )
    new_masters, new_first, new_second = update_call(
        source, scalars, before, own_grad, behind, masters, first_moment_slots,
        second_moment_slots,
    )
    new_small, new_small_first, new_small_second = adamw(
        small_params, small_grad * factor, small_first, small_second, step_value
    )
    return (
        new_masters, new_first, new_second, new_small, new_small_first, new_small_second,
        loss, grad_norm,
    )


def per_device_any(
    pixels, keep_mask, partner_index, partner_emb, masters, first_moment_slots,
    second_moment_slots, slot_unit_index, small_params, small_first, small_second, step_count,
):
    chips, seq = lax.axis_size("img"), lax.axis_size("seq")
    img = lax.axis_index("img")
    images = pixels.shape[0]
    slots, part = masters.shape[0], masters.shape[1]
    near = slots_near(slot_unit_index, img, slots)
    own_w = to_units(low(masters), near, img, chips)
    gathered = lax.all_gather(own_w, ("img", "seq"), axis=0, tiled=False)
    flat = gathered.reshape(chips, seq, slots, part, WIDTH).transpose(0, 2, 1, 3, 4)
    flat = flat.reshape(chips * slots * ROWS_PER_UNIT, WIDTH)
    bounds = [0, PIX, WIDTH, WIDTH, WIDTH, WIDTH, FF, FF, PROJ]
    parts, offset = [], 0
    for size in bounds[1:]:
        parts.append(flat[offset : offset + size])
        offset += size
    embed_w, query_w, key_w, value_w, output_w, fc_in_w, fc_out_w, proj_w = parts
    (
        class_row, pos_rows, patch_bias, gain_one, shift_one, query_bias, value_bias, out_bias,
        gain_two, shift_two, fc_in_bias, fc_out_bias, gain_end, shift_end,
    ) = small_parts(small_params)
    class_state = class_row + pos_rows[0]
    embedded = jnp.einsum("itp,pd->itd", pixels, embed_w, preferred_element_type=F32)
    tokens = jnp.concatenate(
        [
            jnp.broadcast_to(class_state, (images, 1, WIDTH)),
            embedded + patch_bias + pos_rows[1:],
        ],
        axis=1,
    )
    hidden = low(layer_norm(tokens, gain_one, shift_one))
    class_hidden = hidden[0, 0]
    mask16 = head_mask(HEADS)
    query = low((dot(class_hidden[None], query_w)[0] + query_bias) * SCALE)
    query_heads = jnp.where(mask16, query[None], jnp.zeros((), BF))
    qk = low(dot(query_heads, key_w, NT))
    scores = jnp.einsum("hd,itd->iht", qk, hidden, preferred_element_type=F32)
    keep = jnp.concatenate([jnp.ones((images, 1), jnp.int32), keep_mask], axis=1)
    scores = jnp.where(keep[:, None, :] > 0, scores, MASKED)
    weights = jax.nn.softmax(scores, axis=-1)
    weights_low = low(weights)
    pooled = low(jnp.einsum("iht,itd->ihd", weights_low, hidden, preferred_element_type=F32))
    mass = jnp.sum(weights_low.astype(F32), axis=-1)
    mixed = dot(pooled.reshape(-1, WIDTH), value_w).reshape(images, HEADS, WIDTH)
    mixed = mixed + mass[:, :, None] * value_bias
    attended = low(jnp.sum(jnp.where(mask16, mixed, 0.0), axis=1))
    resid = class_state + dot(attended, output_w) + out_bias
    hidden_two = low(layer_norm(resid, gain_two, shift_two))
    preact = dot(hidden_two, fc_in_w, NT) + fc_in_bias
    active = low(exact_gelu(preact))
    state = resid + dot(active, fc_out_w) + fc_out_bias
    final = low(layer_norm(state, gain_end, shift_end))
    projected = dot(final, proj_w, NT)
    unit = low(normalize(projected))
    partners = lax.all_gather(partner_emb, ("img", "seq"), axis=0, tiled=True)
    count = partners.shape[0]
    logits = dot(unit, partners, NT) / SOFTMAX_SCALE
    onehot = (jnp.arange(count, dtype=jnp.int32)[None] == partner_index[:, None]).astype(F32)
    total = jax.nn.logsumexp(logits, axis=-1)
    loss_part = jnp.sum(total - jnp.sum(logits * onehot, axis=-1)) / count
    d_logits = (jax.nn.softmax(logits, axis=-1) - onehot) / count
    d_unit = dot(low(d_logits / SOFTMAX_SCALE), partners)
    d_projected = low(jax.vjp(normalize, projected)[1](d_unit)[0])
    d_final = dot(d_projected, proj_w)
    d_state, d_gain_end, d_shift_end = jax.vjp(layer_norm, state, gain_end, shift_end)[1](d_final)
    d_state_low = low(d_state)
    d_active = dot(d_state_low, fc_out_w, NT)
    d_preact = low(jax.vjp(exact_gelu, preact)[1](d_active)[0])
    d_hidden_two = dot(d_preact, fc_in_w)
    d_norm, d_gain_two, d_shift_two = jax.vjp(layer_norm, resid, gain_two, shift_two)[1](
        d_hidden_two
    )
    d_resid = d_state + d_norm
    d_resid_low = low(d_resid)
    d_attended = low(dot(d_resid_low, output_w, NT))
    wide = jnp.where(mask16, d_attended[:, None, :], jnp.zeros((), BF))
    d_pooled = low(dot(wide.reshape(-1, WIDTH), value_w, NT)).reshape(images, HEADS, WIDTH)
    d_weights = jnp.einsum("ihd,itd->iht", d_pooled, hidden, preferred_element_type=F32)
    d_weights = d_weights + jnp.sum(wide.astype(F32) * value_bias, axis=-1)[:, :, None]
    d_scores = low(weights * (d_weights - jnp.sum(weights * d_weights, axis=-1, keepdims=True)))
    d_hidden = jnp.einsum("iht,ihd->itd", weights_low, d_pooled, preferred_element_type=F32)
    d_hidden = d_hidden + jnp.einsum("iht,hd->itd", d_scores, qk, preferred_element_type=F32)
    pull = jnp.einsum("iht,itd->hd", d_scores, hidden, preferred_element_type=F32)
    d_query = jnp.sum(jnp.where(mask16, dot(low(pull), key_w), 0.0), axis=0) * SCALE
    d_class_hidden = dot(low(d_query)[None], query_w, NT)
    d_tokens, d_gain_one, d_shift_one = jax.vjp(layer_norm, tokens, gain_one, shift_one)[1](
        d_hidden
    )
    d_class, d_gain_cls, d_shift_cls = jax.vjp(layer_norm, class_state[None], gain_one, shift_one)[
        1
    ](d_class_hidden)
    d_class = d_class[0] + jnp.sum(d_tokens[:, 0], axis=0) + jnp.sum(d_resid, axis=0)
    d_patch = d_tokens[:, 1:]
    d_embed_w = jnp.einsum("itp,itd->pd", pixels, low(d_patch), preferred_element_type=F32)
    d_value_w = dot(pooled.reshape(-1, WIDTH), wide.reshape(-1, WIDTH), TN)
    d_key_w = dot(pull, query_heads.astype(F32), TN, precision=lax.Precision.HIGHEST)
    small_local = jnp.concatenate(
        [
            d_class[None],
            d_class[None],
            jnp.sum(d_patch, axis=0),
            jnp.sum(d_patch, axis=(0, 1))[None],
            (d_gain_one + d_gain_cls)[None],
            (d_shift_one + d_shift_cls)[None],
            d_query[None],
            jnp.sum(wide.astype(F32) * mass[:, :, None], axis=(0, 1))[None],
            jnp.sum(d_resid, axis=0)[None],
            d_gain_two[None],
            d_shift_two[None],
            jnp.sum(d_preact.astype(F32), axis=0).reshape(FF // WIDTH, WIDTH),
            jnp.sum(d_state, axis=0)[None],
            d_gain_end[None],
            d_shift_end[None],
        ],
        axis=0,
    )
    grad_table = jnp.concatenate(
        [
            d_embed_w,
            class_hidden.astype(F32)[:, None] * d_query[None, :],
            d_key_w,
            d_value_w,
            dot(attended, d_resid_low, TN),
            dot(d_preact, hidden_two, TN),
            dot(active, d_state_low, TN),
            dot(d_projected, final, TN),
            jnp.zeros(((chips * slots - UNIT_COUNT) * ROWS_PER_UNIT, WIDTH), F32),
        ],
        axis=0,
    ).reshape(chips * slots, ROWS_PER_UNIT, WIDTH)
    small_grad, loss = lax.psum((small_local, loss_part), ("img", "seq"))
    core_half = lax.psum_scatter(low(grad_table), "seq", scatter_dimension=1, tiled=True)
    own_grad = lax.psum_scatter(core_half.astype(F32), "img", scatter_dimension=0, tiled=True)
    owner_total = lax.psum(jnp.sum(own_grad * own_grad), ("img", "seq"))
    grad_norm = jnp.sqrt(owner_total + jnp.sum(small_grad * small_grad))
    factor = 1.0 / jnp.maximum(grad_norm, 1.0)
    slot_grad = to_slots(own_grad, near, img, chips)
    step_value = step_count.astype(F32)
    new_masters, new_first, new_second = adamw(
        masters, slot_grad * factor, first_moment_slots, second_moment_slots, step_value
    )
    new_small, new_small_first, new_small_second = adamw(
        small_params, small_grad * factor, small_first, small_second, step_value
    )
    return (
        new_masters, new_first, new_second, new_small, new_small_first, new_small_second,
        loss, grad_norm,
    )


def solution(mesh):
    chip, devices = "img", ("img", "seq")
    core, body = "seq", per_device_any
    if mesh.shape["img"] == CHIPS and mesh.shape["seq"] == 2:
        mesh = jax.sharding.Mesh(mesh.devices.reshape(4, 2, 2, 2), ALL)
        chip, devices, core, body = CHIP, ALL, "c", per_device_16
    weights = P(chip, core, None)
    return jax.shard_map(
        body,
        mesh=mesh,
        in_specs=(
            P(devices, None, None),
            P(devices, None),
            P(devices),
            P(devices, None),
            weights,
            weights,
            weights,
            P(),
            P(),
            P(),
            P(),
            P(),
        ),
        out_specs=(weights, weights, weights, P(), P(), P(), P(), P()),
        check_vma=False,
    )
```

time: 627 us -> 525 us (0.84)
  waiting for transfers between devices: 212 us -> 115 us
  matrix products: 36.4 us -> 1.95 us
  Pallas kernels: 28.7 us -> 62.2 us
  other arithmetic: 69.9 us -> 55.3 us
    ppermute x68 -> x69, waiting for transfers between devices: 165 us -> 90.8 us  [the longest x47 88.7 us: hop(): return lax.ppermute(values, CHIP, pairs)]
    dot_general x23 -> x4, matrix products: 36.4 us -> 1.95 us  [dot(): lax.dot_general(a, b, (dims, ((), ())), precision=precision, preferred_el...]
    pallas_call x3 -> x13, Pallas kernels: 25.4 us -> 58.8 us  [the longest x10 48 us: call(): pl.pallas_call(kernel, in_specs=[smem()] * len(scalars) + [vmem()] * len(...]
    ppermute x68 -> x69, starting transfers between devices: 107 us -> 137 us  [the longest x47 121 us: hop(): return lax.ppermute(values, CHIP, pairs)]
    all_to_all x10, starting transfers between devices: 72.7 us -> 48.9 us  [the longest x6 28.9 us: from_all(): return lax.all_to_all(sent, ALL, 0, 0, tiled=True)]
    all_to_all x10, waiting for transfers between devices: 46.7 us -> 24.3 us  [the longest x6 15.6 us: from_all(): return lax.all_to_all(sent, ALL, 0, 0, tiled=True)]
    unnamed x238 -> x262, local copies, waits for them, and re-layouts: 24.1 us -> 37.6 us
    sub x2 -> x1, other arithmetic: 13.6 us -> 2.03 us  [adamw(): weight - LEARN_RATE * (first_hat / (jnp.sqrt(second_hat) + ADAM_EPS) + DE...]
  transfers between devices with their start and end apart: 78 -> 79, of which waited for: 31 -> 21; matrix products, arithmetic and copies ran while one was open for 18% -> 17% of each run, Pallas kernels for 5% -> 8%
where the time goes in v2:
time: 525 us; the launch traced here: 515 us
  starting transfers between devices  186 us (35%)
  waiting for transfers between devices  115 us (22%)
  local copies, waits for them, and re-layouts  71.6 us (14%)
  Pallas kernels  62.2 us (12%)
  other arithmetic  55.3 us (11%)
  blocking collectives  16 us (3%)
  between operations  7.53 us (1%)
    ppermute x47, starting transfers between devices, hop(): return lax.ppermute(values, CHIP, pairs)  121 us
    ppermute x47, waiting for transfers between devices, hop(): return lax.ppermute(values, CHIP, pairs)  88.7 us
    pallas_call x10, Pallas kernels, call(): pl.pallas_call(kernel, in_specs=[smem()] * len(scalars) + [vmem()] * len(...  48 us
    unnamed x262, local copies, waits for them, and re-layouts  37.6 us
    all_to_all x6, starting transfers between devices, from_all(): return lax.all_to_all(sent, ALL, 0, 0, tiled=True)  28.9 us
    convert_element_type x13, other arithmetic, low(): return values.astype(BF)  19.8 us
    all_to_all x2, blocking collectives, in_plane(): return lax.all_to_all(values, PLANE, 0, 0, tiled=True)  16 us
    all_to_all x6, waiting for transfers between devices, from_all(): return lax.all_to_all(sent, ALL, 0, 0, tiled=True)  15.6 us
  transfers between devices with their start and end apart: 79, of which 21 were waited for; matrix products, arithmetic and copies ran while one was open for 17% of the time, Pallas kernels for 8%

profile of v2, /device:TPU:0, one launch (start us, length us, event | category | flops | bytes accessed | tf_op | source)
XLA Modules:
  0.0 515.4 jit_solution(11047517004564725265)
XLA Ops:
  3.2 5.8 %collective-permute-start = (bf16[256,1024]{1,0:T(8,128)(2,1)S(1)}, bf16[256,1024]{1,0:T(8,128)(2,1)}, u32[]{:S(2)}, u32[]{:S(2)}) collective-permute-start(bf16[256,1024]{1,0:T(8,128)(2,1)S(1)} %bitcast.86), channel_id=1, source_target_pairs={{0,8},{2,10},{4,12},{10,14},{1,9},{3,11},{5,13},{11,15}} | collective-permute-start | bytes 1572872 | tf_op jit(solution)/shard_map/ppermute | solution.py:732
  10.4 4.5 collective-permute-start.1
  26.5 6.8 %all-to-all-done = f32[32,1,1024]{2,1,0:T(1,128)S(1)} async-done(((f32[32,1,1024]{2,1,0:T(1,128)}), f32[32,1,1024]{2,1,0:T(1,128)S(1)}, u32[]{:S(2)}, u32[]{:S(2)}) %all-to-all-start) | async-done | bytes 131104 | tf_op jit(solution)/shard_map/all_to_all | solution.py:773
  43.7 9.3 %collective-permute-start.9 = (bf16[512,1024]{1,0:T(8,128)(2,1)S(1)}, bf16[512,1024]{1,0:T(8,128)(2,1)S(1)}, u32[]{:S(2)}, u32[]{:S(2)}) collective-permute-start(bf16[512,1024]{1,0:T(8,128)(2,1)S(1)} %pad_maximum_fusion.1.refs_0_), channel_id=1, source_target_pairs={{24,16},{26,18},{28,20},{22,14},{16,8},{18,10},{20,12},{14,6},{25,... | collective-permute-start | bytes 3145736 | tf_op jit(solution)/shard_map/ppermute | solution.py:732
  59.2 7.1 %all-to-all-start.2 = ((bf16[32,16,512]{2,1,0:T(8,128)(2,1)}), bf16[32,16,512]{2,1,0:T(8,128)(2,1)}, u32[]{:S(2)}, u32[]{:S(2)}) async-start(bf16[32,16,512]{2,1,0:T(8,128)(2,1)} %broadcast_in_dim.203), calls=%async_computation.2 | async-start | bytes 1048576 | tf_op jit(solution)/shard_map/all_to_all | solution.py:773
  66.3 4.4 collective-permute-start.6
  73.5 10.7 %collective-permute-done.8 = bf16[128,1024]{1,0:T(8,128)(2,1)S(1)} collective-permute-done((bf16[128,1024]{1,0:T(8,128)(2,1)S(1)}, bf16[128,1024]{1,0:T(8,128)(2,1)S(1)}, u32[]{:S(2)}, u32[]{:S(2)}) %collective-permute-start.8) | collective-permute-done | bytes 262176 | tf_op jit(solution)/shard_map/ppermute | solution.py:732
  86.7 5.1 all-to-all-done.2
  102.1 16.0 %collective-permute-start.14 = (bf16[256,1024]{1,0:T(8,128)(2,1)S(1)}, bf16[256,1024]{1,0:T(8,128)(2,1)}, u32[]{:S(2)}, u32[]{:S(2)}) collective-permute-start(bf16[256,1024]{1,0:T(8,128)(2,1)S(1)} %add_select_fusion.1.refs_0_), channel_id=1, source_target_pairs={{0,4},{2,6},{4,0},{6,2},{8,12},{10,14},{12,8},{14,10},{16,20},{18,... | collective-permute-start | bytes 1572872 | tf_op jit(solution)/shard_map/ppermute | solution.py:732
  121.1 13.2 %collective-permute-done.16 = bf16[128,1024]{1,0:T(8,128)(2,1)S(1)} collective-permute-done((bf16[128,1024]{1,0:T(8,128)(2,1)}, bf16[128,1024]{1,0:T(8,128)(2,1)S(1)}, u32[]{:S(2)}, u32[]{:S(2)}) %collective-permute-start.16) | collective-permute-done | bytes 262176 | tf_op jit(solution)/shard_map/ppermute | solution.py:732
  137.9 18.3 %collective-permute-start.19 = (bf16[256,1024]{1,0:T(8,128)(2,1)S(1)}, bf16[256,1024]{1,0:T(8,128)(2,1)}, u32[]{:S(2)}, u32[]{:S(2)}) collective-permute-start(bf16[256,1024]{1,0:T(8,128)(2,1)S(1)} %add_select_fusion.refs_4_), channel_id=1, source_target_pairs={{0,4},{2,6},{4,0},{6,2},{8,12},{10,14},{12,8},{14,10},{16,20},{18,... | collective-permute-start | bytes 1572872 | tf_op jit(solution)/shard_map/ppermute | solution.py:732
  158.5 8.4 %collective-permute-done.19.refs_6_ = bf16[256,1024]{1,0:T(8,128)(2,1)} collective-permute-done((bf16[256,1024]{1,0:T(8,128)(2,1)S(1)}, bf16[256,1024]{1,0:T(8,128)(2,1)}, u32[]{:S(2)}, u32[]{:S(2)}) %collective-permute-start.19) | collective-permute-done | bytes 524320 | tf_op jit(solution)/shard_map/ppermute | solution.py:732
  170.4 11.2 %collective-permute-start.31 = (bf16[256,1024]{1,0:T(8,128)(2,1)S(1)}, bf16[256,1024]{1,0:T(8,128)(2,1)}, u32[]{:S(2)}, u32[]{:S(2)}) collective-permute-start(bf16[256,1024]{1,0:T(8,128)(2,1)S(1)} %pad_maximum_fusion.3.refs_0_), channel_id=1, source_target_pairs={{0,4},{2,6},{4,0},{6,2},{8,12},{10,14},{12,8},{14,10},{16,20},{18,... | collective-permute-start | bytes 1572872 | tf_op jit(solution)/shard_map/ppermute | solution.py:732
  182.5 12.1 %collective-permute-done.31.refs_2_ = bf16[256,1024]{1,0:T(8,128)(2,1)} collective-permute-done((bf16[256,1024]{1,0:T(8,128)(2,1)S(1)}, bf16[256,1024]{1,0:T(8,128)(2,1)}, u32[]{:S(2)}, u32[]{:S(2)}) %collective-permute-start.31) | collective-permute-done | bytes 524320 | tf_op jit(solution)/shard_map/ppermute | solution.py:732
  234.7 16.4 %forward.1 = (bf16[512,1024]{1,0:T(8,128)(2,1)}, f32[512,1024]{1,0:T(8,128)}, f32[512,128]{1,0:T(8,128)S(1)}, f32[512,16]{1,0:T(8,128)S(1)}, bf16[2,128,512]{2,1...) custom-call(s32[2]{0:T(128)S(1)} %pad_add_fusion.1.where_ref, ...), custom_call_target="tpu_custom_call" | custom-call | flops 1000000000 | bytes 17852416 | tf_op jit(solution)/shard_map/forward/pallas_call | solution.py:159
  254.5 4.4 all-to-all-start.3
  259.4 5.2 %all-to-all-done.3.hid_ref = bf16[8,8,1024]{2,1,0:T(8,128)(2,1)} async-done(((bf16[8,8,1024]{2,1,0:T(8,128)(2,1)}), bf16[8,8,1024]{2,1,0:T(8,128)(2,1)}, u32[]{:S(2)}, u32[]{:S(2)}) %all-to-all-start.3) | async-done | bytes 131104 | tf_op jit(solution)/shard_map/all_to_all | solution.py:768
  284.5 4.7 head.1
  289.2 8.1 %all_to_all.60.dst_ref = bf16[8,8,1024]{2,1,0:T(8,128)(2,1)S(1)} all-to-all(bf16[8,8,1024]{2,1,0:T(8,128)(2,1)S(1)} %get-tuple-element.113), channel_id=1, replica_groups=mesh['z'=4,'y'=2,'x'=2,'c'=2] {'y','x','c'}, dimensions={0} | all-to-all | bytes 262144 | tf_op jit(solution)/shard_map/all_to_all | solution.py:768
  300.3 7.9 %all_to_all.61.part_ref = bf16[8,8,1024]{2,1,0:T(8,128)(2,1)S(1)} all-to-all(bf16[8,8,1024]{2,1,0:T(8,128)(2,1)S(1)} %get-tuple-element.115), channel_id=1, replica_groups=mesh['z'=4,'y'=2,'x'=2,'c'=2] {'y','x','c'}, dimensions={0} | all-to-all | bytes 262144 | tf_op jit(solution)/shard_map/all_to_all | solution.py:768
  308.4 7.5 %backward.1 = (bf16[512,1024]{1,0:T(8,128)(2,1)}, bf16[8,1024]{1,0:T(8,128)(2,1)S(1)}, bf16[8,1024]{1,0:T(8,128)(2,1)S(1)}, f32[64,1024]{1,0:T(8,128)S(1)}, f32[...) custom-call(s32[2]{0:T(128)S(1)} %pad_add_fusion.1.where_ref, bf16[8,8,1024]{2,1,0:T(8,128)(2,1)S(1)} %all_to_all.61.part_ref, ...), custom_call_target="tpu_custom_call" | custom-call | flops 1000000000 | bytes 11870208 | tf_op jit(solution)/shard_map/backward/pallas_call | solution.py:159
  325.1 6.7 %embed_grad_near.1 = (bf16[256,1024]{1,0:T(8,128)(2,1)S(1)}, bf16[256,1024]{1,0:T(8,128)(2,1)S(1)}, bf16[256,1024]{1,0:T(8,128)(2,1)S(1)}, bf16[256,1024]{1,0:T(...) custom-call(s32[2]{0:T(128)S(1)} %pad_add_fusion.1.where_ref, bf16[512,1536]{1,0:T(8,128)(2,1)S(1)} %bitcast.82, ...), custom_call_target="tpu_custom_call" | custom-call | flops 1000000000 | bytes 9732096 | tf_op jit(solution)/shard_map/embed_grad_near/pallas_call | solution.py:159
  338.0 5.6 %collective-permute-start.48 = (bf16[64,3072]{1,0:T(8,128)(2,1)}, bf16[64,3072]{1,0:T(8,128)(2,1)}, u32[]{:S(2)}, u32[]{:S(2)}) collective-permute-start(bf16[64,3072]{1,0:T(8,128)(2,1)} %pad_maximum_fusion.8.refs_0_), channel_id=1, source_target_pairs={{0,8},{2,10},{4,12},{6,14},{8,16},{10,18},{12,20},{14,22},{16,24},... | collective-permute-start | bytes 1179656 | tf_op jit(solution)/shard_map/ppermute | solution.py:732
  351.3 5.8 %all-to-all-start.7 = ((f32[32,3,1024]{2,1,0:T(4,128)}), f32[32,3,1024]{2,1,0:T(4,128)}, u32[]{:S(2)}, u32[]{:S(2)}) async-start(f32[32,3,1024]{2,1,0:T(4,128)} %reshape.220), calls=%async_computation.7 | async-start | bytes 1048576 | tf_op jit(solution)/shard_map/all_to_all | solution.py:1001
  363.8 7.2 %collective-permute-done.53 = bf16[128,1024]{1,0:T(8,128)(2,1)} collective-permute-done((bf16[128,1024]{1,0:T(8,128)(2,1)}, bf16[128,1024]{1,0:T(8,128)(2,1)}, u32[]{:S(2)}, u32[]{:S(2)}) %collective-permute-start.53) | collective-permute-done | bytes 262176 | tf_op jit(solution)/shard_map/ppermute | solution.py:732
  374.6 4.2 all-to-all-start.8
  389.1 5.4 %collective-permute-done.60 = bf16[128,1024]{1,0:T(8,128)(2,1)S(1)} collective-permute-done((bf16[128,1024]{1,0:T(8,128)(2,1)S(1)}, bf16[128,1024]{1,0:T(8,128)(2,1)S(1)}, u32[]{:S(2)}, u32[]{:S(2)}) %collective-permute-start.60) | collective-permute-done | bytes 262176 | tf_op jit(solution)/shard_map/ppermute | solution.py:732
  397.9 5.8 %all-to-all-start.9 = ((bf16[16,8,4096]{2,1,0:T(8,128)(2,1)}), bf16[16,8,4096]{2,1,0:T(8,128)(2,1)}, u32[]{:S(2)}, u32[]{:S(2)}) async-start(bf16[16,8,4096]{2,1,0:T(8,128)(2,1)} %broadcast_in_dim.207), calls=%async_computation.9 | async-start | bytes 2097152 | tf_op jit(solution)/shard_map/all_to_all | solution.py:1036
  417.2 11.1 %collective-permute-done.61 = bf16[256,1024]{1,0:T(8,128)(2,1)} collective-permute-done((bf16[256,1024]{1,0:T(8,128)(2,1)}, bf16[256,1024]{1,0:T(8,128)(2,1)}, u32[]{:S(2)}, u32[]{:S(2)}) %collective-permute-start.61) | collective-permute-done | bytes 524320 | tf_op jit(solution)/shard_map/ppermute | solution.py:732
  437.8 8.5 %all-to-all-start.11 = ((f32[32,2,1024]{2,1,0:T(2,128)}), f32[32,2,1024]{2,1,0:T(2,128)}, u32[]{:S(2)}, u32[]{:S(2)}) async-start(f32[32,2,1024]{2,1,0:T(2,128)} %broadcast_in_dim.211), calls=%async_computation.11 | async-start | bytes 524288 | tf_op jit(solution)/shard_map/all_to_all | solution.py:773
  475.3 9.8 %collective-permute-done.66.refs_3_ = bf16[256,1024]{1,0:T(8,128)(2,1)S(1)} collective-permute-done((bf16[256,1024]{1,0:T(8,128)(2,1)S(1)}, bf16[256,1024]{1,0:T(8,128)(2,1)S(1)}, u32[]{:S(2)}, u32[]{:S(2)}) %collective-permute-start.66) | collective-permute-done | bytes 524320 | tf_op jit(solution)/shard_map/ppermute | solution.py:732
  508.9 5.0 update.1
  (539 shorter events, 245.7 us)
Async XLA Ops:
  3.2 53.9 %collective-permute-start = (bf16[256,1024]{1,0:T(8,128)(2,1)S(1)}, bf16[256,1024]{1,0:T(8,128)(2,1)}, u32[]{:S(2)}, u32[]{:S(2)}) collective-permute-start(bf16[256,1024]{1,0:T(8,128)(2,1)S(1)} %bitcast.86), channel_id=1, source_target_pairs={{0,8},{2,10},{4,12},{10,14},{1,9},{3,11},{5,13},{11,15}} | collective-permute-start | bytes 1572872 | tf_op jit(solution)/shard_map/ppermute | solution.py:732
  34.2 22.9 %all-to-all-start.1 = ((bf16[32,8,1024]{2,1,0:T(8,128)(2,1)}), bf16[32,8,1024]{2,1,0:T(8,128)(2,1)S(1)}, u32[]{:S(2)}, u32[]{:S(2)}) async-start(bf16[32,8,1024]{2,1,0:T(8,128)(2,1)} %broadcast_in_dim.199), calls=%async_computation.1 | async-start | bytes 1048576 | tf_op jit(solution)/shard_map/all_to_all | solution.py:773
  43.7 29.8 %collective-permute-start.9 = (bf16[512,1024]{1,0:T(8,128)(2,1)S(1)}, bf16[512,1024]{1,0:T(8,128)(2,1)S(1)}, u32[]{:S(2)}, u32[]{:S(2)}) collective-permute-start(bf16[512,1024]{1,0:T(8,128)(2,1)S(1)} %pad_maximum_fusion.1.refs_0_), channel_id=1, source_target_pairs={{24,16},{26,18},{28,20},{22,14},{16,8},{18,10},{20,12},{14,6},{25,... | collective-permute-start | bytes 3145736 | tf_op jit(solution)/shard_map/ppermute | solution.py:732
  59.2 32.5 %all-to-all-start.2 = ((bf16[32,16,512]{2,1,0:T(8,128)(2,1)}), bf16[32,16,512]{2,1,0:T(8,128)(2,1)}, u32[]{:S(2)}, u32[]{:S(2)}) async-start(bf16[32,16,512]{2,1,0:T(8,128)(2,1)} %broadcast_in_dim.203), calls=%async_computation.2 | async-start | bytes 1048576 | tf_op jit(solution)/shard_map/all_to_all | solution.py:773
  97.3 37.8 %collective-permute-start.17 = (bf16[512,1024]{1,0:T(8,128)(2,1)S(1)}, bf16[512,1024]{1,0:T(8,128)(2,1)}, u32[]{:S(2)}, u32[]{:S(2)}) collective-permute-start(bf16[512,1024]{1,0:T(8,128)(2,1)S(1)} %collective-permute-done.9.refs_3_), channel_id=1, source_target_pairs={{16,8},{18,10},{20,12},{14,6},{8,0},{10,2},{12,4},{17,9},{19,11},{... | collective-permute-start | bytes 3145736 | tf_op jit(solution)/shard_map/ppermute | solution.py:732
  101.1 33.3 %collective-permute-start.13 = (bf16[256,1024]{1,0:T(8,128)(2,1)S(1)}, bf16[256,1024]{1,0:T(8,128)(2,1)S(1)}, u32[]{:S(2)}, u32[]{:S(2)}) collective-permute-start(bf16[256,1024]{1,0:T(8,128)(2,1)S(1)} %add_select_fusion.1.refs_0_), channel_id=1, source_target_pairs={{0,2},{2,0},{4,6},{6,4},{8,10},{10,8},{12,14},{14,12},{16,18},{18,... | collective-permute-start | bytes 1572872 | tf_op jit(solution)/shard_map/ppermute | solution.py:732
  102.1 32.3 %collective-permute-start.14 = (bf16[256,1024]{1,0:T(8,128)(2,1)S(1)}, bf16[256,1024]{1,0:T(8,128)(2,1)}, u32[]{:S(2)}, u32[]{:S(2)}) collective-permute-start(bf16[256,1024]{1,0:T(8,128)(2,1)S(1)} %add_select_fusion.1.refs_0_), channel_id=1, source_target_pairs={{0,4},{2,6},{4,0},{6,2},{8,12},{10,14},{12,8},{14,10},{16,20},{18,... | collective-permute-start | bytes 1572872 | tf_op jit(solution)/shard_map/ppermute | solution.py:732
  136.4 21.6 %collective-permute-start.18 = (bf16[256,1024]{1,0:T(8,128)(2,1)S(1)}, bf16[256,1024]{1,0:T(8,128)(2,1)}, u32[]{:S(2)}, u32[]{:S(2)}) collective-permute-start(bf16[256,1024]{1,0:T(8,128)(2,1)S(1)} %add_select_fusion.refs_4_), channel_id=1, source_target_pairs={{0,2},{2,0},{4,6},{6,4},{8,10},{10,8},{12,14},{14,12},{16,18},{18,... | collective-permute-start | bytes 1572872 | tf_op jit(solution)/shard_map/ppermute | solution.py:732
  137.9 29.0 %collective-permute-start.19 = (bf16[256,1024]{1,0:T(8,128)(2,1)S(1)}, bf16[256,1024]{1,0:T(8,128)(2,1)}, u32[]{:S(2)}, u32[]{:S(2)}) collective-permute-start(bf16[256,1024]{1,0:T(8,128)(2,1)S(1)} %add_select_fusion.refs_4_), channel_id=1, source_target_pairs={{0,4},{2,6},{4,0},{6,2},{8,12},{10,14},{12,8},{14,10},{16,20},{18,... | collective-permute-start | bytes 1572872 | tf_op jit(solution)/shard_map/ppermute | solution.py:732
  156.3 25.5 %collective-permute-start.38 = (bf16[512,1024]{1,0:T(8,128)(2,1)S(1)}, bf16[512,1024]{1,0:T(8,128)(2,1)}, u32[]{:S(2)}, u32[]{:S(2)}) collective-permute-start(bf16[512,1024]{1,0:T(8,128)(2,1)S(1)} %pad_maximum_fusion.1.refs_0_), channel_id=1, source_target_pairs={{16,24},{18,26},{20,28},{14,22},{22,30},{17,25},{19,27},{21,29},{1... | collective-permute-start | bytes 3145736 | tf_op jit(solution)/shard_map/ppermute | solution.py:732
  158.0 23.8 %collective-permute-start.22 = (bf16[256,1024]{1,0:T(8,128)(2,1)S(1)}, bf16[256,1024]{1,0:T(8,128)(2,1)S(1)}, u32[]{:S(2)}, u32[]{:S(2)}) collective-permute-start(bf16[256,1024]{1,0:T(8,128)(2,1)S(1)} %add_select_fusion.1.refs_0_), channel_id=1, source_target_pairs={{0,1},{1,0},{2,3},{3,2},{4,5},{5,4},{6,7},{7,6},{8,9},{9,8},{10,11... | collective-permute-start | bytes 1572872 | tf_op jit(solution)/shard_map/ppermute | solution.py:736
  158.0 24.3 %collective-permute-start.23 = (bf16[256,1024]{1,0:T(8,128)(2,1)S(1)}, bf16[256,1024]{1,0:T(8,128)(2,1)S(1)}, u32[]{:S(2)}, u32[]{:S(2)}) collective-permute-start(bf16[256,1024]{1,0:T(8,128)(2,1)S(1)} %collective-permute-done.13.refs_1_), channel_id=1, source_target_pairs={{0,1},{1,0},{2,3},{3,2},{4,5},{5,4},{6,7},{7,6},{8,9},{9,8},{10,11... | collective-permute-start | bytes 1572872 | tf_op jit(solution)/shard_map/ppermute | solution.py:736
  170.4 24.2 %collective-permute-start.31 = (bf16[256,1024]{1,0:T(8,128)(2,1)S(1)}, bf16[256,1024]{1,0:T(8,128)(2,1)}, u32[]{:S(2)}, u32[]{:S(2)}) collective-permute-start(bf16[256,1024]{1,0:T(8,128)(2,1)S(1)} %pad_maximum_fusion.3.refs_0_), channel_id=1, source_target_pairs={{0,4},{2,6},{4,0},{6,2},{8,12},{10,14},{12,8},{14,10},{16,20},{18,... | collective-permute-start | bytes 1572872 | tf_op jit(solution)/shard_map/ppermute | solution.py:732
  182.3 22.5 %collective-permute-start.27 = (bf16[256,1024]{1,0:T(8,128)(2,1)}, bf16[256,1024]{1,0:T(8,128)(2,1)S(1)}, u32[]{:S(2)}, u32[]{:S(2)}) collective-permute-start(bf16[256,1024]{1,0:T(8,128)(2,1)} %collective-permute-done.18.refs_5_), channel_id=1, source_target_pairs={{0,1},{1,0},{2,3},{3,2},{4,5},{5,4},{6,7},{7,6},{8,9},{9,8},{10,11... | collective-permute-start | bytes 1572872 | tf_op jit(solution)/shard_map/ppermute | solution.py:736
  209.4 49.9 %collective-permute-start.39 = (bf16[512,1024]{1,0:T(8,128)(2,1)}, bf16[512,1024]{1,0:T(8,128)(2,1)}, u32[]{:S(2)}, u32[]{:S(2)}) collective-permute-start(bf16[512,1024]{1,0:T(8,128)(2,1)} %collective-permute-done.38.refs_1_), channel_id=1, source_target_pairs={{22,30},{23,31}} | collective-permute-start | bytes 3145736 | tf_op jit(solution)/shard_map/ppermute | solution.py:732
  211.1 48.3 %collective-permute-start.40 = (bf16[512,1024]{1,0:T(8,128)(2,1)}, bf16[512,1024]{1,0:T(8,128)(2,1)}, u32[]{:S(2)}, u32[]{:S(2)}) collective-permute-start(bf16[512,1024]{1,0:T(8,128)(2,1)} %collective-permute-done.17.refs_4_), channel_id=1, source_target_pairs={{8,0},{10,2},{12,4},{9,1},{11,3},{13,5}} | collective-permute-start | bytes 3145736 | tf_op jit(solution)/shard_map/ppermute | solution.py:732
  216.2 35.0 %collective-permute-start.35 = (bf16[256,1024]{1,0:T(8,128)(2,1)}, bf16[256,1024]{1,0:T(8,128)(2,1)}, u32[]{:S(2)}, u32[]{:S(2)}) collective-permute-start(bf16[256,1024]{1,0:T(8,128)(2,1)} %collective-permute-done.30.refs_1_), channel_id=1, source_target_pairs={{0,1},{1,0},{2,3},{3,2},{4,5},{5,4},{6,7},{7,6},{8,9},{9,8},{10,11... | collective-permute-start | bytes 1572872 | tf_op jit(solution)/shard_map/ppermute | solution.py:736
  217.1 34.1 %collective-permute-start.36 = (bf16[256,1024]{1,0:T(8,128)(2,1)}, bf16[256,1024]{1,0:T(8,128)(2,1)}, u32[]{:S(2)}, u32[]{:S(2)}) collective-permute-start(bf16[256,1024]{1,0:T(8,128)(2,1)} %collective-permute-done.31.refs_2_), channel_id=1, source_target_pairs={{0,1},{1,0},{2,3},{3,2},{4,5},{5,4},{6,7},{7,6},{8,9},{9,8},{10,11... | collective-permute-start | bytes 1572872 | tf_op jit(solution)/shard_map/ppermute | solution.py:736
  217.5 33.7 %collective-permute-start.37 = (bf16[256,1024]{1,0:T(8,128)(2,1)}, bf16[256,1024]{1,0:T(8,128)(2,1)}, u32[]{:S(2)}, u32[]{:S(2)}) collective-permute-start(bf16[256,1024]{1,0:T(8,128)(2,1)} %constant_dynamic-update-slice_fusion.refs_3_), channel_id=1, source_target_pairs={{0,1},{1,0},{2,3},{3,2},{4,5},{5,4},{6,7},{7,6},{8,9},{9,8},{10,11... | collective-permute-start | bytes 1572872 | tf_op jit(solution)/shard_map/ppermute | solution.py:736
  277.8 41.7 %collective-permute-start.41 = (bf16[512,1536]{1,0:T(8,128)(2,1)}, bf16[512,1536]{1,0:T(8,128)(2,1)}, u32[]{:S(2)}, u32[]{:S(2)}) collective-permute-start(bf16[512,1536]{1,0:T(8,128)(2,1)} %bitcast.23), channel_id=1, source_target_pairs={{0,1},{1,0},{2,3},{3,2},{4,5},{5,4},{6,7},{7,6},{8,9},{9,8},{10,11... | collective-permute-start | bytes 4718600 | tf_op jit(solution)/shard_map/ppermute | solution.py:736
  338.0 45.4 %collective-permute-start.48 = (bf16[64,3072]{1,0:T(8,128)(2,1)}, bf16[64,3072]{1,0:T(8,128)(2,1)}, u32[]{:S(2)}, u32[]{:S(2)}) collective-permute-start(bf16[64,3072]{1,0:T(8,128)(2,1)} %pad_maximum_fusion.8.refs_0_), channel_id=1, source_target_pairs={{0,8},{2,10},{4,12},{6,14},{8,16},{10,18},{12,20},{14,22},{16,24},... | collective-permute-start | bytes 1179656 | tf_op jit(solution)/shard_map/ppermute | solution.py:732
  343.6 107.1 %collective-permute-start.51 = (bf16[64,3072]{1,0:T(8,128)(2,1)}, bf16[64,3072]{1,0:T(8,128)(2,1)}, u32[]{:S(2)}, u32[]{:S(2)}) collective-permute-start(bf16[64,3072]{1,0:T(8,128)(2,1)} %pad_maximum_fusion.8.refs_0_), channel_id=1, source_target_pairs={{24,16},{26,18},{28,20},{30,22},{22,14},{25,17},{27,19},{29,21},{3... | collective-permute-start | bytes 1179656 | tf_op jit(solution)/shard_map/ppermute | solution.py:732
  351.3 21.3 %all-to-all-start.7 = ((f32[32,3,1024]{2,1,0:T(4,128)}), f32[32,3,1024]{2,1,0:T(4,128)}, u32[]{:S(2)}, u32[]{:S(2)}) async-start(f32[32,3,1024]{2,1,0:T(4,128)} %reshape.220), calls=%async_computation.7 | async-start | bytes 1048576 | tf_op jit(solution)/shard_map/all_to_all | solution.py:1001
  363.5 41.1 %collective-permute-start.56 = (bf16[256,1024]{1,0:T(8,128)(2,1)}, bf16[256,1024]{1,0:T(8,128)(2,1)}, u32[]{:S(2)}, u32[]{:S(2)}) collective-permute-start(bf16[256,1024]{1,0:T(8,128)(2,1)} %pad_maximum_fusion.5), channel_id=1, source_target_pairs={{0,4},{2,6},{4,0},{6,2},{8,12},{10,14},{12,8},{14,10},{16,20},{18,... | collective-permute-start | bytes 1572872 | tf_op jit(solution)/shard_map/ppermute | solution.py:732
  381.7 24.8 %collective-permute-start.54 = (bf16[256,1024]{1,0:T(8,128)(2,1)}, bf16[256,1024]{1,0:T(8,128)(2,1)}, u32[]{:S(2)}, u32[]{:S(2)}) collective-permute-start(bf16[256,1024]{1,0:T(8,128)(2,1)} %pad_maximum_fusion.4), channel_id=1, source_target_pairs={{0,2},{2,0},{4,6},{6,4},{8,10},{10,8},{12,14},{14,12},{16,18},{18,... | collective-permute-start | bytes 1572872 | tf_op jit(solution)/shard_map/ppermute | solution.py:732
  384.9 67.2 %collective-permute-start.49 = (bf16[64,3072]{1,0:T(8,128)(2,1)}, bf16[64,3072]{1,0:T(8,128)(2,1)}, u32[]{:S(2)}, u32[]{:S(2)}) collective-permute-start(bf16[64,3072]{1,0:T(8,128)(2,1)} %collective-permute-done.48.refs_1_), channel_id=1, source_target_pairs={{8,16},{10,18},{12,20},{14,22},{16,24},{18,26},{20,28},{22,30},{9,... | collective-permute-start | bytes 1179656 | tf_op jit(solution)/shard_map/ppermute | solution.py:732
  394.5 22.6 %collective-permute-start.63 = (bf16[256,1024]{1,0:T(8,128)(2,1)}, bf16[256,1024]{1,0:T(8,128)(2,1)}, u32[]{:S(2)}, u32[]{:S(2)}) collective-permute-start(bf16[256,1024]{1,0:T(8,128)(2,1)} %pad_maximum_fusion.7), channel_id=1, source_target_pairs={{0,4},{2,6},{4,0},{6,2},{8,12},{10,14},{12,8},{14,10},{16,20},{18,... | collective-permute-start | bytes 1572872 | tf_op jit(solution)/shard_map/ppermute | solution.py:732
  397.9 39.1 %all-to-all-start.9 = ((bf16[16,8,4096]{2,1,0:T(8,128)(2,1)}), bf16[16,8,4096]{2,1,0:T(8,128)(2,1)}, u32[]{:S(2)}, u32[]{:S(2)}) async-start(bf16[16,8,4096]{2,1,0:T(8,128)(2,1)} %broadcast_in_dim.207), calls=%async_computation.9 | async-start | bytes 2097152 | tf_op jit(solution)/shard_map/all_to_all | solution.py:1036
  404.7 23.6 %collective-permute-start.61 = (bf16[256,1024]{1,0:T(8,128)(2,1)}, bf16[256,1024]{1,0:T(8,128)(2,1)}, u32[]{:S(2)}, u32[]{:S(2)}) collective-permute-start(bf16[256,1024]{1,0:T(8,128)(2,1)} %pad_maximum_fusion.6), channel_id=1, source_target_pairs={{0,2},{2,0},{4,6},{6,4},{8,10},{10,8},{12,14},{14,12},{16,18},{18,... | collective-permute-start | bytes 1572872 | tf_op jit(solution)/shard_map/ppermute | solution.py:732
  408.8 23.9 %collective-permute-start.57 = (bf16[256,1024]{1,0:T(8,128)(2,1)}, bf16[256,1024]{1,0:T(8,128)(2,1)}, u32[]{:S(2)}, u32[]{:S(2)}) collective-permute-start(bf16[256,1024]{1,0:T(8,128)(2,1)} %fusion.49), channel_id=1, source_target_pairs={{24,16},{26,18},{28,20},{30,22},{6,14},{25,17},{27,19},{29,21},{31... | collective-permute-start | bytes 1572872 | tf_op jit(solution)/shard_map/ppermute | solution.py:732
  437.8 24.4 %all-to-all-start.11 = ((f32[32,2,1024]{2,1,0:T(2,128)}), f32[32,2,1024]{2,1,0:T(2,128)}, u32[]{:S(2)}, u32[]{:S(2)}) async-start(f32[32,2,1024]{2,1,0:T(2,128)} %broadcast_in_dim.211), calls=%async_computation.11 | async-start | bytes 524288 | tf_op jit(solution)/shard_map/all_to_all | solution.py:773
  446.3 23.4 %collective-permute-start.45 = (bf16[128,4096]{1,0:T(8,128)(2,1)}, bf16[128,4096]{1,0:T(8,128)(2,1)}, u32[]{:S(2)}, u32[]{:S(2)}) collective-permute-start(bf16[128,4096]{1,0:T(8,128)(2,1)} %bitcast.26), channel_id=1, source_target_pairs={{0,1},{1,0},{2,3},{3,2},{4,5},{5,4},{6,7},{7,6},{8,9},{9,8},{10,11... | collective-permute-start | bytes 3145736 | tf_op jit(solution)/shard_map/ppermute | solution.py:736
  (177 other events, 2314.4 us)
